TPU v7x, 32 devices: a whole 2x2x4 slice. The times are simulated.
32 devices in a mesh: wide: 8 (over z, core), rows: 4 (over y, x).
Axes of the slice: x: 2, y: 2, z: 4, core: 2. Of those that a mesh axis runs over, the one named last changes fastest.
Arguments:
- inputs: bfloat16 [8, 1024, 1024], P('rows', 'wide'), may hold values from -6 to 6
- lengths: int32 [8, 6], P('rows'), may hold values from 1 to 1019, as said below
- ffn1_in: bfloat16 [1024, 4096], P(('wide', 'rows')), may hold values from -0.1875 to 0.1875
- ffn1_out: bfloat16 [4096, 1024], P(('wide', 'rows')), may hold values from -0.1875 to 0.1875
- attn_qkv: bfloat16 [1024, 3072], P(('wide', 'rows')), may hold values from -0.1875 to 0.1875
- attn_out: bfloat16 [1024, 1024], P(('wide', 'rows')), may hold values from -0.75 to 0.75
- conv_in: bfloat16 [1024, 2048], P(('wide', 'rows')), may hold values from -0.1875 to 0.1875
- depth_kernel: bfloat16 [31, 1024], P(None, ('wide', 'rows')), may hold values from -1 to 1
- conv_out: bfloat16 [1024, 1024], P(('wide', 'rows')), may hold values from -0.375 to 0.375
- ffn2_in: bfloat16 [1024, 4096], P(('wide', 'rows')), may hold values from -0.1875 to 0.1875
- ffn2_out: bfloat16 [4096, 1024], P(('wide', 'rows')), may hold values from -0.1875 to 0.1875
- norm_gains: bfloat16 [6, 1024], P(None, ('wide', 'rows')), may hold values from 0.5 to 1.5
- cotangent: bfloat16 [8, 1024, 1024], P('rows', 'wide'), may hold values from -6 to 6
Outputs:
- layer_out: bfloat16 [8, 1024, 1024], P('rows', 'wide')
- grad_inputs: bfloat16 [8, 1024, 1024], P('rows', 'wide')
- grad_ffn1_in: float32 [1024, 4096], P(('wide', 'rows'))
- grad_ffn1_out: float32 [4096, 1024], P(('wide', 'rows'))
- grad_attn_qkv: float32 [1024, 3072], P(('wide', 'rows'))
- grad_attn_out: float32 [1024, 1024], P(('wide', 'rows'))
- grad_conv_in: float32 [1024, 2048], P(('wide', 'rows'))
- grad_depth_kernel: float32 [31, 1024], P(None, ('wide', 'rows'))
- grad_conv_out: float32 [1024, 1024], P(('wide', 'rows'))
- grad_ffn2_in: float32 [1024, 4096], P(('wide', 'rows'))
- grad_ffn2_out: float32 [4096, 1024], P(('wide', 'rows'))
- grad_norm_gains: float32 [6, 1024], P(None, ('wide', 'rows'))
Inputs may be any that keep to these rules, and one draw needn't show every extreme that they name: The lengths of each row sum to 1024.
All inputs are finite; a program needn't handle non-finite values.
Results may differ from a plain program's by a relative error of at most 0.017.
Values may be sent and summed in bfloat16 or wider, within the bound.
No kernel may reach another device: no remote copies, remote signals or barrier semaphores. Data moves between devices by JAX's collectives and lax.ppermute only.
A program may use at most 256 MiB of HBM per device.

v0:
```python
import jax
import jax.numpy as jnp
from jax import lax
from jax.sharding import PartitionSpec as P

HEADS = 16
HEAD_DIM = 64


EPSILON = 1e-05


def extended_2(x, sides, width):
    for axis, dim in sides:
        size, length = (lax.axis_size(axis), x.shape[dim])
        up = [(i, (i + 1) % size) for i in range(size - 1)]
        down = [(j, i) for i, j in up]
        last = lax.slice_in_dim(x, length - width, length, axis=dim)
        initial = lax.slice_in_dim(x, 0, width, axis=dim)
        before = lax.ppermute(last, axis, up)
        after = lax.ppermute(initial, axis, down)
        x = jnp.concatenate([before, x, after], axis=dim)
    return x


def segment_info(lengths, frame_total):
    segment_end = jnp.cumsum(lengths, axis=-1, dtype=jnp.int32)
    frame_index = jnp.arange(frame_total, dtype=jnp.int32)
    passed = (frame_index[None, None, :] >= segment_end[:, :, None]).astype(jnp.int32)
    segment_ids = jnp.sum(passed, axis=1, dtype=jnp.int32)
    seg_starts = jnp.sum(passed * lengths[:, :, None], axis=1, dtype=jnp.int32)
    return (segment_ids, frame_index[None, :] - seg_starts)


def layer_norm(values, gain_row):
    centred = values - jnp.mean(values, axis=-1, keepdims=True)
    inv_scale = lax.rsqrt(jnp.mean(centred * centred, axis=-1, keepdims=True) + EPSILON)
    normed = centred * inv_scale
    return (normed * gain_row, normed, inv_scale)


def norm_backward(gradient, gain_row, normed, inv_scale):
    scaled = gradient * gain_row
    gain_grad = jnp.sum(gradient * normed, axis=(0, 1))
    centred_mean = jnp.mean(scaled, axis=-1, keepdims=True)
    product_mean = jnp.mean(scaled * normed, axis=-1, keepdims=True)
    return (inv_scale * (scaled - centred_mean - normed * product_mean), gain_grad)


def swish_slope(values):
    gate_sig = jax.nn.sigmoid(values)
    return gate_sig * (1.0 + values * (1.0 - gate_sig))


def project(left, right):
    return jnp.einsum("rfd,de->rfe", left, right, preferred_element_type=jnp.float32)


def project_back(left, right):
    return jnp.einsum("rfe,de->rfd", left, right, preferred_element_type=jnp.float32)


def outer_sum(left, right):
    return jnp.einsum("rfd,rfe->de", left, right, preferred_element_type=jnp.float32)


def rotation(position, head_size):
    half_width = head_size // 2
    frequency = jnp.power(10000.0, -2.0 * jnp.arange(half_width, dtype=jnp.float32) / head_size)
    angles = position.astype(jnp.float32)[..., None] * frequency
    return (jnp.cos(angles)[..., None, :], jnp.sin(angles)[..., None, :])


def rotate(values, cosine, sine):
    half_width = values.shape[-1] // 2
    front_half = values[..., :half_width]
    back_half = values[..., half_width:]
    return jnp.concatenate(
        [front_half * cosine - back_half * sine, front_half * sine + back_half * cosine], axis=-1
    )


def unrotate(gradient, cosine, sine):
    half_width = gradient.shape[-1] // 2
    front_half = gradient[..., :half_width]
    back_half = gradient[..., half_width:]
    return jnp.concatenate(
        [front_half * cosine + back_half * sine, back_half * cosine - front_half * sine], axis=-1
    )


def score_block(query_heads, key_heads, query_ids, key_ids):
    scores = jnp.einsum(
        "qhd,khd->hqk", query_heads, key_heads, preferred_element_type=jnp.float32
    ) * HEAD_DIM ** (-0.5)
    same_segment = (query_ids[:, None] == key_ids[None, :])[None]
    return (jnp.where(same_segment, scores, -1e30), same_segment)


def attend_row(items):
    queries, keys, values, query_ids, key_ids = items
    scores, same_segment = score_block(
        queries.reshape(-1, HEADS, HEAD_DIM), keys.reshape(-1, HEADS, HEAD_DIM), query_ids, key_ids
    )
    row_max = jnp.max(scores, axis=-1, keepdims=True)
    unnormed = jnp.exp(scores - row_max)
    row_total = jnp.sum(unnormed, axis=-1, keepdims=True)
    probabilities = (unnormed / row_total).astype(jnp.bfloat16)
    mixed = jnp.einsum(
        "hqk,khd->qhd",
        probabilities,
        values.reshape(-1, HEADS, HEAD_DIM),
        preferred_element_type=jnp.float32,
    )
    return (
        mixed.reshape(queries.shape).astype(jnp.bfloat16),
        (row_max + jnp.log(row_total))[..., 0],
    )


def score_grads_of(
    query_heads, key_heads, value_heads, grad_heads, query_ids, key_ids, log_total, delta_sum
):
    scores, same_segment = score_block(query_heads, key_heads, query_ids, key_ids)
    probabilities = jnp.where(same_segment, jnp.exp(scores - log_total[..., None]), 0.0)
    prob_grads = jnp.einsum(
        "qhd,khd->hqk", grad_heads, value_heads, preferred_element_type=jnp.float32
    )
    delta_sum = jnp.sum(probabilities * prob_grads, axis=-1, keepdims=True)
    score_grads = (probabilities * (prob_grads - delta_sum)).astype(jnp.bfloat16)
    return (probabilities, score_grads, delta_sum)


def attend_back(items):
    queries, keys, values, query_ids, key_ids, log_total, head_grads = items
    query_heads = queries.reshape(-1, HEADS, HEAD_DIM)
    key_heads = keys.reshape(-1, HEADS, HEAD_DIM)
    grad_heads = head_grads.reshape(-1, HEADS, HEAD_DIM)
    probabilities, score_grads, delta_sum = score_grads_of(
        query_heads,
        key_heads,
        values.reshape(-1, HEADS, HEAD_DIM),
        grad_heads,
        query_ids,
        key_ids,
        log_total,
        None,
    )
    scale_factor = HEAD_DIM ** (-0.5)
    query_grad = (
        jnp.einsum("hqk,khd->qhd", score_grads, key_heads, preferred_element_type=jnp.float32)
        * scale_factor
    )
    key_grad = (
        jnp.einsum("hqk,qhd->khd", score_grads, query_heads, preferred_element_type=jnp.float32)
        * scale_factor
    )
    value_grad = jnp.einsum(
        "hqk,qhd->khd",
        probabilities.astype(jnp.bfloat16),
        grad_heads,
        preferred_element_type=jnp.float32,
    )
    key_share, value_share = (
        lax.psum_scatter(
            key_grad.reshape(keys.shape).astype(jnp.bfloat16),
            "wide",
            scatter_dimension=0,
            tiled=True,
        ).astype(jnp.float32),
        lax.psum_scatter(
            value_grad.reshape(values.shape).astype(jnp.bfloat16),
            "wide",
            scatter_dimension=0,
            tiled=True,
        ).astype(jnp.float32),
    )
    return (query_grad.reshape(queries.shape), key_share, value_share)


def feed_forward(residual, gain_row, weight_in, weight_out):
    normed_out, normed, inv_scale = layer_norm(residual, gain_row)
    hidden = normed_out.astype(jnp.bfloat16)
    before = project(hidden, weight_in)
    after = (before * jax.nn.sigmoid(before)).astype(jnp.bfloat16)
    return (residual + 0.5 * project(after, weight_out), (hidden, before, after, normed, inv_scale))


def feed_back(gradient, gain_row, weight_in, weight_out, saved):
    hidden, before, after, normed, inv_scale = saved
    branch_grad = (0.5 * gradient).astype(jnp.bfloat16)
    grad_out = outer_sum(after, branch_grad)
    before_grad = (project_back(branch_grad, weight_out) * swish_slope(before)).astype(jnp.bfloat16)
    grad_in = outer_sum(hidden, before_grad)
    input_grad, gain_grad = norm_backward(
        project_back(before_grad, weight_in), gain_row, normed, inv_scale
    )
    return (gradient + input_grad, gain_grad, grad_in, grad_out)


def per_device(
    inputs,
    lengths,
    ffn1_in,
    ffn1_out,
    attn_qkv,
    attn_out,
    conv_in,
    depth_kernel,
    conv_out,
    ffn2_in,
    ffn2_out,
    norm_gains,
    cotangent,
):
    row_count, frames_here, model_width = inputs.shape
    frame_total = frames_here * lax.axis_size("wide")
    kernel_size = depth_kernel.shape[0]
    half_width = kernel_size // 2
    offset = lax.axis_index("wide") * frames_here
    segment_ids, position = segment_info(lengths, frame_total)
    padded_ids = jnp.pad(segment_ids, ((0, 0), (half_width, half_width)), constant_values=-1)
    edge_ids = lax.dynamic_slice_in_dim(padded_ids, offset, frames_here + 2 * half_width, 1)
    local_ids = lax.dynamic_slice_in_dim(segment_ids, offset, frames_here, 1)
    local_position = lax.dynamic_slice_in_dim(position, offset, frames_here, 1)
    tap_masks = jnp.stack(
        [
            (edge_ids[:, tap_index : tap_index + frames_here] == local_ids).astype(jnp.float32)
            for tap_index in range(kernel_size)
        ]
    )
    cosine, sine = rotation(local_position, HEAD_DIM)
    heads_shape = (row_count, frames_here, HEADS, HEAD_DIM)
    flat_shape = (row_count, frames_here, model_width)
    gathered = (
        lax.all_gather(ffn1_in, ("wide", "rows"), axis=0, tiled=True),
        lax.all_gather(ffn1_out, ("wide", "rows"), axis=0, tiled=True),
        lax.all_gather(attn_qkv, ("wide", "rows"), axis=0, tiled=True),
        lax.all_gather(attn_out, ("wide", "rows"), axis=0, tiled=True),
        lax.all_gather(conv_in, ("wide", "rows"), axis=0, tiled=True),
        lax.all_gather(conv_out, ("wide", "rows"), axis=0, tiled=True),
        lax.all_gather(ffn2_in, ("wide", "rows"), axis=0, tiled=True),
        lax.all_gather(ffn2_out, ("wide", "rows"), axis=0, tiled=True),
        lax.all_gather(depth_kernel, ("wide", "rows"), axis=1, tiled=True),
        lax.all_gather(norm_gains, ("wide", "rows"), axis=1, tiled=True),
    )
    kernel = gathered[8].astype(jnp.float32)
    gains = gathered[9].astype(jnp.float32)
    residual = inputs.astype(jnp.float32)
    first, ffn1_saved = feed_forward(residual, gains[0], gathered[0], gathered[1])
    attn_norm, attn_normed, attn_scale = layer_norm(first, gains[1])
    attn_hidden = attn_norm.astype(jnp.bfloat16)
    packed = project(attn_hidden, gathered[2])
    queries = (
        rotate(packed[..., :model_width].reshape(heads_shape), cosine, sine)
        .astype(jnp.bfloat16)
        .reshape(flat_shape)
    )
    keys = (
        rotate(packed[..., model_width : 2 * model_width].reshape(heads_shape), cosine, sine)
        .astype(jnp.bfloat16)
        .reshape(flat_shape)
    )
    values = packed[..., 2 * model_width :].astype(jnp.bfloat16)
    key_rows, value_rows = (
        lax.all_gather(keys, "wide", axis=1, tiled=True),
        lax.all_gather(values, "wide", axis=1, tiled=True),
    )
    mixed, log_total = lax.map(attend_row, (queries, key_rows, value_rows, local_ids, segment_ids))
    second = first + project(mixed, gathered[3])
    conv_norm, conv_normed, conv_scale = layer_norm(second, gains[2])
    conv_hidden = conv_norm.astype(jnp.bfloat16)
    gated = project(conv_hidden, gathered[4])
    gate_sig = jax.nn.sigmoid(gated[..., model_width:])
    glu = (gated[..., :model_width] * gate_sig).astype(jnp.bfloat16)
    extended = extended_2(glu, (("wide", 1),), half_width)
    convolved = jnp.zeros(glu.shape, jnp.float32)
    for tap_index in range(kernel_size):
        convolved = convolved + extended[:, tap_index : tap_index + frames_here] * (
            tap_masks[tap_index][..., None] * kernel[tap_index]
        )
    inner_out, inner_normed, inner_scale = layer_norm(convolved, gains[3])
    activated = (inner_out * jax.nn.sigmoid(inner_out)).astype(jnp.bfloat16)
    third = second + project(activated, gathered[5])
    fourth, ffn2_saved = feed_forward(third, gains[4], gathered[6], gathered[7])
    final_out, final_normed, final_scale = layer_norm(fourth, gains[5])
    layer_out = final_out.astype(jnp.bfloat16)
    weights_back = (
        lax.all_gather(ffn1_in, ("wide", "rows"), axis=0, tiled=True),
        lax.all_gather(ffn1_out, ("wide", "rows"), axis=0, tiled=True),
        lax.all_gather(attn_qkv, ("wide", "rows"), axis=0, tiled=True),
        lax.all_gather(attn_out, ("wide", "rows"), axis=0, tiled=True),
        lax.all_gather(conv_in, ("wide", "rows"), axis=0, tiled=True),
        lax.all_gather(conv_out, ("wide", "rows"), axis=0, tiled=True),
        lax.all_gather(ffn2_in, ("wide", "rows"), axis=0, tiled=True),
        lax.all_gather(ffn2_out, ("wide", "rows"), axis=0, tiled=True),
        lax.all_gather(depth_kernel, ("wide", "rows"), axis=1, tiled=True),
        lax.all_gather(norm_gains, ("wide", "rows"), axis=1, tiled=True),
    )
    keys_back, values_back = (
        lax.all_gather(keys, "wide", axis=1, tiled=True),
        lax.all_gather(values, "wide", axis=1, tiled=True),
    )
    gradient, gain_final = norm_backward(
        cotangent.astype(jnp.float32), gains[5], final_normed, final_scale
    )
    gradient, gain_ffn2, grad_ffn2_in, grad_ffn2_out = feed_back(
        gradient, gains[4], weights_back[6], weights_back[7], ffn2_saved
    )
    conv_branch = gradient.astype(jnp.bfloat16)
    grad_conv_out = outer_sum(activated, conv_branch)
    act_grad = project_back(conv_branch, weights_back[5]) * swish_slope(inner_out)
    conv_grad, gain_inner = norm_backward(act_grad, gains[3], inner_normed, inner_scale)
    ext_grad = jnp.zeros(extended.shape, jnp.float32)
    kernel_terms = []
    for tap_index in range(kernel_size):
        masked = conv_grad * tap_masks[tap_index][..., None]
        kernel_terms.append(
            jnp.sum(extended[:, tap_index : tap_index + frames_here] * masked, axis=(0, 1))
        )
        ext_grad = ext_grad.at[:, tap_index : tap_index + frames_here].add(
            masked * kernel[tap_index]
        )
    grad_kernel = jnp.stack(kernel_terms)
    rims = jnp.concatenate(
        [ext_grad[:, :half_width], ext_grad[:, frames_here + half_width :]], axis=1
    )
    arrived = extended_2(rims.astype(jnp.bfloat16), (("wide", 1),), half_width).astype(rims.dtype)
    glu_grad = ext_grad[:, half_width : half_width + frames_here]
    glu_grad = glu_grad.at[:, :half_width].add(arrived[:, :half_width])
    glu_grad = glu_grad.at[:, frames_here - half_width :].add(arrived[:, 3 * half_width :])
    gated_grad = jnp.concatenate(
        [glu_grad * gate_sig, glu_grad * gated[..., :model_width] * gate_sig * (1.0 - gate_sig)],
        axis=-1,
    ).astype(jnp.bfloat16)
    grad_conv_in = outer_sum(conv_hidden, gated_grad)
    norm_grad, gain_conv = norm_backward(
        project_back(gated_grad, weights_back[4]), gains[2], conv_normed, conv_scale
    )
    gradient = gradient + norm_grad
    attn_branch = gradient.astype(jnp.bfloat16)
    grad_attn_out = outer_sum(mixed, attn_branch)
    head_grads = project_back(attn_branch, weights_back[3]).astype(jnp.bfloat16)
    query_grad, key_grad, value_grad = lax.map(
        attend_back,
        (queries, keys_back, values_back, local_ids, segment_ids, log_total, head_grads),
    )
    packed_grad = jnp.concatenate(
        [
            unrotate(query_grad.reshape(heads_shape), cosine, sine).reshape(flat_shape),
            unrotate(key_grad.reshape(heads_shape), cosine, sine).reshape(flat_shape),
            value_grad,
        ],
        axis=-1,
    ).astype(jnp.bfloat16)
    grad_qkv = outer_sum(attn_hidden, packed_grad)
    norm_grad, gain_attn = norm_backward(
        project_back(packed_grad, weights_back[2]), gains[1], attn_normed, attn_scale
    )
    gradient = gradient + norm_grad
    gradient, gain_ffn1, grad_ffn1_in, grad_ffn1_out = feed_back(
        gradient, gains[0], weights_back[0], weights_back[1], ffn1_saved
    )
    grad_gains = jnp.stack([gain_ffn1, gain_attn, gain_conv, gain_inner, gain_ffn2, gain_final])
    summed = (
        lax.psum_scatter(grad_ffn1_in, ("wide", "rows"), scatter_dimension=0, tiled=True),
        lax.psum_scatter(grad_ffn1_out, ("wide", "rows"), scatter_dimension=0, tiled=True),
        lax.psum_scatter(grad_qkv, ("wide", "rows"), scatter_dimension=0, tiled=True),
        lax.psum_scatter(grad_attn_out, ("wide", "rows"), scatter_dimension=0, tiled=True),
        lax.psum_scatter(grad_conv_in, ("wide", "rows"), scatter_dimension=0, tiled=True),
        lax.psum_scatter(grad_conv_out, ("wide", "rows"), scatter_dimension=0, tiled=True),
        lax.psum_scatter(grad_ffn2_in, ("wide", "rows"), scatter_dimension=0, tiled=True),
        lax.psum_scatter(grad_ffn2_out, ("wide", "rows"), scatter_dimension=0, tiled=True),
        lax.psum_scatter(grad_kernel, ("wide", "rows"), scatter_dimension=1, tiled=True),
        lax.psum_scatter(grad_gains, ("wide", "rows"), scatter_dimension=1, tiled=True),
    )
    shares = (
        summed[0],
        summed[1],
        summed[2],
        summed[3],
        summed[4],
        summed[8],
        summed[5],
        summed[6],
        summed[7],
        summed[9],
    )
    return (
        layer_out,
        gradient.astype(jnp.bfloat16),
        shares[0],
        shares[1],
        shares[2],
        shares[3],
        shares[4],
        shares[5],
        shares[6],
        shares[7],
        shares[8],
        shares[9],
    )


def solution(mesh):
    return jax.shard_map(
        per_device,
        mesh=mesh,
        in_specs=(
            P("rows", "wide", None),
            P("rows", None),
            P(("wide", "rows"), None),
            P(("wide", "rows"), None),
            P(("wide", "rows"), None),
            P(("wide", "rows"), None),
            P(("wide", "rows"), None),
            P(None, ("wide", "rows")),
            P(("wide", "rows"), None),
            P(("wide", "rows"), None),
            P(("wide", "rows"), None),
            P(None, ("wide", "rows")),
            P("rows", "wide", None),
        ),
        out_specs=(
            P("rows", "wide", None),
            P("rows", "wide", None),
            P(("wide", "rows"), None),
            P(("wide", "rows"), None),
            P(("wide", "rows"), None),
            P(("wide", "rows"), None),
            P(("wide", "rows"), None),
            P(None, ("wide", "rows")),
            P(("wide", "rows"), None),
            P(("wide", "rows"), None),
            P(("wide", "rows"), None),
            P(None, ("wide", "rows")),
        ),
        check_vma=False,
    )
```

profile of v0, /device:TPU:0, one launch (start us, length us, event | category | flops | bytes accessed | tf_op | source)
XLA Modules:
  0.0 3430.6 jit_solution(5806183303446775319)
XLA Ops:
  9.4 71.3 %all-gather = bf16[32,32,6]{1,2,0:T(8,128)(2,1)S(1)} all-gather(bf16[1,32,6]{1,2,0:T(8,128)(2,1)} %bitcast.371), channel_id=1, replica_groups=mesh['wide'=8,'rows'=4] {'wide','rows'}, dimensions={0}, use_global_device_ids=true | all-gather | bytes 12672 | tf_op jit(solution)/shard_map/all_gather | solution.py:245
  84.0 7.1 all-gather.12.cloned.1.call-done
  91.1 8.1 fusion.30
  99.2 71.1 %all-gather.14.cloned.1.call-done = bf16[4096,1024]{1,0:T(8,128)(2,1)} async-done(((bf16[128,1024]{1,0:T(8,128)(2,1)}), bf16[4096,1024]{1,0:T(8,128)(2,1)}) %all-gather.14.cloned.1.call-update) | async-done | bytes 8388624 | tf_op jit(solution)/shard_map/all_gather | solution.py:237
  170.3 7.1 fusion.218
  177.7 63.7 %all-gather.16.cloned.1.call-done = bf16[1024,3072]{1,0:T(8,128)(2,1)} async-done(((bf16[32,3072]{1,0:T(8,128)(2,1)}), bf16[1024,3072]{1,0:T(8,128)(2,1)}) %all-gather.16.cloned.1.call-update) | async-done | bytes 6291472 | tf_op jit(solution)/shard_map/all_gather | solution.py:238
  241.4 4.7 fusion.34
  262.9 70.2 %all_gather.54 = bf16[31,1024]{0,1:T(8,128)(2,1)S(1)} all-gather(bf16[31,32]{0,1:T(8,128)(2,1)S(1)} %copy.123), channel_id=1, replica_groups=mesh['wide'=8,'rows'=4] {'wide','rows'}, dimensions={1}, use_global_device_ids=true | all-gather | bytes 65472 | tf_op jit(solution)/shard_map/all_gather | solution.py:244
  335.3 5.4 slice_reduce_fusion.30
  341.7 6.2 copy.121
  347.9 21.2 while.59
  369.2 32.4 all-gather.22.cloned.1.call-done
  404.3 61.1 %all-gather.24.cloned.1.call-done = bf16[1024,2048]{1,0:T(8,128)(2,1)} async-done(((bf16[32,2048]{1,0:T(8,128)(2,1)}), bf16[1024,2048]{1,0:T(8,128)(2,1)}) %all-gather.24.cloned.1.call-update) | async-done | bytes 4194320 | tf_op jit(solution)/shard_map/all_gather | solution.py:240
  477.8 8.1 fusion.213
  486.2 37.1 %all-gather.26.cloned.1.call-done = bf16[1024,1024]{1,0:T(8,128)(2,1)} async-done(((bf16[32,1024]{1,0:T(8,128)(2,1)}), bf16[1024,1024]{1,0:T(8,128)(2,1)}) %all-gather.26.cloned.1.call-update) | async-done | bytes 2097168 | tf_op jit(solution)/shard_map/all_gather | solution.py:241
  526.5 76.0 %all-gather.28.cloned.1.call-done = bf16[1024,4096]{1,0:T(8,128)(2,1)} async-done(((bf16[32,4096]{1,0:T(8,128)(2,1)}), bf16[1024,4096]{1,0:T(8,128)(2,1)}) %all-gather.28.cloned.1.call-update) | async-done | bytes 8388624 | tf_op jit(solution)/shard_map/all_gather | solution.py:242
  602.6 7.8 fusion.22
  610.4 71.1 %all-gather.30.cloned.1.call-done = bf16[4096,1024]{1,0:T(8,128)(2,1)} async-done(((bf16[128,1024]{1,0:T(8,128)(2,1)}), bf16[4096,1024]{1,0:T(8,128)(2,1)}) %all-gather.30.cloned.1.call-update) | async-done | bytes 8388624 | tf_op jit(solution)/shard_map/all_gather | solution.py:243
  681.5 7.1 fusion.221
  691.2 6.4 fusion.42
  856.5 5.0 fusion.158
  861.5 4.8 fusion.138
  866.3 5.2 fusion.160
  883.8 177.4 %while.60 = (s32[]{:T(128)}, f32[2,128,1024]{1,2,0:T(8,128)}, f32[2,128,1024]{1,2,0:T(8,128)}, bf16[2,128,1024]{2,1,0:T(8,128)(2,1)}, bf16[2,1024,1024]{1,2,0:T(...) while((s32[]{:T(128)}, f32[2,128,1024]{1,2,0:T(8,128)}, ...), condition=%wide.region_31.32_spmd, body=%wide.region_27.31_spmd.sunk | while | flops 1383462912 | bytes 191698832 | solution.py:344
  898.8 7.8 multiply_reduce_fusion.20
  921.9 12.5 reduce-scatter.47.cloned.1.call-done
  935.7 35.4 %reduce-scatter.45.cloned.1.call-done = bf16[128,1024]{1,0:T(8,128)(2,1)} async-done(((bf16[1024,1024]{1,0:T(8,128)(2,1)}), bf16[128,1024]{1,0:T(8,128)(2,1)}) %reduce-scatter.45.cloned.1.call-update) | async-done | bytes 262160 | tf_op jit(solution)/shard_map/while
  987.9 7.8 multiply_reduce_fusion.20
  1011.0 11.6 reduce-scatter.47.cloned.1.call-done
  1023.9 35.3 %reduce-scatter.45.cloned.1.call-done = bf16[128,1024]{1,0:T(8,128)(2,1)} async-done(((bf16[1024,1024]{1,0:T(8,128)(2,1)}), bf16[128,1024]{1,0:T(8,128)(2,1)}) %reduce-scatter.45.cloned.1.call-update) | async-done | bytes 262160 | tf_op jit(solution)/shard_map/while
  1064.0 5.2 multiply_reduce_fusion.4
  1071.5 6.9 fusion.45
  1097.0 4.7 convolution_bitcast_fusion.5
  1103.0 6.4 convolution_bitcast_fusion.4
  1110.5 10.4 convolution_bitcast_fusion
  1122.9 8.2 convolution_bitcast_fusion.1
  1132.3 10.4 convolution_bitcast_fusion.2
  1143.8 9.8 convolution_bitcast_fusion.3
  1156.1 60.1 %reduce-scatter.43.cloned.1.call-done = f32[32,6]{1,0:T(8,128)} async-done(((f32[1024,6]{1,0:T(8,128)}), f32[32,6]{1,0:T(8,128)}) %reduce-scatter.43.cloned.1.call-update) | async-done | bytes 784
  1217.6 130.6 %reduce-scatter.41.cloned.1.call-done = f32[32,31]{1,0:T(8,128)} async-done(((f32[1024,31]{1,0:T(8,128)}), f32[32,31]{1,0:T(8,128)}) %reduce-scatter.41.cloned.1.call-update) | async-done | bytes 3984
  1349.5 138.7 %reduce-scatter.35.cloned.1.call-done = f32[32,1024]{1,0:T(8,128)} async-done(((f32[1024,1024]{1,0:T(8,128)}), f32[32,1024]{1,0:T(8,128)}) %reduce-scatter.35.cloned.1.call-update) | async-done | bytes 131088 | tf_op jit(solution)/shard_map/reduce_scatter | solution.py:371
  1488.2 142.4 %reduce-scatter.31.cloned.1.call-done = f32[32,1024]{1,0:T(8,128)} async-done(((f32[1024,1024]{1,0:T(8,128)}), f32[32,1024]{1,0:T(8,128)}) %reduce-scatter.31.cloned.1.call-update) | async-done | bytes 131088 | tf_op jit(solution)/shard_map/reduce_scatter | solution.py:369
  1630.6 184.3 %reduce-scatter.33.cloned.1.call-done = f32[32,2048]{1,0:T(8,128)} async-done(((f32[1024,2048]{1,0:T(8,128)}), f32[32,2048]{1,0:T(8,128)}) %reduce-scatter.33.cloned.1.call-update) | async-done | bytes 262160 | tf_op jit(solution)/shard_map/reduce_scatter | solution.py:370
  1814.9 162.9 %reduce-scatter.29.cloned.1.call-done = f32[32,3072]{1,0:T(8,128)} async-done(((f32[1024,3072]{1,0:T(8,128)}), f32[32,3072]{1,0:T(8,128)}) %reduce-scatter.29.cloned.1.call-update) | async-done | bytes 393232 | tf_op jit(solution)/shard_map/reduce_scatter | solution.py:368
  1977.8 359.8 %reduce-scatter.39.cloned.1.call-done = f32[128,1024]{1,0:T(8,128)} async-done(((f32[4096,1024]{1,0:T(8,128)}), f32[128,1024]{1,0:T(8,128)}) %reduce-scatter.39.cloned.1.call-update) | async-done | bytes 524304 | tf_op jit(solution)/shard_map/reduce_scatter | solution.py:373
  2337.6 362.0 %reduce-scatter.37.cloned.1.call-done = f32[32,4096]{1,0:T(8,128)} async-done(((f32[1024,4096]{1,0:T(8,128)}), f32[32,4096]{1,0:T(8,128)}) %reduce-scatter.37.cloned.1.call-update) | async-done | bytes 524304 | tf_op jit(solution)/shard_map/reduce_scatter | solution.py:372
  2699.6 362.1 %reduce-scatter.27.cloned.1.call-done = f32[128,1024]{1,0:T(8,128)} async-done(((f32[4096,1024]{1,0:T(8,128)}), f32[128,1024]{1,0:T(8,128)}) %reduce-scatter.27.cloned.1.call-update) | async-done | bytes 524304 | tf_op jit(solution)/shard_map/reduce_scatter | solution.py:367
  3061.7 361.9 %reduce-scatter.25.cloned.1.call-done = f32[32,4096]{1,0:T(8,128)} async-done(((f32[1024,4096]{1,0:T(8,128)}), f32[32,4096]{1,0:T(8,128)}) %reduce-scatter.25.cloned.1.call-update) | async-done | bytes 524304 | tf_op jit(solution)/shard_map/reduce_scatter | solution.py:366
  (656 shorter events, 338.3 us)
Async XLA Ops:
  7.2 83.9 %all-gather.12.cloned.1.call-start = ((), (), s32[]{:S(2)}) async-start(), calls=%async_computation.12 | async-start | bytes 8650752 | tf_op jit(solution)/shard_map/all_gather | solution.py:236
  7.9 162.4 %all-gather.14.cloned.1.call-start = ((), (), s32[]{:S(2)}) async-start(), calls=%async_computation.13 | async-start | bytes 8650752 | tf_op jit(solution)/shard_map/all_gather | solution.py:237
  8.7 232.7 %all-gather.16.cloned.1.call-start = ((), (), s32[]{:S(2)}) async-start(), calls=%async_computation.14 | async-start | bytes 6488064 | tf_op jit(solution)/shard_map/all_gather | solution.py:238
  9.4 332.3 %all-gather.18.cloned.1.call-start = ((), (), s32[]{:S(2)}) async-start(), calls=%async_computation.15 | async-start | bytes 4718592 | tf_op jit(solution)/shard_map/all_gather | solution.py:267
  84.0 157.4 %copy-start.48 = (f32[1,1024]{1,0:T(1,128)}, f32[1,1024]{1,0:T(1,128)S(1)}, u32[]{:S(2)}) copy-start(f32[1,1024]{1,0:T(1,128)S(1)} %get-tuple-element.790) | copy-start | bytes 12292
  84.0 616.8 %copy-start.43 = (f32[1,1024]{1,0:T(1,128)}, f32[1,1024]{1,0:T(1,128)S(1)}, u32[]{:S(2)}) copy-start(f32[1,1024]{1,0:T(1,128)S(1)} %get-tuple-element.787) | copy-start | bytes 12292
  84.0 797.1 %copy-start.58 = (f32[1,1024]{1,0:T(1,128)}, f32[1,1024]{1,0:T(1,128)S(1)}, u32[]{:S(2)}) copy-start(f32[1,1024]{1,0:T(1,128)S(1)} %get-tuple-element.789) | copy-start | bytes 12292
  177.4 224.2 %copy-start.5 = (f32[2,128,1024]{2,1,0:T(8,128)}, f32[2,128,1024]{2,1,0:T(8,128)S(1)}, u32[]{:S(2)}) copy-start(f32[2,128,1024]{2,1,0:T(8,128)S(1)} %get-tuple-element.825) | copy-start | bytes 3145732
  248.7 99.2 %all-gather.20.cloned.1.call-start = ((), (), s32[]{:S(2)}) async-start(), calls=%async_computation.16 | async-start | bytes 4718592 | tf_op jit(solution)/shard_map/all_gather | solution.py:266
  259.3 142.3 %all-gather.22.cloned.1.call-start = ((), (), s32[]{:S(2)}) async-start(), calls=%async_computation.17 | async-start | bytes 2162688 | tf_op jit(solution)/shard_map/all_gather | solution.py:239
  259.9 205.5 %all-gather.24.cloned.1.call-start = ((), (), s32[]{:S(2)}) async-start(), calls=%async_computation.18 | async-start | bytes 4325376 | tf_op jit(solution)/shard_map/all_gather | solution.py:240
  260.6 262.6 %all-gather.26.cloned.1.call-start = ((), (), s32[]{:S(2)}) async-start(), calls=%async_computation.19 | async-start | bytes 2162688 | tf_op jit(solution)/shard_map/all_gather | solution.py:241
  261.4 341.2 %all-gather.28.cloned.1.call-start = ((), (), s32[]{:S(2)}) async-start(), calls=%async_computation.20 | async-start | bytes 8650752 | tf_op jit(solution)/shard_map/all_gather | solution.py:242
  262.1 419.3 %all-gather.30.cloned.1.call-start = ((), (), s32[]{:S(2)}) async-start(), calls=%async_computation.21 | async-start | bytes 8650752 | tf_op jit(solution)/shard_map/all_gather | solution.py:243
  340.7 136.9 %copy-start.90 = (f32[1024]{0:T(1024)}, f32[1024]{0:T(1024)S(1)}, u32[]{:S(2)}) copy-start(f32[1024]{0:T(1024)S(1)} %get-tuple-element.686) | copy-start | bytes 12292
  340.7 136.9 %copy-start.91 = (f32[1024]{0:T(1024)}, f32[1024]{0:T(1024)S(1)}, u32[]{:S(2)}) copy-start(f32[1024]{0:T(1024)S(1)} %get-tuple-element.687) | copy-start | bytes 12292
  340.7 136.9 %copy-start.92 = (f32[1024]{0:T(1024)}, f32[1024]{0:T(1024)S(1)}, u32[]{:S(2)}) copy-start(f32[1024]{0:T(1024)S(1)} %get-tuple-element.688) | copy-start | bytes 12292
  340.8 136.9 %copy-start.94 = (f32[1024]{0:T(1024)}, f32[1024]{0:T(1024)S(1)}, u32[]{:S(2)}) copy-start(f32[1024]{0:T(1024)S(1)} %get-tuple-element.689) | copy-start | bytes 12292
  340.8 136.9 %copy-start.95 = (f32[1024]{0:T(1024)}, f32[1024]{0:T(1024)S(1)}, u32[]{:S(2)}) copy-start(f32[1024]{0:T(1024)S(1)} %get-tuple-element.690) | copy-start | bytes 12292
  404.0 477.1 %copy-start.7 = (f32[2,128,1024]{2,1,0:T(8,128)}, f32[2,128,1024]{2,1,0:T(8,128)S(1)}, u32[]{:S(2)}) copy-start(f32[2,128,1024]{2,1,0:T(8,128)S(1)} %get-tuple-element.827) | copy-start | bytes 3145732
  470.6 233.9 %copy-start.9 = (bf16[2,128,1024]{2,1,0:T(8,128)(2,1)}, bf16[2,128,1024]{2,1,0:T(8,128)(2,1)S(1)}, u32[]{:S(2)}) copy-start(bf16[2,128,1024]{2,1,0:T(8,128)(2,1)S(1)} %multiply_convert_fusion.11) | copy-start | bytes 1572868
  470.6 7.0 collective-permute-start
  472.8 4.8 collective-permute-start.1
  477.6 383.9 %copy-start.46 = (bf16[2,15,1024]{2,1,0:T(8,128)(2,1)}, bf16[2,15,1024]{2,1,0:T(8,128)(2,1)S(1)}, u32[]{:S(2)}) copy-start(bf16[2,15,1024]{2,1,0:T(8,128)(2,1)S(1)} %collective-permute-done) | copy-start | bytes 184324
  485.9 216.7 %copy-start.165 = (f32[2,128]{1,0:T(2,128)}, f32[2,128]{1,0:T(2,128)S(1)}, u32[]{:S(2)}) copy-start(f32[2,128]{1,0:T(2,128)S(1)} %broadcast_multiply_fusion.14) | copy-start | bytes 3076
  486.1 216.4 %copy-start.172 = (f32[2,128]{1,0:T(2,128)}, f32[2,128]{1,0:T(2,128)S(1)}, u32[]{:S(2)}) copy-start(f32[2,128]{1,0:T(2,128)S(1)} %add_rsqrt_fusion.2) | copy-start | bytes 3076
  526.2 174.6 %copy-start.11 = (f32[2,128,1024]{2,1,0:T(8,128)}, f32[2,128,1024]{2,1,0:T(8,128)S(1)}, u32[]{:S(2)}) copy-start(f32[2,128,1024]{2,1,0:T(8,128)S(1)} %get-tuple-element.829) | copy-start | bytes 3145732
  526.2 174.6 %copy-start.70 = (f32[2,128]{1,0:T(2,128)}, f32[2,128]{1,0:T(2,128)S(1)}, u32[]{:S(2)}) copy-start(f32[2,128]{1,0:T(2,128)S(1)} %broadcast_multiply_fusion.13) | copy-start | bytes 3076
  526.5 174.3 %copy-start.74 = (f32[2,128]{1,0:T(2,128)}, f32[2,128]{1,0:T(2,128)S(1)}, u32[]{:S(2)}) copy-start(f32[2,128]{1,0:T(2,128)S(1)} %add_rsqrt_fusion.1) | copy-start | bytes 3076
  707.7 158.6 %copy-start = (f32[2,128,1024]{2,1,0:T(8,128)}, f32[2,128,1024]{2,1,0:T(8,128)S(1)}, u32[]{:S(2)}) copy-start(f32[2,128,1024]{2,1,0:T(8,128)S(1)} %get-tuple-element.751) | copy-start | bytes 3145732
  852.2 19.5 collective-permute-start.3
  853.5 18.2 collective-permute-start.2
  883.8 177.7 %copy-start.61 = (f32[2,128,32]{1,2,0:T(8,128)S(1)}, f32[2,128,32]{1,2,0:T(8,128)}, u32[]{:S(2)}) copy-start(f32[2,128,32]{1,2,0:T(8,128)} %copy-done.60) | copy-start | bytes 98308
  883.8 177.7 %copy-start.63 = (f32[2,128,32]{1,2,0:T(8,128)S(1)}, f32[2,128,32]{1,2,0:T(8,128)}, u32[]{:S(2)}) copy-start(f32[2,128,32]{1,2,0:T(8,128)} %copy-done.62) | copy-start | bytes 98308
  884.0 50.4 %reduce-scatter.47.cloned.1.call-start = ((), (), s32[]{:S(2)}) async-start(), calls=%async_computation.33 | async-start | bytes 2359296 | tf_op jit(solution)/shard_map/while
  898.7 72.5 %reduce-scatter.45.cloned.1.call-start = ((), (), s32[]{:S(2)}) async-start(), calls=%async_computation.32 | async-start | bytes 2359296 | tf_op jit(solution)/shard_map/while
  973.2 49.4 %reduce-scatter.47.cloned.1.call-start = ((), (), s32[]{:S(2)}) async-start(), calls=%async_computation.33 | async-start | bytes 2359296 | tf_op jit(solution)/shard_map/while
  987.8 71.4 %reduce-scatter.45.cloned.1.call-start = ((), (), s32[]{:S(2)}) async-start(), calls=%async_computation.32 | async-start | bytes 2359296 | tf_op jit(solution)/shard_map/while
  1061.2 154.9 %reduce-scatter.43.cloned.1.call-start = ((), (), s32[]{:S(2)}) async-start(), calls=%async_computation.31 | async-start | bytes 540672
  1083.5 264.6 %reduce-scatter.41.cloned.1.call-start = ((), (), s32[]{:S(2)}) async-start(), calls=%async_computation.30 | async-start | bytes 540672
  1087.3 400.9 %reduce-scatter.35.cloned.1.call-start = ((), (), s32[]{:S(2)}) async-start(), calls=%async_computation.27 | async-start | bytes 4325376 | tf_op jit(solution)/shard_map/reduce_scatter | solution.py:371
  1091.9 538.7 %reduce-scatter.31.cloned.1.call-start = ((), (), s32[]{:S(2)}) async-start(), calls=%async_computation.25 | async-start | bytes 4325376 | tf_op jit(solution)/shard_map/reduce_scatter | solution.py:369
  1095.8 719.1 %reduce-scatter.33.cloned.1.call-start = ((), (), s32[]{:S(2)}) async-start(), calls=%async_computation.26 | async-start | bytes 8650752 | tf_op jit(solution)/shard_map/reduce_scatter | solution.py:370
  1101.7 876.1 %reduce-scatter.29.cloned.1.call-start = ((), (), s32[]{:S(2)}) async-start(), calls=%async_computation.24 | async-start | bytes 12976128 | tf_op jit(solution)/shard_map/reduce_scatter | solution.py:368
  1109.5 1228.1 %reduce-scatter.39.cloned.1.call-start = ((), (), s32[]{:S(2)}) async-start(), calls=%async_computation.29 | async-start | bytes 17301504 | tf_op jit(solution)/shard_map/reduce_scatter | solution.py:373
  1121.0 1578.6 %reduce-scatter.37.cloned.1.call-start = ((), (), s32[]{:S(2)}) async-start(), calls=%async_computation.28 | async-start | bytes 17301504 | tf_op jit(solution)/shard_map/reduce_scatter | solution.py:372
  1131.1 1930.5 %reduce-scatter.27.cloned.1.call-start = ((), (), s32[]{:S(2)}) async-start(), calls=%async_computation.23 | async-start | bytes 17301504 | tf_op jit(solution)/shard_map/reduce_scatter | solution.py:367
  1142.8 2280.8 %reduce-scatter.25.cloned.1.call-start = ((), (), s32[]{:S(2)}) async-start(), calls=%async_computation.22 | async-start | bytes 17301504 | tf_op jit(solution)/shard_map/reduce_scatter | solution.py:366
  (168 other events, 4068.4 us)
Sparse Core Ops, SparseCore 0:
  10.9 80.1 all-gather.11
  94.0 76.2 all-gather.13
  173.2 68.1 all-gather.15
  248.8 46.1 all-gather.17
  297.0 47.0 all-gather.19
  346.8 54.7 all-gather.21
  404.5 60.8 all-gather.23
  468.2 54.9 all-gather.25
  526.1 76.3 all-gather.27
  605.3 76.1 all-gather.29
  898.8 35.5 reduce-scatter.46
  936.7 34.4 reduce-scatter.44
  987.9 34.6 reduce-scatter.46
  1024.8 34.3 reduce-scatter.44
  1083.6 132.4 reduce-scatter.42
  1218.4 129.7 reduce-scatter.40
  1350.8 137.3 reduce-scatter.34
  1490.9 139.6 reduce-scatter.30
  1633.5 181.4 reduce-scatter.32
  1821.4 156.3 reduce-scatter.28
  1980.8 356.7 reduce-scatter.38
  2340.6 358.9 reduce-scatter.36
  2702.6 359.0 reduce-scatter.26
  3064.5 359.0 reduce-scatter.24
where the time goes:
time: 3440 us; the launch traced here: 3430 us
  waiting for transfers between devices  2780 us (81%)
  local copies, waits for them, and re-layouts  182 us (5%)
  matrix products  179 us (5%)
  blocking collectives  142 us (4%)
  other arithmetic  116 us (3%)
    reduce_scatter x1, waiting for transfers between devices, per_device(): lax.psum_scatter(grad_ffn1_out, ('wide', 'rows'), scatter_dimension=0, ti...  362 us
    reduce_scatter x1, waiting for transfers between devices, per_device(): lax.psum_scatter(grad_ffn2_in, ('wide', 'rows'), scatter_dimension=0, til...  362 us
    reduce_scatter x1, waiting for transfers between devices, per_device(): lax.psum_scatter(grad_ffn1_in, ('wide', 'rows'), scatter_dimension=0, til...  362 us
    reduce_scatter x1, waiting for transfers between devices, per_device(): lax.psum_scatter(grad_ffn2_out, ('wide', 'rows'), scatter_dimension=0, ti...  360 us
    unnamed x22, waiting for transfers between devices  196 us
    reduce_scatter x1, waiting for transfers between devices, per_device(): lax.psum_scatter(grad_conv_in, ('wide', 'rows'), scatter_dimension=0, til...  184 us
    reduce_scatter x1, waiting for transfers between devices, per_device(): lax.psum_scatter(grad_qkv, ('wide', 'rows'), scatter_dimension=0, tiled=T...  163 us
    reduce_scatter x1, waiting for transfers between devices, per_device(): lax.psum_scatter(grad_attn_out, ('wide', 'rows'), scatter_dimension=0, ti...  142 us
  transfers between devices with their start and end apart: 28, of which 22 were waited for; matrix products, arithmetic and copies ran while one was open for 6% of the time, Pallas kernels for 0%

commit v1 on v0

v1 whole, which is shorter than its diff:
```python
import functools

import jax
import jax.numpy as jnp
import numpy as np
from jax import lax
from jax.experimental import pallas as pl
from jax.experimental.pallas import tpu as pltpu
from jax.sharding import PartitionSpec as P

HEADS = 16
HEAD_DIM = 64
EPSILON = 1e-05
BOTH = ("wide", "rows")
F32 = jnp.float32
BF16 = jnp.bfloat16
HIGHEST = lax.Precision.HIGHEST
VMEM_LIMIT = 60 * 1024 * 1024


class Plan:
    def __init__(self, wide, rows):
        self.wide, self.rows, self.total = wide, rows, wide * rows
        self.far = [k * 2 * rows for k in range(1, wide // 2)]
        row_bits = [1 << b for b in range(rows.bit_length() - 1)]
        self.flips = (row_bits, row_bits[1:] + row_bits[:1])
        self.stages = len(row_bits)
        self.far_bits = [1 << b for b in range((wide // 2).bit_length() - 1)]
        self.blocks = self.total // 2
        self.table = [
            np.array(
                [
                    far ^ sum(f for t, f in enumerate(flips) if p >> t & 1)
                    for p in range(1 << self.stages)
                    for far in [0, *self.far]
                ],
                np.int32,
            )
            for flips in self.flips
        ]

    def core_of(self, index):
        return (index // self.rows) % 2

    def stage_pairs(self, stage):
        return [(i, i ^ self.flips[self.core_of(i)][stage]) for i in range(self.total)]

    def flip_pairs(self, flip):
        return [(i, i ^ flip) for i in range(self.total)]

    def orders(self):
        index = lax.axis_index(BOTH)
        core = self.core_of(index)
        table = jnp.stack([jnp.asarray(t) for t in self.table])
        own = index ^ jnp.take(table, core, axis=0)
        other = (index ^ self.rows) ^ jnp.take(table, 1 - core, axis=0)
        return own, other


def send(x, pairs):
    return lax.ppermute(x, BOTH, pairs)


def held(arrays):
    return [pl.BlockSpec(memory_space=pl.ANY)] * len(arrays)


def there(tokens, before=None):
    tokens = jax.tree.leaves((tokens, before))
    if not tokens:
        return None

    def kernel(*refs):
        refs[-1][0] = 1

    return pl.pallas_call(
        kernel,
        out_shape=jax.ShapeDtypeStruct((1,), jnp.int32),
        in_specs=held(tokens),
        out_specs=pl.BlockSpec(memory_space=pltpu.SMEM),
        cost_estimate=pl.CostEstimate(flops=0, transcendentals=0, bytes_accessed=0),
        name="there",
    )(*tokens)


def after(values, tokens, before=None):
    flag = there(tokens, before) if jax.tree.leaves(tokens) else before
    if flag is None or not jax.tree.leaves(values):
        return values
    flag = flag[0] > 0
    return jax.tree.map(lambda x: jnp.where(flag, x, jnp.zeros((), x.dtype)), values)


class Lane:
    def __init__(self, steps):
        self.steps, self.result, self.arriving = steps, None, None
        self.operand, self.pairs = next(steps)

    def go(self):
        if isinstance(self.pairs[0], list):
            self.arriving = [send(x, pairs) for x, pairs in zip(self.operand, self.pairs)]
        else:
            self.arriving = jax.tree.map(lambda x: send(x, self.pairs), self.operand)

    def landed(self, arrived):
        self.arriving = None
        try:
            self.operand, self.pairs = self.steps.send(arrived)
        except StopIteration as stop:
            self.operand, self.result = None, stop.value


def step(land=(), go=(), chain=(), since=()):
    land = [lane for lane in land if lane.arriving is not None]
    flag = there(list(since)) if since else None
    for lane in land:
        lane.landed(after(lane.arriving, [], flag))
    if jax.tree.leaves(chain):
        chain = after(chain, jax.tree.leaves(ready(*land)))
    for lane in go:
        if lane.operand is not None and lane.arriving is None:
            lane.go()
    return chain


def hold(lane, *tokens):
    lane.operand = after(lane.operand, list(tokens))
    lane.go()


def waited(*lanes):
    return [lane.arriving for lane in lanes if lane.arriving is not None]


def ready(*lanes):
    return [lane.operand for lane in lanes if lane.operand is not None]


def finish(*lanes):
    while any(lane.operand is not None for lane in lanes):
        for lane in lanes:
            step(land=[lane], go=[lane])
    return lanes[0].result


def gather_lane(plan, shard, finish):
    held = shard[None]
    for bit in reversed(plan.far_bits):
        pairs = plan.flip_pairs(bit * 2 * plan.rows)
        arrived = yield held, pairs
        held = jnp.stack([held, arrived], axis=1).reshape(-1, *shard.shape)
    for stage in range(plan.stages - 1):
        held = jnp.concatenate([held, (yield held, plan.stage_pairs(stage))], axis=0)
    last = yield held, plan.stage_pairs(plan.stages - 1)
    from_core = yield [held, last], plan.flip_pairs(plan.rows)
    return finish([held, last, *from_core])


def grad_lane(plan, own, other, right, small=None):
    swapped = yield [other, right], plan.flip_pairs(plan.rows)
    left = jnp.concatenate([own, swapped[0]], axis=0)
    both = jnp.concatenate([right, swapped[1]], axis=0)
    left, both = lax.optimization_barrier((left, both))
    half = left.shape[1] // 2
    away = [dot_over_frames(left[:, half:], both).astype(BF16)]
    kept = None
    if small:
        little = small()
        columns = little.shape[1] // 2
        away.append(after(little[:, columns:], away[0]))
        little = little[:, :columns]
    for stage in reversed(range(plan.stages)):
        arrived = yield away, plan.stage_pairs(stage)
        if kept is None:
            kept = dot_over_frames(left[:, :half], both).astype(BF16)
        if small:
            little = little + after(arrived[1], arrived[0])
        if stage > 0:
            half = kept.shape[0] // 2
            away = [(kept[half:].astype(F32) + arrived[0][half:].astype(F32)).astype(BF16)]
            kept = kept[:half].astype(F32) + arrived[0][:half].astype(F32)
            kept = kept.astype(BF16)
            if small:
                columns = little.shape[1] // 2
                away.append(little[:, columns:])
                little = little[:, :columns]
    size = kept.shape[0] // (len(plan.far) + 1)
    away = []
    for block in range(1, len(plan.far) + 1):
        rows = slice(block * size, (block + 1) * size)
        away.append([(kept[rows].astype(F32) + arrived[0][rows].astype(F32)).astype(BF16)])
    total = kept[:size].astype(F32) + arrived[0][:size].astype(F32)
    if small:
        size = little.shape[1] // (len(plan.far) + 1)
        for block in range(1, len(plan.far) + 1):
            away[block - 1].append(little[:, block * size : (block + 1) * size])
        little = little[:, :size]
    arrived = yield (
        [x for pair in away for x in pair],
        [plan.flip_pairs(far) for far in plan.far for _ in range(2 if small else 1)],
    )
    step = 2 if small else 1
    for one in arrived[::step]:
        total = total + one.astype(F32)
    if small:
        little = little + sum(after(arrived[1::2], arrived[::2]))
    return (total, little) if small else total


def heads_lane(plan, x):
    sent = x.reshape(plan.wide // 2, 2, *x.shape[1:])
    from_core = yield sent[:, 1], plan.flip_pairs(plan.rows)
    pair = jnp.stack([sent[:, 0], from_core], axis=1)
    arrived = yield (
        [pair[k] for k in range(1, plan.wide // 2)],
        [plan.flip_pairs(far) for far in plan.far],
    )
    return jnp.stack([pair[0], *arrived]).reshape(x.shape)


def assemble(plan, pieces, shapes, orders):
    half = plan.blocks // 2
    width = pieces[0].shape[-1]
    index = jnp.concatenate(orders)
    if any(rows % 16 for rows, _ in shapes):
        stacked = jnp.concatenate(pieces, axis=0)
        place = jnp.zeros((plan.total,), jnp.int32).at[index].set(jnp.arange(plan.total))
        stacked = jnp.take(stacked, place, axis=0)
        outs, start = [], 0
        for rows, columns in shapes:
            parts = []
            for _ in range(columns // width):
                parts.append(stacked[:, start : start + rows].reshape(-1, width))
                start += rows
            outs.append(jnp.concatenate(parts, axis=1))
        return outs

    def kernel(order, *refs):
        sources, outs = refs[:4], refs[4:-3]
        held, in_sems, out_sems = refs[-3:]
        loads = [
            pltpu.make_async_copy(sources[which], held.at[which], in_sems.at[which])
            for which in range(4)
        ]
        for load in loads:
            load.start()
        for which in range(4):
            loads[which].wait()
            for place in range(half):
                block = order[which * half + place]
                start = 0
                for out, (rows, columns) in enumerate(shapes):
                    for part in range(columns // width):
                        pltpu.make_async_copy(
                            held.at[which, place, pl.ds(start, rows)],
                            outs[out].at[
                                pl.ds(pl.multiple_of(block * rows, rows), rows),
                                pl.ds(part * width, width),
                            ],
                            out_sems.at[out],
                        ).start()
                        start += rows
        for out in range(len(shapes)):
            pltpu.make_async_copy(outs[out], outs[out], out_sems.at[out]).wait()

    return pl.pallas_call(
        kernel,
        out_shape=[
            jax.ShapeDtypeStruct((rows * plan.total, columns), BF16) for rows, columns in shapes
        ],
        in_specs=[pl.BlockSpec(memory_space=pltpu.SMEM)] + [pl.BlockSpec(memory_space=pl.ANY)] * 4,
        out_specs=[pl.BlockSpec(memory_space=pl.ANY)] * len(shapes),
        scratch_shapes=[
            pltpu.VMEM((4,) + pieces[0].shape, BF16),
            pltpu.SemaphoreType.DMA((4,)),
            pltpu.SemaphoreType.DMA((len(shapes),)),
        ],
        compiler_params=pltpu.CompilerParams(vmem_limit_bytes=24 * 1024 * 1024),
        cost_estimate=pl.CostEstimate(
            flops=0, transcendentals=0, bytes_accessed=8 * pieces[0].size * 2
        ),
        name="assemble",
    )(index, *pieces)


def pick_columns(plan, x, orders):
    index = jnp.concatenate(orders)
    length, columns = x.shape
    size = columns // plan.total
    if size % 128:
        split = jnp.take(x.reshape(length, plan.total, size), index, axis=1)
        split = split.reshape(length, columns)
        return split[:, : columns // 2], split[:, columns // 2 :]

    def kernel(order, source, first, second):
        for place in range(plan.total):
            out = (first, second)[place // plan.blocks]
            start = pl.multiple_of(order[place] * size, size)
            out[:, pl.ds((place % plan.blocks) * size, size)] = source[:, pl.ds(start, size)]

    whole = pl.BlockSpec(memory_space=pltpu.VMEM)
    return pl.pallas_call(
        kernel,
        out_shape=[jax.ShapeDtypeStruct((length, columns // 2), x.dtype)] * 2,
        in_specs=[pl.BlockSpec(memory_space=pltpu.SMEM), whole],
        out_specs=[whole] * 2,
        compiler_params=pltpu.CompilerParams(vmem_limit_bytes=16 * 1024 * 1024),
        cost_estimate=pl.CostEstimate(
            flops=0, transcendentals=0, bytes_accessed=4 * x.size
        ),
        name="pick_columns",
    )(index, x)


def dot(left, right):
    return jnp.dot(left, right, preferred_element_type=F32)


def dot_back(left, right):
    return lax.dot_general(left, right, (((1,), (1,)), ((), ())), preferred_element_type=F32)


def dot_over_frames(left, right):
    return lax.dot_general(left, right, (((0,), (0,)), ((), ())), preferred_element_type=F32)


def head_lanes(size, head):
    lane = lax.broadcasted_iota(jnp.int32, (1, size), 1)
    return (lane >= head * HEAD_DIM) & (lane < (head + 1) * HEAD_DIM)


def attend_kernel(q_ref, k_ref, v_ref, idq_ref, idk_ref, o_ref, total_ref):
    size = q_ref.shape[-1]
    query, keys, values = q_ref[0] * HEAD_DIM**-0.5, k_ref[0], v_ref[0]
    same = idq_ref[0] == idk_ref[0]
    mixed = jnp.zeros(query.shape, F32)
    totals = []
    for head in range(size // HEAD_DIM):
        lanes = head_lanes(size, head)
        scores = lax.dot_general(
            jnp.where(lanes, query, 0), keys, (((1,), (1,)), ((), ())), preferred_element_type=F32
        )
        scores = jnp.where(same, scores, -1e30)
        most = jnp.max(scores, axis=-1, keepdims=True)
        unnormed = jnp.exp(scores - most)
        total = jnp.sum(unnormed, axis=-1, keepdims=True)
        probs = (unnormed * (1.0 / total)).astype(BF16)
        mixed += jnp.dot(probs, jnp.where(lanes, values, 0), preferred_element_type=F32)
        totals.append(most + jnp.log(total))
    o_ref[0] = mixed.astype(BF16)
    total_ref[0] = jnp.concatenate(totals, axis=1)


def attend_back_kernel(
    q_ref, k_ref, v_ref, o_ref, do_ref, total_ref, idq_ref, idk_ref, cq_ref, sq_ref, ck_ref,
    sk_ref, turn_ref, dq_ref, dk_ref, dv_ref, dk_sum, dv_sum,
):
    step = pl.program_id(1)
    size = q_ref.shape[-1]
    scale = HEAD_DIM**-0.5
    query, keys, values, grads = q_ref[0] * scale, k_ref[0], v_ref[0], do_ref[0]
    different = idk_ref[0] != idq_ref[0]
    product = grads.astype(F32) * o_ref[0].astype(F32)

    @pl.when(step == 0)
    def _():
        dk_sum[...] = jnp.zeros_like(dk_sum)
        dv_sum[...] = jnp.zeros_like(dv_sum)

    turned_sum = jnp.zeros((size, query.shape[0]), F32)
    for head in range(size // HEAD_DIM):
        lanes = head_lanes(size, head)
        one_query = jnp.where(lanes, query, 0)
        one_grad = jnp.where(lanes, grads, 0)
        delta = lax.dot_general(
            jnp.where(lanes, jnp.ones((8, size), F32), 0.0),
            product,
            (((1,), (1,)), ((), ())),
            precision=HIGHEST,
            preferred_element_type=F32,
        )[:1]
        scores = lax.dot_general(
            keys, one_query, (((1,), (1,)), ((), ())), preferred_element_type=F32
        )
        probs = jnp.exp(jnp.where(different, -1e30, scores - total_ref[0, head : head + 1]))
        prob_grads = lax.dot_general(
            values, one_grad, (((1,), (1,)), ((), ())), preferred_element_type=F32
        )
        score_grads = (probs * (prob_grads - delta)).astype(BF16)
        dk_sum[...] += jnp.dot(score_grads, one_query, preferred_element_type=F32)
        dv_sum[...] += jnp.dot(probs.astype(BF16), one_grad, preferred_element_type=F32)
        turned_sum += dot_over_frames(jnp.where(lanes, keys, 0), score_grads)

    def turned(grad, cosine, sine):
        partner = jnp.dot(grad, turn_ref[...], precision=HIGHEST, preferred_element_type=F32)
        return (grad * cosine + partner * sine).astype(BF16)

    dq_ref[0] = turned(turned_sum.T * scale, cq_ref[0], sq_ref[0])

    @pl.when(step == pl.num_programs(1) - 1)
    def _():
        dk_ref[0] = turned(dk_sum[...], ck_ref[0], sk_ref[0])
        dv_ref[0] = dv_sum[...].astype(BF16)


def attend(query, keys, values, ids, tokens=()):
    rows, length, size = query.shape
    tile = 256
    heads = size // HEAD_DIM
    whole = pl.BlockSpec((1, length, size), lambda r, t: (r, 0, 0))
    part = pl.BlockSpec((1, tile, size), lambda r, t: (r, t, 0))
    return pl.pallas_call(
        lambda *refs: attend_kernel(*refs[:5], *refs[5 + len(tokens) :]),
        out_shape=[
            jax.ShapeDtypeStruct(query.shape, BF16),
            jax.ShapeDtypeStruct((rows, length, heads), F32),
        ],
        grid=(rows, length // tile),
        in_specs=[
            part,
            whole,
            whole,
            pl.BlockSpec((1, tile, 1), lambda r, t: (r, t, 0)),
            pl.BlockSpec((1, 1, length), lambda r, t: (r, 0, 0)),
            *held(tokens),
        ],
        out_specs=[part, pl.BlockSpec((1, tile, heads), lambda r, t: (r, t, 0))],
        compiler_params=pltpu.CompilerParams(vmem_limit_bytes=VMEM_LIMIT),
        name="attend",
    )(query, keys, values, ids[:, :, None], ids[:, None, :], *tokens)


def attend_back(query, keys, values, mixed, grads, totals, ids, cosine, sine, tokens=()):
    rows, length, size = query.shape
    tile = 256
    heads = size // HEAD_DIM
    whole = pl.BlockSpec((1, length, size), lambda r, t: (r, 0, 0))
    part = pl.BlockSpec((1, tile, size), lambda r, t: (r, t, 0))
    lane = np.arange(size)
    turn = jnp.asarray((lane[:, None] == (lane ^ (HEAD_DIM // 2))[None, :]).astype(np.float32))
    return pl.pallas_call(
        lambda *refs: attend_back_kernel(*refs[:13], *refs[13 + len(tokens) :]),
        out_shape=[jax.ShapeDtypeStruct(query.shape, BF16)] * 3,
        grid=(rows, length // tile),
        in_specs=[
            part,
            whole,
            whole,
            part,
            part,
            pl.BlockSpec((1, heads, tile), lambda r, t: (r, 0, t)),
            pl.BlockSpec((1, 1, tile), lambda r, t: (r, 0, t)),
            pl.BlockSpec((1, length, 1), lambda r, t: (r, 0, 0)),
            part,
            part,
            whole,
            whole,
            pl.BlockSpec((size, size), lambda r, t: (0, 0)),
            *held(tokens),
        ],
        out_specs=[part, whole, whole],
        scratch_shapes=[pltpu.VMEM((length, size), F32)] * 2,
        compiler_params=pltpu.CompilerParams(vmem_limit_bytes=VMEM_LIMIT),
        name="attend_back",
    )(
        query, keys, values, mixed, grads, totals.transpose(0, 2, 1), ids[:, None, :],
        ids[:, :, None], cosine, sine, cosine, sine, turn, *tokens,
    )


def set_masks(ids_ref, ids, masks, count):
    ids[...] = jnp.broadcast_to(ids_ref[0], ids.shape)
    here = ids[pl.ds(masks.shape[0] // 2, count)]
    for tap in range(masks.shape[0]):
        masks[tap] = jnp.where(ids[pl.ds(tap, count)] == here, 1.0, 0.0)


def conv_kernel(ext_ref, ids_ref, taps_ref, out_ref, frames, ids, masks):
    count, taps = out_ref.shape[1], taps_ref.shape[0]

    @pl.when(pl.program_id(1) == 0)
    def _():
        set_masks(ids_ref, ids, masks, count)

    frames[...] = ext_ref[0].astype(F32)
    total = jnp.zeros((count, frames.shape[1]), F32)
    for odd in range(8):
        shifted = frames[pl.ds(odd, frames.shape[0] - 8)]
        for tap in range(odd, taps, 8):
            part = shifted[tap - odd : tap - odd + count]
            total += part * masks[tap] * taps_ref[tap : tap + 1]
    out_ref[0] = total


def conv_back_kernel(
    ext_ref, ids_ref, grad_ref, taps_ref, dtaps_ref, dext_ref, frames, ids, masks, total, some
):
    count, taps = grad_ref.shape[1], taps_ref.shape[0]

    @pl.when(pl.program_id(1) == 0)
    def _():
        set_masks(ids_ref, ids, masks, count)

    frames[...] = ext_ref[0].astype(F32)
    grad = grad_ref[0]
    total[...] = jnp.zeros_like(total)
    rows = [None] * taps
    for odd in range(8):
        shifted = frames[pl.ds(odd, frames.shape[0] - 8)]
        some[...] = jnp.zeros_like(some)
        for tap in range(odd, taps, 8):
            kept = grad * masks[tap]
            rows[tap] = jnp.sum(shifted[tap - odd : tap - odd + count] * kept, axis=0, keepdims=True)
            some[pl.ds(tap - odd, count)] += kept * taps_ref[tap : tap + 1]
        total[pl.ds(odd, some.shape[0])] += some[...]
    dext_ref[0] = total[...]
    dtaps_ref[0] = jnp.concatenate(rows, axis=0)


def depthwise(extended, ids, taps, tokens=()):
    rows, padded, width = extended.shape
    count = padded - 32
    block = 128
    return pl.pallas_call(
        lambda *refs: conv_kernel(*refs[:3], *refs[3 + len(tokens) :]),
        out_shape=jax.ShapeDtypeStruct((rows, count, width), F32),
        grid=(rows, width // block),
        in_specs=[
            pl.BlockSpec((1, padded, block), lambda r, c: (r, 0, c)),
            pl.BlockSpec((1, padded, 1), lambda r, c: (r, 0, 0)),
            pl.BlockSpec((taps.shape[0], block), lambda r, c: (0, c)),
            *held(tokens),
        ],
        out_specs=pl.BlockSpec((1, count, block), lambda r, c: (r, 0, c)),
        scratch_shapes=[pltpu.VMEM((padded, block), F32)] * 2
        + [pltpu.VMEM((taps.shape[0], count, block), F32)],
        compiler_params=pltpu.CompilerParams(vmem_limit_bytes=16 * 1024 * 1024),
        name="depthwise",
    )(extended, ids, taps, *tokens)


def depthwise_back(extended, ids, grad, taps, tokens=()):
    rows, padded, width = extended.shape
    count = padded - 32
    block = 128
    return pl.pallas_call(
        lambda *refs: conv_back_kernel(*refs[:4], *refs[4 + len(tokens) :]),
        out_shape=[
            jax.ShapeDtypeStruct((rows, taps.shape[0], width), F32),
            jax.ShapeDtypeStruct((rows, padded, width), F32),
        ],
        grid=(rows, width // block),
        in_specs=[
            pl.BlockSpec((1, padded, block), lambda r, c: (r, 0, c)),
            pl.BlockSpec((1, padded, 1), lambda r, c: (r, 0, 0)),
            pl.BlockSpec((1, count, block), lambda r, c: (r, 0, c)),
            pl.BlockSpec((taps.shape[0], block), lambda r, c: (0, c)),
            *held(tokens),
        ],
        out_specs=[
            pl.BlockSpec((1, taps.shape[0], block), lambda r, c: (r, 0, c)),
            pl.BlockSpec((1, padded, block), lambda r, c: (r, 0, c)),
        ],
        scratch_shapes=[pltpu.VMEM((padded, block), F32)] * 2
        + [
            pltpu.VMEM((taps.shape[0], count, block), F32),
            pltpu.VMEM((padded, block), F32),
            pltpu.VMEM((padded - 8, block), F32),
        ],
        compiler_params=pltpu.CompilerParams(vmem_limit_bytes=16 * 1024 * 1024),
        name="depthwise_back",
    )(extended, ids, grad, taps, *tokens)


def segment_info(lengths, frame_total):
    segment_end = jnp.cumsum(lengths, axis=-1, dtype=jnp.int32)
    frame_index = jnp.arange(frame_total, dtype=jnp.int32)
    passed = (frame_index[None, None, :] >= segment_end[:, :, None]).astype(jnp.int32)
    segment_ids = jnp.sum(passed, axis=1, dtype=jnp.int32)
    seg_starts = jnp.sum(passed * lengths[:, :, None], axis=1, dtype=jnp.int32)
    return (segment_ids, frame_index[None, :] - seg_starts)


def layer_norm(values, gain_row):
    centred = values - jnp.mean(values, axis=-1, keepdims=True)
    inv_scale = lax.rsqrt(jnp.mean(centred * centred, axis=-1, keepdims=True) + EPSILON)
    normed = centred * inv_scale
    return (normed * gain_row, normed, inv_scale)


def norm_backward(gradient, gain_row, normed, inv_scale):
    scaled = gradient * gain_row
    gain_grad = jnp.sum(gradient * normed, axis=0)
    centred_mean = jnp.mean(scaled, axis=-1, keepdims=True)
    product_mean = jnp.mean(scaled * normed, axis=-1, keepdims=True)
    return (inv_scale * (scaled - centred_mean - normed * product_mean), gain_grad)


def swish_slope(values):
    gate_sig = jax.nn.sigmoid(values)
    return gate_sig * (1.0 + values * (1.0 - gate_sig))


def neighbours(x, width, axis):
    size, length = lax.axis_size("wide"), x.shape[axis]
    up = [(i, i + 1) for i in range(size - 1)]
    before = lax.ppermute(lax.slice_in_dim(x, length - width, length, axis=axis), "wide", up)
    after = lax.ppermute(
        lax.slice_in_dim(x, 0, width, axis=axis), "wide", [(j, i) for i, j in up]
    )
    return before, after


def half_turn(values):
    half = HEAD_DIM // 2
    lane = lax.broadcasted_iota(jnp.int32, (1, values.shape[-1]), 1) % HEAD_DIM
    ahead = jnp.roll(values, -half, axis=-1)
    behind = jnp.roll(values, half, axis=-1)
    return jnp.where(lane < half, -ahead, behind)


def per_device(
    inputs,
    lengths,
    ffn1_in,
    ffn1_out,
    attn_qkv,
    attn_out,
    conv_in,
    depth_kernel,
    conv_out,
    ffn2_in,
    ffn2_out,
    norm_gains,
    cotangent,
):
    wide, rows = lax.axis_size("wide"), lax.axis_size("rows")
    plan = Plan(wide, rows)
    row_count, frames_here, width = inputs.shape
    tokens = row_count * frames_here
    frame_total = frames_here * wide
    taps = depth_kernel.shape[0]
    half_width = taps // 2
    me = lax.axis_index("wide")
    orders = plan.orders()
    segment_ids, position = segment_info(lengths, frame_total)

    def packed_shards(shards):
        parts = []
        for shard in shards:
            for column in range(0, shard.shape[1], width):
                parts.append(shard[:, column : column + width])
        return jnp.concatenate(parts, axis=0) if len(parts) > 1 else parts[0]

    def weights_lane(*shards):
        shapes = [shard.shape for shard in shards]
        return Lane(
            gather_lane(
                plan, packed_shards(shards), lambda held: assemble(plan, held, shapes, orders)
            )
        )

    def small_lane(small):
        flip = 1
        while flip < plan.total:
            small = jnp.concatenate([small, (yield small, plan.flip_pairs(flip))], axis=1)
            flip *= 2
        return dot_back(small, small_pick.astype(BF16))

    feature = jnp.arange(width, dtype=jnp.int32)
    block = width // plan.total
    small_source = (feature // block ^ lax.axis_index(BOTH)) * block + feature % block
    small_pick = feature[:, None] == small_source[None, :]
    small = Lane(small_lane(jnp.concatenate([norm_gains, depth_kernel], axis=0)))
    g1, g2 = weights_lane(ffn1_in), weights_lane(ffn1_out)
    w_qkv = lax.all_gather(attn_qkv, BOTH, axis=0, tiled=True)
    wides = (attn_out, conv_in, conv_out, ffn2_in)

    def late_weights(*tokens):
        shards = after((jnp.concatenate(wides, axis=1), ffn2_out), list(tokens))
        middle = lax.all_gather(shards[0], BOTH, axis=0, tiled=True)
        cuts = np.cumsum([0] + [shard.shape[1] for shard in wides])
        parts = tuple(middle[:, start:stop] for start, stop in zip(cuts[:-1], cuts[1:]))
        return parts + (lax.all_gather(shards[1], BOTH, axis=0, tiled=True),)

    source = jnp.repeat(jnp.concatenate(orders), block) * block + feature % block
    tree_pick = (feature[:, None] == source[None, :]).astype(BF16)
    group = width // wide
    head_source = (feature // group ^ me) * group + feature % group
    head_pick = (feature[:, None] == head_source[None, :]).astype(BF16)

    def pick(x):
        both = dot(x, tree_pick).astype(BF16)
        return both[:, : width // 2], both[:, width // 2 :]

    def to_groups(x):
        return dot(x, head_pick).astype(BF16).reshape(tokens, wide, group).transpose(1, 0, 2)

    def from_groups(x):
        return dot_back(x.transpose(1, 0, 2).reshape(tokens, width), head_pick).astype(BF16)

    offset = me * frames_here
    padded_ids = jnp.pad(segment_ids, ((0, 0), (half_width, 32 - half_width)), constant_values=-1)
    edge_ids = lax.dynamic_slice_in_dim(padded_ids, offset, frames_here + 32, 1)
    edge_ids = edge_ids.astype(F32)[:, :, None]
    local_position = lax.dynamic_slice_in_dim(position, offset, frames_here, 1)
    by_device = jnp.arange(wide, dtype=jnp.int32) ^ me

    def row_order(x):
        x = x.reshape(row_count, wide, frames_here)
        return jnp.take(x, by_device, axis=1).reshape(row_count, frame_total)

    row_ids, row_position = row_order(segment_ids), row_order(position)

    def rotation(at, size):
        lane = jnp.arange(size, dtype=jnp.int32) % HEAD_DIM
        frequency = jnp.power(
            10000.0, -2.0 * (lane % (HEAD_DIM // 2)).astype(F32) / HEAD_DIM
        )
        angles = at.astype(F32)[..., None] * frequency
        sign = jnp.where(lane < HEAD_DIM // 2, 1.0, -1.0)
        return jnp.cos(angles), jnp.sin(angles), sign

    cosine, sine, _ = rotation(local_position.reshape(tokens), HEAD_DIM)
    cosine = jnp.tile(cosine, (1, HEADS))
    sine = jnp.tile(sine, (1, HEADS))
    row_cosine, row_sine, sign = rotation(row_position, group)
    row_sine = row_sine * sign

    tables = (row_cosine, row_sine, cosine, sine, edge_ids)
    def follow(lane, leader):
        lane.operand = after(lane.operand, jax.tree.leaves(ready(leader)))
        lane.go()

    step(go=[g1, small])
    for _ in range(3):
        step(land=[small], go=[small])
    step(land=[g1, small], go=[small])
    follow(g1, small)
    finish(small)
    gains, kernel = small.result[: norm_gains.shape[0]], small.result[norm_gains.shape[0] :]
    residual = inputs.astype(F32).reshape(tokens, width)
    ffn1_norm, ffn1_normed, ffn1_scale = layer_norm(residual, gains[0])
    ffn1_hidden = after(ffn1_norm.astype(BF16), tables)
    follow(g2, g1)
    step(land=[g1])
    g1.operand = after(g1.operand, [gains])
    g1.go()
    step(land=[g2])
    follow(g2, g1)
    for _ in range(2):
        step(land=[g1], go=[g1])
        step(land=[g2])
        follow(g2, g1)
    w_attn_out, w_conv_in, w_conv_out, w_ffn2_in, w_ffn2_out = late_weights(*ready(g2))
    (w_ffn1_in,) = finish(g1)
    before_1 = dot(ffn1_hidden, w_ffn1_in)
    after_1 = (before_1 * jax.nn.sigmoid(before_1)).astype(BF16)
    (w_ffn1_out,) = finish(g2)
    first = residual + 0.5 * dot(after_1, w_ffn1_out)
    attn_norm, attn_normed, attn_scale = layer_norm(first, gains[1])
    attn_hidden = attn_norm.astype(BF16)
    packed = dot(attn_hidden, w_qkv)
    queries = packed[:, :width]
    keys = packed[:, width : 2 * width]
    queries = (queries * cosine + half_turn(queries) * sine).astype(BF16)
    keys = (keys * cosine + half_turn(keys) * sine).astype(BF16)
    values = packed[:, 2 * width :].astype(BF16)
    heads = Lane(
        heads_lane(
            plan,
            jnp.concatenate([to_groups(queries), to_groups(keys), to_groups(values)], axis=-1),
        )
    )

    def as_rows(x):
        x = x.reshape(wide, row_count, frames_here, group)
        return x.transpose(1, 0, 2, 3).reshape(row_count, frame_total, group)

    def as_blocks(x):
        x = x.reshape(row_count, wide, frames_here, group)
        return x.transpose(1, 0, 2, 3).reshape(wide, tokens, group)

    arrived = finish(heads)
    row_queries = as_rows(arrived[..., :group])
    row_keys = as_rows(arrived[..., group : 2 * group])
    row_values = as_rows(arrived[..., 2 * group :])
    mixed_rows, row_totals = attend(row_queries, row_keys, row_values, row_ids)
    heads = Lane(heads_lane(plan, as_blocks(mixed_rows)))
    mixed = from_groups(finish(heads))
    second = first + dot(mixed, w_attn_out)
    conv_norm, conv_normed, conv_scale = layer_norm(second, gains[2])
    conv_hidden = conv_norm.astype(BF16)
    gated = dot(conv_hidden, w_conv_in)
    gate_sig = jax.nn.sigmoid(gated[:, width:])
    glu = (gated[:, :width] * gate_sig).astype(BF16).reshape(row_count, frames_here, width)
    before, after_frames = neighbours(glu, half_width, 1)
    extended = jnp.concatenate(
        [before, glu, after_frames, jnp.zeros((row_count, 32 - 2 * half_width, width), BF16)],
        axis=1,
    )
    convolved = depthwise(extended, edge_ids, kernel).reshape(tokens, width)
    inner_out, inner_normed, inner_scale = layer_norm(convolved, gains[3])
    activated = (inner_out * jax.nn.sigmoid(inner_out)).astype(BF16)
    third = second + dot(activated, w_conv_out)
    ffn2_norm, ffn2_normed, ffn2_scale = layer_norm(third, gains[4])
    ffn2_hidden = ffn2_norm.astype(BF16)
    before_2 = dot(ffn2_hidden, w_ffn2_in)
    after_2 = (before_2 * jax.nn.sigmoid(before_2)).astype(BF16)
    fourth = third + 0.5 * dot(after_2, w_ffn2_out)
    final_out, final_normed, final_scale = layer_norm(fourth, gains[5])
    layer_out = final_out.astype(BF16).reshape(inputs.shape)

    def grads(left, right, small=None):
        return Lane(grad_lane(plan, *left, right, small))

    gradient, gain_final = norm_backward(
        cotangent.astype(F32).reshape(tokens, width), gains[5], final_normed, final_scale
    )
    branch = (0.5 * gradient).astype(BF16)
    r1 = grads(pick_columns(plan, after_2, orders), branch)
    r1.go()
    before_grad = (dot_back(branch, w_ffn2_out) * swish_slope(before_2)).astype(BF16)
    r2 = grads(pick(ffn2_hidden), before_grad)
    r2.go()
    step(land=[r1], go=[r1], since=[before_grad])
    input_grad, gain_ffn2 = norm_backward(
        dot_back(before_grad, w_ffn2_in), gains[4], ffn2_normed, ffn2_scale
    )
    gradient = gradient + input_grad
    conv_branch = after(gradient.astype(BF16), jax.tree.leaves(ready(r1)))
    r3 = grads(pick(activated), conv_branch)
    r3.go()
    act_grad = dot_back(conv_branch, w_conv_out) * swish_slope(inner_out)
    conv_grad, gain_inner = norm_backward(act_grad, gains[3], inner_normed, inner_scale)
    step(land=[r2], go=[r2], since=[conv_branch])
    kernel_terms, ext_grad = depthwise_back(
        extended,
        edge_ids,
        conv_grad.reshape(row_count, frames_here, width),
        kernel,
        jax.tree.leaves(ready(r1, r2)),
    )
    grad_kernel = jnp.sum(kernel_terms, axis=0)
    end = half_width + frames_here
    rims = ext_grad[:, :half_width], ext_grad[:, end : end + half_width]
    to_before, to_after = (rim.astype(BF16) for rim in rims)
    up = [(i, i + 1) for i in range(wide - 1)]
    from_before = lax.ppermute(to_after, "wide", up).astype(F32)
    from_after = lax.ppermute(to_before, "wide", [(j, i) for i, j in up]).astype(F32)
    middle = jnp.zeros((row_count, frames_here - 2 * half_width, width), F32)
    glu_grad = ext_grad[:, half_width:end] + jnp.concatenate(
        [from_before, middle, from_after], axis=1
    )
    glu_grad = glu_grad.reshape(tokens, width)
    gated_grad = jnp.concatenate(
        [glu_grad * gate_sig, glu_grad * gated[:, :width] * gate_sig * (1.0 - gate_sig)],
        axis=-1,
    ).astype(BF16)
    r4 = grads(pick(conv_hidden), gated_grad)
    r4.go()
    norm_grad, gain_conv = norm_backward(
        dot_back(gated_grad, w_conv_in), gains[2], conv_normed, conv_scale
    )
    gradient = gradient + norm_grad
    attn_branch = step(
        land=[r1, r3], go=[r1, r3], chain=gradient.astype(BF16), since=[kernel_terms]
    )
    head_grads = dot_back(attn_branch, w_attn_out).astype(BF16)
    heads = Lane(heads_lane(plan, to_groups(head_grads)))
    r5 = grads(pick(mixed), attn_branch)
    r5.go()
    step(go=[heads])
    step(land=[heads], go=[heads])
    step(land=[r2, r4], go=[r2, r4], since=ready(heads)[0])
    row_grads = as_rows(finish(heads))
    query_grad, key_grad, value_grad = attend_back(
        row_queries,
        row_keys,
        row_values,
        mixed_rows,
        row_grads,
        row_totals,
        row_ids,
        row_cosine,
        row_sine,
        jax.tree.leaves(ready(r2, r4)),
    )
    heads = Lane(
        heads_lane(
            plan,
            jnp.concatenate(
                [as_blocks(query_grad), as_blocks(key_grad), as_blocks(value_grad)], axis=-1
            ),
        )
    )
    step(go=[heads])
    step(land=[heads], go=[heads])
    step(land=[r1, r2, r3, r4, r5], go=[r3, r4, r5], since=ready(heads)[0])
    returned = finish(heads)
    returned = after(returned, jax.tree.leaves(ready(r1, r2, r3, r4, r5)))
    hold(r1, returned)
    hold(r2, returned)
    packed_grad = jnp.concatenate(
        [from_groups(returned[..., part * group : (part + 1) * group]) for part in range(3)],
        axis=-1,
    )
    packed_grad = lax.optimization_barrier(packed_grad)
    r6 = grads(pick(attn_hidden), packed_grad)
    r6.go()
    norm_grad, gain_attn = norm_backward(
        dot_back(packed_grad, w_qkv), gains[1], attn_normed, attn_scale
    )
    gradient = gradient + norm_grad
    branch = (0.5 * gradient).astype(BF16)
    branch = step(land=[r6], go=[r6], chain=branch)
    r7 = grads(pick_columns(plan, after_1, orders), branch)
    r7.go()
    before_grad = (dot_back(branch, w_ffn1_out) * swish_slope(before_1)).astype(BF16)
    before_grad = lax.optimization_barrier(before_grad)

    def small_sums():
        total = jnp.concatenate([grad_gains, grad_kernel], axis=0)
        total = jnp.dot(total, tree_pick.astype(F32), precision=HIGHEST)
        return total[:, : width // 2] + send(total[:, width // 2 :], plan.flip_pairs(plan.rows))

    before_grad = lax.optimization_barrier(before_grad)
    r8 = grads(pick(ffn1_hidden), before_grad, small_sums)
    r8.go()
    before_grad = step(land=[r7], go=[r7], chain=before_grad)
    input_grad, gain_ffn1 = norm_backward(
        dot_back(before_grad, w_ffn1_in), gains[0], ffn1_normed, ffn1_scale
    )
    gradient = gradient + input_grad
    grad_gains = jnp.stack([gain_ffn1, gain_attn, gain_conv, gain_inner, gain_ffn2, gain_final])
    step(land=[r8], go=[r8])
    step(land=[r1, r2, r3, r4, r5], go=[r3, r4, r5], since=[gradient])
    step(land=[r6], go=[r6])
    finish(r1, r2, r3, r4, r5, r6, r7, r8)
    grad_ffn1_in, small_shard = r8.result
    grad_ffn1_out, grad_qkv = r7.result, r6.result
    grad_attn_out, grad_conv_in, grad_conv_out = r5.result, r4.result, r3.result
    grad_ffn2_in, grad_ffn2_out = r2.result, r1.result
    shard_gains, shard_kernel = small_shard[: grad_gains.shape[0]], small_shard[grad_gains.shape[0] :]

    return (
        layer_out,
        gradient.astype(BF16).reshape(inputs.shape),
        grad_ffn1_in,
        grad_ffn1_out,
        grad_qkv,
        grad_attn_out,
        grad_conv_in,
        shard_kernel,
        grad_conv_out,
        grad_ffn2_in,
        grad_ffn2_out,
        shard_gains,
    )


def solution(mesh):
    frames = P("rows", "wide", None)
    split_rows = P(BOTH, None)
    split_columns = P(None, BOTH)
    weights = (split_rows,) * 5 + (split_columns,) + (split_rows,) * 3 + (split_columns,)
    return jax.shard_map(
        per_device,
        mesh=mesh,
        in_specs=(frames, P("rows", None)) + weights + (frames,),
        out_specs=(frames, frames) + weights,
        check_vma=False,
    )
```

time: 3440 us -> 822 us (0.24)
  waiting for transfers between devices: 2780 us -> 221 us
  starting transfers between devices: 9.55 us -> 164 us
  blocking collectives: 142 us -> 0 us
  local copies, waits for them, and re-layouts: 182 us -> 53.6 us
  Pallas kernels: 0 us -> 74.9 us
  matrix products: 179 us -> 142 us
    reduce_scatter x8 -> x0, waiting for transfers between devices: 2070 us -> none  [the longest x1 362 us: per_device(): lax.psum_scatter(grad_ffn1_out, ('wide', 'rows'), scatter_dimension=0, ti...]
    all_gather x10 -> x3, waiting for transfers between devices: 420 us -> 3.12 us  [the longest x1 3.1 us: late_weights(): return parts + (lax.all_gather(shards[1], BOTH, axis=0, tiled=True),)]
    ppermute x4 -> x99, waiting for transfers between devices: 0.01 us -> 217 us  [the longest x95 216 us: send(): return lax.ppermute(x, BOTH, pairs)]
    unnamed x22 -> x3, waiting for transfers between devices: 196 us -> 0.71 us
    ppermute x4 -> x99, starting transfers between devices: 7.79 us -> 164 us  [the longest x95 158 us: send(): return lax.ppermute(x, BOTH, pairs)]
    all_gather x2 -> x0, blocking collectives: 142 us -> none  [the longest x1 71.3 us: per_device(): lax.all_gather(norm_gains, ('wide', 'rows'), axis=1, tiled=True)]
    while x8 -> x0, waiting for transfers between devices: 95 us -> none
    scatter-add x30 -> x0, local copies, waits for them, and re-layouts: 89.4 us -> none  [the longest x28 87.7 us: per_device(): ext_grad.at[:, tap_index:tap_index + frames_here]]
  transfers between devices with their start and end apart: 28 -> 102, of which waited for: 22 -> 34; matrix products, arithmetic and copies ran while one was open for 6% -> 36% of each run, Pallas kernels for 0% -> 6%
where the time goes in v1:
time: 822 us; the launch traced here: 811 us
  waiting for transfers between devices  221 us (27%)
  starting transfers between devices  164 us (20%)
  matrix products  142 us (17%)
  other arithmetic  123 us (15%)
  Pallas kernels  74.9 us (9%)
  local copies, waits for them, and re-layouts  53.6 us (7%)
  between operations  32.9 us (4%)
    ppermute x95, waiting for transfers between devices, send(): return lax.ppermute(x, BOTH, pairs)  216 us
    ppermute x95, starting transfers between devices, send(): return lax.ppermute(x, BOTH, pairs)  158 us
    dot_general x18, matrix products, dot(): return jnp.dot(left, right, preferred_element_type=F32)  52.5 us
    dot_general x12, matrix products, dot_back(): lax.dot_general(left, right, (((1,), (1,)), ((), ())), preferred_element_...  49.1 us
    select_n x37, other arithmetic, after(): jnp.where(flag, x, jnp.zeros((), x.dtype))  47.7 us
    dot_general x16, matrix products, dot_over_frames(): lax.dot_general(left, right, (((0,), (0,)), ((), ())), preferred_element_...  39.1 us
    pallas_call x1, Pallas kernels, attend_back(): pl.pallas_call(lambda *refs: attend_back_kernel(*refs[:13], *refs[13 + le...  23.7 us
    unnamed x278, local copies, waits for them, and re-layouts  18.5 us
  transfers between devices with their start and end apart: 102, of which 34 were waited for; matrix products, arithmetic and copies ran while one was open for 36% of the time, Pallas kernels for 6%

profile of v1, /device:TPU:0, one launch (start us, length us, event | category | flops | bytes accessed | tf_op | source)
XLA Modules:
  0.0 811.4 jit_solution(7928942250309376666)
XLA Ops:
  24.2 4.4 collective-permute-done.3
  30.7 5.0 collective-permute-start.4
  35.7 10.4 %collective-permute-done.4 = bf16[37,512]{1,0:T(8,128)(2,1)S(1)} collective-permute-done((bf16[37,512]{1,0:T(8,128)(2,1)}, bf16[37,512]{1,0:T(8,128)(2,1)S(1)}, u32[]{:S(2)}, u32[]{:S(2)}) %collective-permute-start.4) | collective-permute-done | bytes 37920 | tf_op jit(solution)/shard_map/ppermute | solution.py:61
  52.4 5.6 collective-permute-start.11
  59.1 5.7 collective-permute-done.7
  72.2 5.4 collective-permute-start.12
  77.6 19.0 %collective-permute-done.12 = bf16[2,128,1024]{2,1,0:T(8,128)(2,1)S(1)} collective-permute-done((bf16[2,128,1024]{2,1,0:T(8,128)(2,1)S(1)}, bf16[2,128,1024]{2,1,0:T(8,128)(2,1)S(1)}, u32[]{:S(2)}, u32[]{:S(2)}) %collective-permute-start.12) | collective-permute-done | bytes 524320 | tf_op jit(solution)/shard_map/ppermute | solution.py:61
  102.1 12.2 %collective-permute-done.13 = bf16[4,128,1024]{2,1,0:T(8,128)(2,1)} collective-permute-done((bf16[4,128,1024]{2,1,0:T(8,128)(2,1)}, bf16[4,128,1024]{2,1,0:T(8,128)(2,1)}, u32[]{:S(2)}, u32[]{:S(2)}) %collective-permute-start.13) | collective-permute-done | bytes 1048608 | tf_op jit(solution)/shard_map/ppermute | solution.py:61
  125.5 5.6 fusion.92
  131.2 21.0 %collective-permute-done.14.refs_1_ = bf16[8,128,1024]{2,1,0:T(8,128)(2,1)} collective-permute-done((bf16[8,128,1024]{2,1,0:T(8,128)(2,1)}, bf16[8,128,1024]{2,1,0:T(8,128)(2,1)}, u32[]{:S(2)}, u32[]{:S(2)}) %collective-permute-start.14) | collective-permute-done | bytes 2097184 | tf_op jit(solution)/shard_map/ppermute | solution.py:61
  162.5 4.4 assemble.2
  167.0 4.6 multiply_convert_fusion.1
  171.6 4.5 assemble.3
  179.7 4.7 fusion.215
  199.2 9.0 %collective-permute-start.19 = (bf16[2,256,384]{2,1,0:T(8,128)(2,1)S(1)}, bf16[2,256,384]{2,1,0:T(8,128)(2,1)S(1)}, u32[]{:S(2)}, u32[]{:S(2)}) collective-permute-start(bf16[2,256,384]{2,1,0:T(8,128)(2,1)S(1)} %get-tuple-element.163), channel_id=1, source_target_pairs={{0,16},{1,17},{2,18},{3,19},{4,20},{5,21},{6,22},{7,23},{8,24},{9,... | collective-permute-start | bytes 1179656 | tf_op jit(solution)/shard_map/ppermute | solution.py:61
  212.4 25.2 %collective-permute-done.18 = bf16[2,256,384]{2,1,0:T(8,128)(2,1)S(1)} collective-permute-done((bf16[2,256,384]{2,1,0:T(8,128)(2,1)S(1)}, bf16[2,256,384]{2,1,0:T(8,128)(2,1)S(1)}, u32[]{:S(2)}, u32[]{:S(2)}) %collective-permute-start.18) | collective-permute-done | bytes 393248 | tf_op jit(solution)/shard_map/ppermute | solution.py:61
  237.6 8.3 %collective-permute-done.19 = bf16[2,256,384]{2,1,0:T(8,128)(2,1)S(1)} collective-permute-done((bf16[2,256,384]{2,1,0:T(8,128)(2,1)S(1)}, bf16[2,256,384]{2,1,0:T(8,128)(2,1)S(1)}, u32[]{:S(2)}, u32[]{:S(2)}) %collective-permute-start.19) | collective-permute-done | bytes 393248 | tf_op jit(solution)/shard_map/ppermute | solution.py:61
  246.0 13.7 %collective-permute-done.20 = bf16[2,256,384]{2,1,0:T(8,128)(2,1)S(1)} collective-permute-done((bf16[2,256,384]{2,1,0:T(8,128)(2,1)S(1)}, bf16[2,256,384]{2,1,0:T(8,128)(2,1)S(1)}, u32[]{:S(2)}, u32[]{:S(2)}) %collective-permute-start.20) | collective-permute-done | bytes 393248 | tf_op jit(solution)/shard_map/ppermute | solution.py:61
  262.7 13.6 %attend.1 = (bf16[2,1024,128]{2,1,0:T(8,128)(2,1)}, f32[2,1024,2]{2,1,0:T(8,128)}) custom-call(bf16[2,1024,128]{2,1,0:T(8,128)(2,1)} %bitcast.350, bf16[2,1024,128]{2,1,0:T(8,128)(2,1)} %bitcast.352, bf16[2,1024,128]{2,1,0:T(8,128)(2,1)} %bitcast.354, s32[2,1024,1]{2,1,0:T(8,128)} %copy.137.refs_3_.refs_7_, s32[2,1,1024]{2,1,0:T(1,128)} %bitcast.404), custom_call_target="tpu_custom_call" | custom-call | tf_op jit(solution)/shard_map/attend/pallas_call | solution.py:412
  279.3 10.5 %collective-permute-start.22 = (bf16[2,256,128]{2,1,0:T(8,128)(2,1)S(1)}, bf16[2,256,128]{2,1,0:T(8,128)(2,1)S(1)}, u32[]{:S(2)}, u32[]{:S(2)}) collective-permute-start(bf16[2,256,128]{2,1,0:T(8,128)(2,1)S(1)} %get-tuple-element.204), channel_id=1, source_target_pairs={{0,8},{1,9},{2,10},{3,11},{4,12},{5,13},{6,14},{7,15},{8,0},{9,1},... | collective-permute-start | bytes 393224 | tf_op jit(solution)/shard_map/ppermute | solution.py:61
  297.0 5.9 collective-permute-done.23
  317.3 8.5 %collective-permute-start.41 = (bf16[256,512]{1,0:T(8,128)(2,1)}, bf16[256,512]{1,0:T(8,128)(2,1)}, u32[]{:S(2)}, u32[]{:S(2)}) collective-permute-start(bf16[256,512]{1,0:T(8,128)(2,1)} %get-tuple-element.188), channel_id=1, source_target_pairs={{0,4},{1,5},{2,6},{3,7},{4,0},{5,1},{6,2},{7,3},{8,12},{9,13},{10,... | collective-permute-start | bytes 786440 | tf_op jit(solution)/shard_map/ppermute | solution.py:61
  326.1 4.7 depthwise.1
  335.4 8.0 multiply_convert_fusion
  351.6 6.2 fusion.237
  361.6 8.9 %fusion.4.refs_0_ = bf16[256,4096]{1,0:T(8,128)(2,1)} fusion(bf16[256,1024]{1,0:T(8,128)(2,1)} %get-tuple-element.166, bf16[4096,1024]{1,0:T(8,128)(2,1)} %all-gather.8.cloned.1.call-done, f32[256,4096]{1,0:T(8,128)} %get-tuple-element.250), kind=kOutput, calls=%fused_computation.8 | convolution fusion | flops 2156920832 | bytes 15204352 | tf_op jit(solution)/shard_map/dot_general | solution.py:320
  370.7 5.5 multiply_reduce_fusion
  414.1 8.4 %depthwise_back.1 = (f32[2,31,1024]{2,1,0:T(8,128)S(1)}, f32[2,160,1024]{2,1,0:T(8,128)S(1)}) custom-call(bf16[2,160,1024]{2,1,0:T(8,128)(2,1)S(1)} %maximum_maximum_fusion.refs_0_, f32[2,160,1]{2,1,0:T(8,128)S(1)} %copy-done.6, f32[2,128,1024]{2,1,0:T(8,128)S(1)} %bitcast.342, f32[31,1024]{1,0:T(8,128)S(1)} %slice.879.refs_2_.refs_3_, ...), custom_call_target="tpu_custom_call" | custom-call | tf_op jit(solution)/shard_map/depthwise_back/pallas_call | solution.py:546
  439.3 5.3 multiply_reduce_fusion.2
  453.8 4.0 fusion.88
  459.8 4.8 convolution_convert_fusion.2
  467.3 3.7 collective-permute-start.39
  485.1 23.7 %attend_back.1 = (bf16[2,1024,128]{2,1,0:T(8,128)(2,1)}, bf16[2,1024,128]{2,1,0:T(8,128)(2,1)}, bf16[2,1024,128]{2,1,0:T(8,128)(2,1)}) custom-call(bf16[2,1024,128]{2,1,0:T(8,128)(2,1)} %bitcast.351, bf16[2,1024,128]{2,1,0:T(8,128)(2,1)} %bitcast.353, bf16[2,1024,128]{2,1,0:T(8,128)(2,1)} %bitcast.355, bf16[2,1024,128]{2,1,0:T(8,128)(2,1)} %get-tuple-element.41.refs_3_, ...), custom_call_target="tpu_custom_call" | custom-call | tf_op jit(solution)/shard_map/attend_back/pallas_call | solution.py:441
  534.1 8.6 %collective-permute-done.44 = bf16[512,1024]{1,0:T(8,128)(2,1)} collective-permute-done((bf16[512,1024]{1,0:T(8,128)(2,1)}, bf16[512,1024]{1,0:T(8,128)(2,1)}, u32[]{:S(2)}, u32[]{:S(2)}) %collective-permute-start.44) | collective-permute-done | bytes 1048608 | tf_op jit(solution)/shard_map/ppermute | solution.py:61
  570.7 7.7 collective-permute-start.96
  583.5 6.3 multiply_reduce_fusion.3
  599.5 7.6 fusion.5
  615.2 6.7 multiply_reduce_fusion.4
  629.4 4.0 convolution_convert_fusion.8
  643.2 13.8 %collective-permute-done.94 = bf16[32,4096]{1,0:T(8,128)(2,1)S(1)} collective-permute-done((bf16[32,4096]{1,0:T(8,128)(2,1)}, bf16[32,4096]{1,0:T(8,128)(2,1)S(1)}, u32[]{:S(2)}, u32[]{:S(2)}) %collective-permute-start.94) | collective-permute-done | bytes 262176 | tf_op jit(solution)/shard_map/ppermute | solution.py:61
  666.0 5.5 collective-permute-start.80
  677.7 6.6 collective-permute-done.81
  685.8 7.8 collective-permute-done.75
  711.1 13.1 %collective-permute-done.70 = bf16[128,3072]{1,0:T(8,128)(2,1)} collective-permute-done((bf16[128,3072]{1,0:T(8,128)(2,1)}, bf16[128,3072]{1,0:T(8,128)(2,1)}, u32[]{:S(2)}, u32[]{:S(2)}) %collective-permute-start.70) | collective-permute-done | bytes 786464 | tf_op jit(solution)/shard_map/ppermute | solution.py:61
  732.4 4.6 collective-permute-done.59.refs_0_
  742.8 9.0 %collective-permute-done.65 = bf16[512,1024]{1,0:T(8,128)(2,1)S(1)} collective-permute-done((bf16[512,1024]{1,0:T(8,128)(2,1)S(1)}, bf16[512,1024]{1,0:T(8,128)(2,1)S(1)}, u32[]{:S(2)}, u32[]{:S(2)}) %collective-permute-start.65) | collective-permute-done | bytes 1048608 | tf_op jit(solution)/shard_map/ppermute | solution.py:61
  770.1 5.3 collective-permute-done.67
  775.4 16.8 %collective-permute-start.87 = (f32[37,32]{1,0:T(8,128)S(1)}, f32[37,32]{1,0:T(8,128)S(1)}, u32[]{:S(2)}, u32[]{:S(2)}) collective-permute-start(f32[37,32]{1,0:T(8,128)S(1)} %get-tuple-element.227), channel_id=1, source_target_pairs={{0,16},{1,17},{2,18},{3,19},{4,20},{5,21},{6,22},{7,23},{8,24},{9,... | collective-permute-start | bytes 14216 | tf_op jit(solution)/shard_map/ppermute | solution.py:61
  (747 shorter events, 364.3 us)
Async XLA Ops:
  7.2 172.6 %all-gather.4.cloned.1.call-start = ((), (), s32[]{:S(2)}) async-start(), calls=%async_computation | async-start | bytes 6488064 | tf_op jit(solution)/shard_map/all_gather | solution.py:676
  7.9 298.2 %all-gather.6.cloned.1.call-start = ((), (), s32[]{:S(2)}) async-start(), calls=%async_computation.1 | async-start | bytes 17301504 | tf_op jit(solution)/shard_map/all_gather | solution.py:681
  67.2 33.6 %collective-permute-start.8 = (bf16[8,128,1024]{2,1,0:T(8,128)(2,1)S(1)}, bf16[8,128,1024]{2,1,0:T(8,128)(2,1)}, u32[]{:S(2)}, u32[]{:S(2)}) collective-permute-start(bf16[8,128,1024]{2,1,0:T(8,128)(2,1)S(1)} %pad_maximum_fusion.3.refs_0_), channel_id=1, source_target_pairs={{0,2},{1,3},{2,0},{3,1},{4,5},{5,4},{6,7},{7,6},{8,10},{9,11},{10,... | collective-permute-start | bytes 6291464 | tf_op jit(solution)/shard_map/ppermute | solution.py:61
  72.2 24.5 %collective-permute-start.12 = (bf16[2,128,1024]{2,1,0:T(8,128)(2,1)S(1)}, bf16[2,128,1024]{2,1,0:T(8,128)(2,1)S(1)}, u32[]{:S(2)}, u32[]{:S(2)}) collective-permute-start(bf16[2,128,1024]{2,1,0:T(8,128)(2,1)S(1)} %get-tuple-element.210), channel_id=1, source_target_pairs={{0,8},{1,9},{2,10},{3,11},{4,12},{5,13},{6,14},{7,15},{8,0},{9,1},... | collective-permute-start | bytes 1572872 | tf_op jit(solution)/shard_map/ppermute | solution.py:61
  120.3 231.3 %all-gather.8.cloned.1.call-start = ((), (), s32[]{:S(2)}) async-start(), calls=%async_computation.2 | async-start | bytes 8650752 | tf_op jit(solution)/shard_map/all_gather | solution.py:684
  122.1 30.2 %collective-permute-start.14 = (bf16[8,128,1024]{2,1,0:T(8,128)(2,1)}, bf16[8,128,1024]{2,1,0:T(8,128)(2,1)}, u32[]{:S(2)}, u32[]{:S(2)}) collective-permute-start(bf16[8,128,1024]{2,1,0:T(8,128)(2,1)} %get-tuple-element.144.refs_0_), channel_id=1, source_target_pairs={{0,2},{1,3},{2,0},{3,1},{4,5},{5,4},{6,7},{7,6},{8,10},{9,11},{10,... | collective-permute-start | bytes 6291464 | tf_op jit(solution)/shard_map/ppermute | solution.py:61
  123.8 38.4 %collective-permute-start.9 = (bf16[8,128,1024]{2,1,0:T(8,128)(2,1)S(1)}, bf16[8,128,1024]{2,1,0:T(8,128)(2,1)}, u32[]{:S(2)}, u32[]{:S(2)}) collective-permute-start(bf16[8,128,1024]{2,1,0:T(8,128)(2,1)S(1)} %copy-done.1), channel_id=1, source_target_pairs={{0,4},{1,5},{2,6},{3,7},{4,0},{5,1},{6,2},{7,3},{8,12},{9,13},{10,... | collective-permute-start | bytes 6291464 | tf_op jit(solution)/shard_map/ppermute | solution.py:61
  123.9 38.3 %collective-permute-start.10 = (bf16[8,128,1024]{2,1,0:T(8,128)(2,1)}, bf16[8,128,1024]{2,1,0:T(8,128)(2,1)}, u32[]{:S(2)}, u32[]{:S(2)}) collective-permute-start(bf16[8,128,1024]{2,1,0:T(8,128)(2,1)} %collective-permute-done.8.refs_1_), channel_id=1, source_target_pairs={{0,4},{1,5},{2,6},{3,7},{4,0},{5,1},{6,2},{7,3},{8,12},{9,13},{10,... | collective-permute-start | bytes 6291464 | tf_op jit(solution)/shard_map/ppermute | solution.py:61
  131.1 40.5 %collective-permute-start.15 = (bf16[8,128,1024]{2,1,0:T(8,128)(2,1)}, bf16[8,128,1024]{2,1,0:T(8,128)(2,1)}, u32[]{:S(2)}, u32[]{:S(2)}) collective-permute-start(bf16[8,128,1024]{2,1,0:T(8,128)(2,1)} %get-tuple-element.145.refs_0_), channel_id=1, source_target_pairs={{0,4},{1,5},{2,6},{3,7},{4,0},{5,1},{6,2},{7,3},{8,12},{9,13},{10,... | collective-permute-start | bytes 6291464 | tf_op jit(solution)/shard_map/ppermute | solution.py:61
  198.2 39.5 %collective-permute-start.18 = (bf16[2,256,384]{2,1,0:T(8,128)(2,1)S(1)}, bf16[2,256,384]{2,1,0:T(8,128)(2,1)S(1)}, u32[]{:S(2)}, u32[]{:S(2)}) collective-permute-start(bf16[2,256,384]{2,1,0:T(8,128)(2,1)S(1)} %get-tuple-element.161), channel_id=1, source_target_pairs={{0,8},{1,9},{2,10},{3,11},{4,12},{5,13},{6,14},{7,15},{8,0},{9,1},... | collective-permute-start | bytes 1179656 | tf_op jit(solution)/shard_map/ppermute | solution.py:61
  199.2 46.7 %collective-permute-start.19 = (bf16[2,256,384]{2,1,0:T(8,128)(2,1)S(1)}, bf16[2,256,384]{2,1,0:T(8,128)(2,1)S(1)}, u32[]{:S(2)}, u32[]{:S(2)}) collective-permute-start(bf16[2,256,384]{2,1,0:T(8,128)(2,1)S(1)} %get-tuple-element.163), channel_id=1, source_target_pairs={{0,16},{1,17},{2,18},{3,19},{4,20},{5,21},{6,22},{7,23},{8,24},{9,... | collective-permute-start | bytes 1179656 | tf_op jit(solution)/shard_map/ppermute | solution.py:61
  208.3 51.4 %collective-permute-start.20 = (bf16[2,256,384]{2,1,0:T(8,128)(2,1)S(1)}, bf16[2,256,384]{2,1,0:T(8,128)(2,1)S(1)}, u32[]{:S(2)}, u32[]{:S(2)}) collective-permute-start(bf16[2,256,384]{2,1,0:T(8,128)(2,1)S(1)} %get-tuple-element.162), channel_id=1, source_target_pairs={{0,24},{1,25},{2,26},{3,27},{4,28},{5,29},{6,30},{7,31},{8,16},{9,... | collective-permute-start | bytes 1179656 | tf_op jit(solution)/shard_map/ppermute | solution.py:61
  212.4 79.9 %collective-permute-start.53 = (bf16[256,2048]{1,0:T(8,128)(2,1)}, bf16[256,2048]{1,0:T(8,128)(2,1)}, u32[]{:S(2)}, u32[]{:S(2)}) collective-permute-start(bf16[256,2048]{1,0:T(8,128)(2,1)} %get-tuple-element.61), channel_id=1, source_target_pairs={{0,4},{1,5},{2,6},{3,7},{4,0},{5,1},{6,2},{7,3},{8,12},{9,13},{10,... | collective-permute-start | bytes 3145736 | tf_op jit(solution)/shard_map/ppermute | solution.py:61
  317.3 150.0 %collective-permute-start.41 = (bf16[256,512]{1,0:T(8,128)(2,1)}, bf16[256,512]{1,0:T(8,128)(2,1)}, u32[]{:S(2)}, u32[]{:S(2)}) collective-permute-start(bf16[256,512]{1,0:T(8,128)(2,1)} %get-tuple-element.188), channel_id=1, source_target_pairs={{0,4},{1,5},{2,6},{3,7},{4,0},{5,1},{6,2},{7,3},{8,12},{9,13},{10,... | collective-permute-start | bytes 786440 | tf_op jit(solution)/shard_map/ppermute | solution.py:61
  360.0 21.7 %collective-permute-start.28 = (bf16[256,1024]{1,0:T(8,128)(2,1)}, bf16[256,1024]{1,0:T(8,128)(2,1)}, u32[]{:S(2)}, u32[]{:S(2)}) collective-permute-start(bf16[256,1024]{1,0:T(8,128)(2,1)} %get-tuple-element.166), channel_id=1, source_target_pairs={{0,4},{1,5},{2,6},{3,7},{4,0},{5,1},{6,2},{7,3},{8,12},{9,13},{10,... | collective-permute-start | bytes 1572872 | tf_op jit(solution)/shard_map/ppermute | solution.py:61
  370.5 37.3 %collective-permute-start.30 = (bf16[256,4096]{1,0:T(8,128)(2,1)}, bf16[256,4096]{1,0:T(8,128)(2,1)}, u32[]{:S(2)}, u32[]{:S(2)}) collective-permute-start(bf16[256,4096]{1,0:T(8,128)(2,1)} %fusion.4.refs_0_), channel_id=1, source_target_pairs={{0,4},{1,5},{2,6},{3,7},{4,0},{5,1},{6,2},{7,3},{8,12},{9,13},{10,... | collective-permute-start | bytes 6291464 | tf_op jit(solution)/shard_map/ppermute | solution.py:61
  381.7 47.9 %collective-permute-start.34 = (bf16[256,512]{1,0:T(8,128)(2,1)}, bf16[256,512]{1,0:T(8,128)(2,1)}, u32[]{:S(2)}, u32[]{:S(2)}) collective-permute-start(bf16[256,512]{1,0:T(8,128)(2,1)} %get-tuple-element.196), channel_id=1, source_target_pairs={{0,4},{1,5},{2,6},{3,7},{4,0},{5,1},{6,2},{7,3},{8,12},{9,13},{10,... | collective-permute-start | bytes 786440 | tf_op jit(solution)/shard_map/ppermute | solution.py:61
  395.2 31.4 %collective-permute-start.35 = (bf16[256,1024]{1,0:T(8,128)(2,1)}, bf16[256,1024]{1,0:T(8,128)(2,1)}, u32[]{:S(2)}, u32[]{:S(2)}) collective-permute-start(bf16[256,1024]{1,0:T(8,128)(2,1)} %get-tuple-element.106.refs_0_), channel_id=1, source_target_pairs={{0,4},{1,5},{2,6},{3,7},{4,0},{5,1},{6,2},{7,3},{8,12},{9,13},{10,... | collective-permute-start | bytes 1572872 | tf_op jit(solution)/shard_map/ppermute | solution.py:61
  396.1 48.5 %collective-permute-start.33 = (bf16[1024,1024]{1,0:T(8,128)(2,1)}, bf16[1024,1024]{1,0:T(8,128)(2,1)}, u32[]{:S(2)}, u32[]{:S(2)}) collective-permute-start(bf16[1024,1024]{1,0:T(8,128)(2,1)} %convolution_convert_fusion.11.refs_0_.refs_4_), channel_id=1, source_target_pairs={{0,2},{1,3},{2,0},{3,1},{4,5},{5,4},{6,7},{7,6},{8,10},{9,11},{10,... | collective-permute-start | bytes 6291464 | tf_op jit(solution)/shard_map/ppermute | solution.py:61
  413.6 67.2 %collective-permute-start.40 = (bf16[256,4096]{1,0:T(8,128)(2,1)S(1)}, bf16[256,4096]{1,0:T(8,128)(2,1)}, u32[]{:S(2)}, u32[]{:S(2)}) collective-permute-start(bf16[256,4096]{1,0:T(8,128)(2,1)S(1)} %convolution_convert_fusion.3.refs_5_), channel_id=1, source_target_pairs={{0,2},{1,3},{2,0},{3,1},{4,5},{5,4},{6,7},{7,6},{8,10},{9,11},{10,... | collective-permute-start | bytes 6291464 | tf_op jit(solution)/shard_map/ppermute | solution.py:61
  436.0 36.0 %collective-permute-start.42 = (bf16[256,2048]{1,0:T(8,128)(2,1)}, bf16[256,2048]{1,0:T(8,128)(2,1)}, u32[]{:S(2)}, u32[]{:S(2)}) collective-permute-start(bf16[256,2048]{1,0:T(8,128)(2,1)} %pad_maximum_fusion.15), channel_id=1, source_target_pairs={{0,4},{1,5},{2,6},{3,7},{4,0},{5,1},{6,2},{7,3},{8,12},{9,13},{10,... | collective-permute-start | bytes 3145736 | tf_op jit(solution)/shard_map/ppermute | solution.py:61
  518.6 24.1 %collective-permute-start.44 = (bf16[512,1024]{1,0:T(8,128)(2,1)}, bf16[512,1024]{1,0:T(8,128)(2,1)}, u32[]{:S(2)}, u32[]{:S(2)}) collective-permute-start(bf16[512,1024]{1,0:T(8,128)(2,1)} %get-tuple-element.117.refs_0_), channel_id=1, source_target_pairs={{0,1},{1,0},{2,3},{3,2},{4,6},{5,7},{6,4},{7,5},{8,9},{9,8},{10,11... | collective-permute-start | bytes 3145736 | tf_op jit(solution)/shard_map/ppermute | solution.py:61
  522.6 26.7 %collective-permute-start.47 = (bf16[256,2048]{1,0:T(8,128)(2,1)}, bf16[256,2048]{1,0:T(8,128)(2,1)}, u32[]{:S(2)}, u32[]{:S(2)}) collective-permute-start(bf16[256,2048]{1,0:T(8,128)(2,1)} %convolution_convert_fusion.7.refs_14_), channel_id=1, source_target_pairs={{0,2},{1,3},{2,0},{3,1},{4,5},{5,4},{6,7},{7,6},{8,10},{9,11},{10,... | collective-permute-start | bytes 3145736 | tf_op jit(solution)/shard_map/ppermute | solution.py:61
  526.6 29.6 %collective-permute-start.45 = (bf16[128,4096]{1,0:T(8,128)(2,1)S(1)}, bf16[128,4096]{1,0:T(8,128)(2,1)S(1)}, u32[]{:S(2)}, u32[]{:S(2)}) collective-permute-start(bf16[128,4096]{1,0:T(8,128)(2,1)S(1)} %copy-done.58), channel_id=1, source_target_pairs={{0,1},{1,0},{2,3},{3,2},{4,6},{5,7},{6,4},{7,5},{8,9},{9,8},{10,11... | collective-permute-start | bytes 3145736 | tf_op jit(solution)/shard_map/ppermute | solution.py:61
  528.8 32.2 %collective-permute-start.50 = (bf16[2,256,384]{2,1,0:T(8,128)(2,1)}, bf16[2,256,384]{2,1,0:T(8,128)(2,1)}, u32[]{:S(2)}, u32[]{:S(2)}) collective-permute-start(bf16[2,256,384]{2,1,0:T(8,128)(2,1)} %get-tuple-element.152.refs_0_), channel_id=1, source_target_pairs={{0,8},{1,9},{2,10},{3,11},{4,12},{5,13},{6,14},{7,15},{8,0},{9,1},... | collective-permute-start | bytes 1179656 | tf_op jit(solution)/shard_map/ppermute | solution.py:61
  532.9 30.2 %collective-permute-start.51 = (bf16[2,256,384]{2,1,0:T(8,128)(2,1)}, bf16[2,256,384]{2,1,0:T(8,128)(2,1)}, u32[]{:S(2)}, u32[]{:S(2)}) collective-permute-start(bf16[2,256,384]{2,1,0:T(8,128)(2,1)} %get-tuple-element.153.refs_1_), channel_id=1, source_target_pairs={{0,16},{1,17},{2,18},{3,19},{4,20},{5,21},{6,22},{7,23},{8,24},{9,... | collective-permute-start | bytes 1179656 | tf_op jit(solution)/shard_map/ppermute | solution.py:61
  542.7 20.3 %collective-permute-start.52 = (bf16[2,256,384]{2,1,0:T(8,128)(2,1)S(1)}, bf16[2,256,384]{2,1,0:T(8,128)(2,1)}, u32[]{:S(2)}, u32[]{:S(2)}) collective-permute-start(bf16[2,256,384]{2,1,0:T(8,128)(2,1)S(1)} %copy-done.87), channel_id=1, source_target_pairs={{0,24},{1,25},{2,26},{3,27},{4,28},{5,29},{6,30},{7,31},{8,16},{9,... | collective-permute-start | bytes 1179656 | tf_op jit(solution)/shard_map/ppermute | solution.py:61
  549.3 75.3 %collective-permute-start.89 = (bf16[128,1024]{1,0:T(8,128)(2,1)}, bf16[128,1024]{1,0:T(8,128)(2,1)}, u32[]{:S(2)}, u32[]{:S(2)}) collective-permute-start(bf16[128,1024]{1,0:T(8,128)(2,1)} %get-tuple-element.169.refs_6_), channel_id=1, source_target_pairs={{0,1},{1,0},{2,3},{3,2},{4,6},{5,7},{6,4},{7,5},{8,9},{9,8},{10,11... | collective-permute-start | bytes 786440 | tf_op jit(solution)/shard_map/ppermute | solution.py:61
  556.2 70.9 %collective-permute-start.79 = (bf16[128,2048]{1,0:T(8,128)(2,1)}, bf16[128,2048]{1,0:T(8,128)(2,1)}, u32[]{:S(2)}, u32[]{:S(2)}) collective-permute-start(bf16[128,2048]{1,0:T(8,128)(2,1)} %get-tuple-element.131.refs_7_), channel_id=1, source_target_pairs={{0,1},{1,0},{2,3},{3,2},{4,6},{5,7},{6,4},{7,5},{8,9},{9,8},{10,11... | collective-permute-start | bytes 1572872 | tf_op jit(solution)/shard_map/ppermute | solution.py:61
  561.0 74.3 %collective-permute-start.74 = (bf16[256,1024]{1,0:T(8,128)(2,1)}, bf16[256,1024]{1,0:T(8,128)(2,1)}, u32[]{:S(2)}, u32[]{:S(2)}) collective-permute-start(bf16[256,1024]{1,0:T(8,128)(2,1)} %convolution_convert_fusion.13.refs_8_), channel_id=1, source_target_pairs={{0,2},{1,3},{2,0},{3,1},{4,5},{5,4},{6,7},{7,6},{8,10},{9,11},{10,... | collective-permute-start | bytes 1572872 | tf_op jit(solution)/shard_map/ppermute | solution.py:61
  570.7 67.6 %collective-permute-start.96 = (bf16[128,1024]{1,0:T(8,128)(2,1)}, bf16[128,1024]{1,0:T(8,128)(2,1)}, u32[]{:S(2)}, u32[]{:S(2)}) collective-permute-start(bf16[128,1024]{1,0:T(8,128)(2,1)} %broadcast_select_fusion.19), channel_id=1, source_target_pairs={{0,8},{1,9},{2,10},{3,11},{4,12},{5,13},{6,14},{7,15},{8,0},{9,1},... | collective-permute-start | bytes 786440 | tf_op jit(solution)/shard_map/ppermute | solution.py:61
  609.3 30.6 %collective-permute-start.97 = (bf16[128,1024]{1,0:T(8,128)(2,1)}, bf16[128,1024]{1,0:T(8,128)(2,1)}, u32[]{:S(2)}, u32[]{:S(2)}) collective-permute-start(bf16[128,1024]{1,0:T(8,128)(2,1)} %broadcast_select_fusion.18), channel_id=1, source_target_pairs={{0,16},{1,17},{2,18},{3,19},{4,20},{5,21},{6,22},{7,23},{8,24},{9,... | collective-permute-start | bytes 786440 | tf_op jit(solution)/shard_map/ppermute | solution.py:61
  635.3 21.7 %collective-permute-start.94 = (bf16[32,4096]{1,0:T(8,128)(2,1)}, bf16[32,4096]{1,0:T(8,128)(2,1)S(1)}, u32[]{:S(2)}, u32[]{:S(2)}) collective-permute-start(bf16[32,4096]{1,0:T(8,128)(2,1)} %broadcast_select_fusion.21), channel_id=1, source_target_pairs={{0,16},{1,17},{2,18},{3,19},{4,20},{5,21},{6,22},{7,23},{8,24},{9,... | collective-permute-start | bytes 786440 | tf_op jit(solution)/shard_map/ppermute | solution.py:61
  639.8 55.7 %collective-permute-start.58 = (bf16[256,4096]{1,0:T(8,128)(2,1)}, bf16[256,4096]{1,0:T(8,128)(2,1)S(1)}, u32[]{:S(2)}, u32[]{:S(2)}) collective-permute-start(bf16[256,4096]{1,0:T(8,128)(2,1)} %fusion.5), channel_id=1, source_target_pairs={{0,4},{1,5},{2,6},{3,7},{4,0},{5,1},{6,2},{7,3},{8,12},{9,13},{10,... | collective-permute-start | bytes 6291464 | tf_op jit(solution)/shard_map/ppermute | solution.py:61
  639.8 61.4 %collective-permute-start.69 = (bf16[256,3072]{1,0:T(8,128)(2,1)S(1)}, bf16[256,3072]{1,0:T(8,128)(2,1)S(1)}, u32[]{:S(2)}, u32[]{:S(2)}) collective-permute-start(bf16[256,3072]{1,0:T(8,128)(2,1)S(1)} %copy-done.41), channel_id=1, source_target_pairs={{0,2},{1,3},{2,0},{3,1},{4,5},{5,4},{6,7},{7,6},{8,10},{9,11},{10,... | collective-permute-start | bytes 4718600 | tf_op jit(solution)/shard_map/ppermute | solution.py:61
  643.2 20.1 %collective-permute-start.90 = (bf16[32,1024]{1,0:T(8,128)(2,1)}, bf16[32,1024]{1,0:T(8,128)(2,1)S(1)}, u32[]{:S(2)}, u32[]{:S(2)}) collective-permute-start(bf16[32,1024]{1,0:T(8,128)(2,1)} %get-tuple-element.177), channel_id=1, source_target_pairs={{0,8},{1,9},{2,10},{3,11},{4,12},{5,13},{6,14},{7,15},{8,0},{9,1},... | collective-permute-start | bytes 196616 | tf_op jit(solution)/shard_map/ppermute | solution.py:61
  677.1 50.2 %collective-permute-start.64 = (bf16[1024,1024]{1,0:T(8,128)(2,1)}, bf16[1024,1024]{1,0:T(8,128)(2,1)}, u32[]{:S(2)}, u32[]{:S(2)}) collective-permute-start(bf16[1024,1024]{1,0:T(8,128)(2,1)} %convolution_convert_fusion.9.refs_0_), channel_id=1, source_target_pairs={{0,2},{1,3},{2,0},{3,1},{4,5},{5,4},{6,7},{7,6},{8,10},{9,11},{10,... | collective-permute-start | bytes 6291464 | tf_op jit(solution)/shard_map/ppermute | solution.py:61
  701.3 35.8 %collective-permute-start.59 = (bf16[256,4096]{1,0:T(8,128)(2,1)}, bf16[256,4096]{1,0:T(8,128)(2,1)S(1)}, u32[]{:S(2)}, u32[]{:S(2)}) collective-permute-start(bf16[256,4096]{1,0:T(8,128)(2,1)} %convolution_convert_fusion.refs_0_), channel_id=1, source_target_pairs={{0,2},{1,3},{2,0},{3,1},{4,5},{5,4},{6,7},{7,6},{8,10},{9,11},{10,... | collective-permute-start | bytes 6291464 | tf_op jit(solution)/shard_map/ppermute | solution.py:61
  703.4 20.8 %collective-permute-start.70 = (bf16[128,3072]{1,0:T(8,128)(2,1)}, bf16[128,3072]{1,0:T(8,128)(2,1)}, u32[]{:S(2)}, u32[]{:S(2)}) collective-permute-start(bf16[128,3072]{1,0:T(8,128)(2,1)} %get-tuple-element.119), channel_id=1, source_target_pairs={{0,1},{1,0},{2,3},{3,2},{4,6},{5,7},{6,4},{7,5},{8,9},{9,8},{10,11... | collective-permute-start | bytes 2359304 | tf_op jit(solution)/shard_map/ppermute | solution.py:61
  705.9 52.6 %collective-permute-start.84 = (f32[37,256]{1,0:T(8,128)S(1)}, f32[37,256]{1,0:T(8,128)}, u32[]{:S(2)}, u32[]{:S(2)}) collective-permute-start(f32[37,256]{1,0:T(8,128)S(1)} %slice_select_fusion), channel_id=1, source_target_pairs={{0,2},{1,3},{2,0},{3,1},{4,5},{5,4},{6,7},{7,6},{8,10},{9,11},{10,... | collective-permute-start | bytes 113672 | tf_op jit(solution)/shard_map/ppermute | solution.py:61
  739.6 23.5 %collective-permute-start.60 = (bf16[128,4096]{1,0:T(8,128)(2,1)}, bf16[128,4096]{1,0:T(8,128)(2,1)S(1)}, u32[]{:S(2)}, u32[]{:S(2)}) collective-permute-start(bf16[128,4096]{1,0:T(8,128)(2,1)} %get-tuple-element.113), channel_id=1, source_target_pairs={{0,1},{1,0},{2,3},{3,2},{4,6},{5,7},{6,4},{7,5},{8,9},{9,8},{10,11... | collective-permute-start | bytes 3145736 | tf_op jit(solution)/shard_map/ppermute | solution.py:61
  753.6 21.7 %collective-permute-start.67 = (bf16[128,1024]{1,0:T(8,128)(2,1)}, bf16[128,1024]{1,0:T(8,128)(2,1)}, u32[]{:S(2)}, u32[]{:S(2)}) collective-permute-start(bf16[128,1024]{1,0:T(8,128)(2,1)} %get-tuple-element.134), channel_id=1, source_target_pairs={{0,16},{1,17},{2,18},{3,19},{4,20},{5,21},{6,22},{7,23},{8,24},{9,... | collective-permute-start | bytes 786440 | tf_op jit(solution)/shard_map/ppermute | solution.py:61
  754.7 20.7 %collective-permute-start.68 = (bf16[128,1024]{1,0:T(8,128)(2,1)}, bf16[128,1024]{1,0:T(8,128)(2,1)}, u32[]{:S(2)}, u32[]{:S(2)}) collective-permute-start(bf16[128,1024]{1,0:T(8,128)(2,1)} %get-tuple-element.133), channel_id=1, source_target_pairs={{0,24},{1,25},{2,26},{3,27},{4,28},{5,29},{6,30},{7,31},{8,16},{9,... | collective-permute-start | bytes 786440 | tf_op jit(solution)/shard_map/ppermute | solution.py:61
  764.3 27.9 %collective-permute-start.61 = (bf16[32,4096]{1,0:T(8,128)(2,1)}, bf16[32,4096]{1,0:T(8,128)(2,1)S(1)}, u32[]{:S(2)}, u32[]{:S(2)}) collective-permute-start(bf16[32,4096]{1,0:T(8,128)(2,1)} %get-tuple-element.135), channel_id=1, source_target_pairs={{0,8},{1,9},{2,10},{3,11},{4,12},{5,13},{6,14},{7,15},{8,0},{9,1},... | collective-permute-start | bytes 786440 | tf_op jit(solution)/shard_map/ppermute | solution.py:61
  766.1 31.8 %collective-permute-start.62 = (bf16[32,4096]{1,0:T(8,128)(2,1)}, bf16[32,4096]{1,0:T(8,128)(2,1)S(1)}, u32[]{:S(2)}, u32[]{:S(2)}) collective-permute-start(bf16[32,4096]{1,0:T(8,128)(2,1)} %get-tuple-element.137), channel_id=1, source_target_pairs={{0,16},{1,17},{2,18},{3,19},{4,20},{5,21},{6,22},{7,23},{8,24},{9,... | collective-permute-start | bytes 786440 | tf_op jit(solution)/shard_map/ppermute | solution.py:61
  767.3 30.6 %collective-permute-start.63 = (bf16[32,4096]{1,0:T(8,128)(2,1)}, bf16[32,4096]{1,0:T(8,128)(2,1)S(1)}, u32[]{:S(2)}, u32[]{:S(2)}) collective-permute-start(bf16[32,4096]{1,0:T(8,128)(2,1)} %get-tuple-element.136), channel_id=1, source_target_pairs={{0,24},{1,25},{2,26},{3,27},{4,28},{5,29},{6,30},{7,31},{8,16},{9,... | collective-permute-start | bytes 786440 | tf_op jit(solution)/shard_map/ppermute | solution.py:61
  775.4 25.1 %collective-permute-start.86 = (f32[37,32]{1,0:T(8,128)S(1)}, f32[37,32]{1,0:T(8,128)S(1)}, u32[]{:S(2)}, u32[]{:S(2)}) collective-permute-start(f32[37,32]{1,0:T(8,128)S(1)} %get-tuple-element.225), channel_id=1, source_target_pairs={{0,8},{1,9},{2,10},{3,11},{4,12},{5,13},{6,14},{7,15},{8,0},{9,1},... | collective-permute-start | bytes 14216 | tf_op jit(solution)/shard_map/ppermute | solution.py:61
  775.4 25.7 %collective-permute-start.87 = (f32[37,32]{1,0:T(8,128)S(1)}, f32[37,32]{1,0:T(8,128)S(1)}, u32[]{:S(2)}, u32[]{:S(2)}) collective-permute-start(f32[37,32]{1,0:T(8,128)S(1)} %get-tuple-element.227), channel_id=1, source_target_pairs={{0,16},{1,17},{2,18},{3,19},{4,20},{5,21},{6,22},{7,23},{8,24},{9,... | collective-permute-start | bytes 14216 | tf_op jit(solution)/shard_map/ppermute | solution.py:61
  (192 other events, 2076.9 us)
Sparse Core Ops, SparseCore 0:
  10.9 86.1 all-gather.3
  120.4 148.5 all-gather.5
  272.4 79.1 all-gather.7

commit v2 on v1

--- a/solution.py
+++ b/solution.py
@@ -27,17 +27,24 @@
         self.stages = len(row_bits)
         self.far_bits = [1 << b for b in range((wide // 2).bit_length() - 1)]
         self.blocks = self.total // 2
+        far = [0]
+        for bit in reversed(self.far_bits):
+            far += [k | bit for k in far]
         self.table = [
             np.array(
                 [
-                    far ^ sum(f for t, f in enumerate(flips) if p >> t & 1)
+                    (k * 2 * rows) ^ sum(f for t, f in enumerate(flips) if p >> t & 1)
                     for p in range(1 << self.stages)
-                    for far in [0, *self.far]
+                    for k in far
                 ],
                 np.int32,
             )
             for flips in self.flips
         ]
+
+    def halvings(self):
+        near = [self.stage_pairs(t) for t in reversed(range(self.stages))]
+        return near + [self.flip_pairs(bit * 2 * self.rows) for bit in self.far_bits]
 
     def core_of(self, index):
         return (index // self.rows) % 2
@@ -124,8 +131,9 @@
 
 
 def hold(lane, *tokens):
-    lane.operand = after(lane.operand, list(tokens))
-    lane.go()
+    if lane.operand is not None:
+        lane.operand = after(lane.operand, list(tokens))
+        lane.go()
 
 
 def waited(*lanes):
@@ -136,10 +144,10 @@
     return [lane.operand for lane in lanes if lane.operand is not None]
 
 
-def finish(*lanes):
+def finish(*lanes, since=()):
     while any(lane.operand is not None for lane in lanes):
         for lane in lanes:
-            step(land=[lane], go=[lane])
+            step(land=[lane], go=[lane], since=since)
     return lanes[0].result
 
 
@@ -148,7 +156,7 @@
     for bit in reversed(plan.far_bits):
         pairs = plan.flip_pairs(bit * 2 * plan.rows)
         arrived = yield held, pairs
-        held = jnp.stack([held, arrived], axis=1).reshape(-1, *shard.shape)
+        held = jnp.concatenate([held, arrived], axis=0)
     for stage in range(plan.stages - 1):
         held = jnp.concatenate([held, (yield held, plan.stage_pairs(stage))], axis=0)
     last = yield held, plan.stage_pairs(plan.stages - 1)
@@ -156,55 +164,66 @@
     return finish([held, last, *from_core])
 
 
-def grad_lane(plan, own, other, right, small=None):
-    swapped = yield [other, right], plan.flip_pairs(plan.rows)
-    left = jnp.concatenate([own, swapped[0]], axis=0)
-    both = jnp.concatenate([right, swapped[1]], axis=0)
+def grad_lane(plan, lefts, rights, split=0):
+    others = [other for _, other in lefts]
+    if len(rights) > 1:
+        others, sent = [jnp.concatenate(others, axis=1)], [jnp.concatenate(rights, axis=1)]
+    else:
+        sent = rights
+    arrived = yield [others[0], sent[0]], plan.flip_pairs(plan.rows)
+    columns = np.cumsum([0] + [right.shape[1] for right in rights])
+    size = lefts[0][0].shape[1]
+    left = [
+        jnp.concatenate([own, arrived[0][:, k * size : (k + 1) * size]], axis=0)
+        for k, (own, _) in enumerate(lefts)
+    ]
+    both = [
+        jnp.concatenate([right, arrived[1][:, columns[k] : columns[k + 1]]], axis=0)
+        for k, right in enumerate(rights)
+    ]
     left, both = lax.optimization_barrier((left, both))
-    half = left.shape[1] // 2
-    away = [dot_over_frames(left[:, half:], both).astype(BF16)]
-    kept = None
-    if small:
-        little = small()
-        columns = little.shape[1] // 2
-        away.append(after(little[:, columns:], away[0]))
-        little = little[:, :columns]
-    for stage in reversed(range(plan.stages)):
-        arrived = yield away, plan.stage_pairs(stage)
-        if kept is None:
-            kept = dot_over_frames(left[:, :half], both).astype(BF16)
-        if small:
-            little = little + after(arrived[1], arrived[0])
-        if stage > 0:
+
+    def products(first, last):
+        parts = [
+            dot_over_frames(one[:, size * first // 4 : size * last // 4], other).astype(BF16)
+            for one, other in zip(left, both)
+        ]
+        return jnp.concatenate(parts, axis=1) if len(parts) > 1 else parts[0]
+
+    away, kept = None, None
+    halvings = plan.halvings()
+    for count, pairs in enumerate(halvings):
+        if count == 0:
+            parts = (products(3, 4), products(2, 3)) if split else (products(2, 4),)
+        elif count < split:
+            half, quarter = kept.shape[0] // 2, kept.shape[0] // 4
+            parts = (
+                (kept[half + quarter :].astype(F32) + onward[quarter:].astype(F32)).astype(BF16),
+                (kept[half : half + quarter].astype(F32) + onward[:quarter].astype(F32)).astype(BF16),
+            )
+        else:
             half = kept.shape[0] // 2
-            away = [(kept[half:].astype(F32) + arrived[0][half:].astype(F32)).astype(BF16)]
-            kept = kept[:half].astype(F32) + arrived[0][:half].astype(F32)
-            kept = kept.astype(BF16)
-            if small:
-                columns = little.shape[1] // 2
-                away.append(little[:, columns:])
-                little = little[:, :columns]
-    size = kept.shape[0] // (len(plan.far) + 1)
-    away = []
-    for block in range(1, len(plan.far) + 1):
-        rows = slice(block * size, (block + 1) * size)
-        away.append([(kept[rows].astype(F32) + arrived[0][rows].astype(F32)).astype(BF16)])
-    total = kept[:size].astype(F32) + arrived[0][:size].astype(F32)
-    if small:
-        size = little.shape[1] // (len(plan.far) + 1)
-        for block in range(1, len(plan.far) + 1):
-            away[block - 1].append(little[:, block * size : (block + 1) * size])
-        little = little[:, :size]
-    arrived = yield (
-        [x for pair in away for x in pair],
-        [plan.flip_pairs(far) for far in plan.far for _ in range(2 if small else 1)],
-    )
-    step = 2 if small else 1
-    for one in arrived[::step]:
-        total = total + one.astype(F32)
-    if small:
-        little = little + sum(after(arrived[1::2], arrived[::2]))
-    return (total, little) if small else total
+            parts = ((kept[half:].astype(F32) + onward.astype(F32)).astype(BF16),)
+        if count == 0:
+            kept = products(0, 2)
+        else:
+            kept = (kept[:half].astype(F32) + stay.astype(F32)).astype(BF16)
+        if len(parts) == 2:
+            onward, stay = yield list(parts), pairs
+        else:
+            arrived = yield parts[0], pairs
+            onward, stay = arrived[arrived.shape[0] // 2 :], arrived[: arrived.shape[0] // 2]
+    total = kept.astype(F32) + arrived.astype(F32)
+    return [total[:, columns[k] : columns[k + 1]] for k in range(len(rights))]
+
+
+def small_grad_lane(plan, both):
+    half = both.shape[1] // 2
+    total = both[:, :half] + (yield both[:, half:], plan.flip_pairs(plan.rows))
+    for pairs in plan.halvings():
+        half = total.shape[1] // 2
+        total = total[:, :half] + (yield total[:, half:], pairs)
+    return total
 
 
 def heads_lane(plan, x):
@@ -674,14 +693,14 @@
     small = Lane(small_lane(jnp.concatenate([norm_gains, depth_kernel], axis=0)))
     g1, g2 = weights_lane(ffn1_in), weights_lane(ffn1_out)
     w_qkv = lax.all_gather(attn_qkv, BOTH, axis=0, tiled=True)
-    wides = (attn_out, conv_in, conv_out, ffn2_in)
-
-    def late_weights(*tokens):
-        shards = after((jnp.concatenate(wides, axis=1), ffn2_out), list(tokens))
-        middle = lax.all_gather(shards[0], BOTH, axis=0, tiled=True)
-        cuts = np.cumsum([0] + [shard.shape[1] for shard in wides])
-        parts = tuple(middle[:, start:stop] for start, stop in zip(cuts[:-1], cuts[1:]))
-        return parts + (lax.all_gather(shards[1], BOTH, axis=0, tiled=True),)
+    wides = (attn_out, conv_in, conv_out)
+    middle = lax.all_gather(jnp.concatenate(wides, axis=1), BOTH, axis=0, tiled=True)
+    cuts = np.cumsum([0] + [shard.shape[1] for shard in wides])
+    w_attn_out, w_conv_in, w_conv_out = (
+        middle[:, start:stop] for start, stop in zip(cuts[:-1], cuts[1:])
+    )
+    w_ffn2_in = lax.all_gather(ffn2_in, BOTH, axis=0, tiled=True)
+    g4 = weights_lane(ffn2_out)
 
     source = jnp.repeat(jnp.concatenate(orders), block) * block + feature % block
     tree_pick = (feature[:, None] == source[None, :]).astype(BF16)
@@ -752,7 +771,7 @@
         step(land=[g1], go=[g1])
         step(land=[g2])
         follow(g2, g1)
-    w_attn_out, w_conv_in, w_conv_out, w_ffn2_in, w_ffn2_out = late_weights(*ready(g2))
+    follow(g4, g2)
     (w_ffn1_in,) = finish(g1)
     before_1 = dot(ffn1_hidden, w_ffn1_in)
     after_1 = (before_1 * jax.nn.sigmoid(before_1)).astype(BF16)
@@ -761,6 +780,7 @@
     attn_norm, attn_normed, attn_scale = layer_norm(first, gains[1])
     attn_hidden = attn_norm.astype(BF16)
     packed = dot(attn_hidden, w_qkv)
+    step(land=[g4], go=[g4], since=[packed])
     queries = packed[:, :width]
     keys = packed[:, width : 2 * width]
     queries = (queries * cosine + half_turn(queries) * sine).astype(BF16)
@@ -781,12 +801,19 @@
         x = x.reshape(row_count, wide, frames_here, group)
         return x.transpose(1, 0, 2, 3).reshape(wide, tokens, group)
 
+    step(go=[heads])
+    step(land=[heads], go=[heads])
+    step(land=[g4], since=ready(heads)[0])
     arrived = finish(heads)
+    hold(g4, arrived)
     row_queries = as_rows(arrived[..., :group])
     row_keys = as_rows(arrived[..., group : 2 * group])
     row_values = as_rows(arrived[..., 2 * group :])
     mixed_rows, row_totals = attend(row_queries, row_keys, row_values, row_ids)
     heads = Lane(heads_lane(plan, as_blocks(mixed_rows)))
+    step(go=[heads])
+    step(land=[heads], go=[heads])
+    step(land=[g4], go=[g4], since=ready(heads)[0])
     mixed = from_groups(finish(heads))
     second = first + dot(mixed, w_attn_out)
     conv_norm, conv_normed, conv_scale = layer_norm(second, gains[2])
@@ -799,6 +826,7 @@
         [before, glu, after_frames, jnp.zeros((row_count, 32 - 2 * half_width, width), BF16)],
         axis=1,
     )
+    step(land=[g4], go=[g4], since=[gate_sig])
     convolved = depthwise(extended, edge_ids, kernel).reshape(tokens, width)
     inner_out, inner_normed, inner_scale = layer_norm(convolved, gains[3])
     activated = (inner_out * jax.nn.sigmoid(inner_out)).astype(BF16)
@@ -807,33 +835,33 @@
     ffn2_hidden = ffn2_norm.astype(BF16)
     before_2 = dot(ffn2_hidden, w_ffn2_in)
     after_2 = (before_2 * jax.nn.sigmoid(before_2)).astype(BF16)
+    (w_ffn2_out,) = finish(g4)
     fourth = third + 0.5 * dot(after_2, w_ffn2_out)
     final_out, final_normed, final_scale = layer_norm(fourth, gains[5])
     layer_out = final_out.astype(BF16).reshape(inputs.shape)
 
-    def grads(left, right, small=None):
-        return Lane(grad_lane(plan, *left, right, small))
+    def grads(*pairs, split=0):
+        lefts, rights = [left for left, _ in pairs], [right for _, right in pairs]
+        return Lane(grad_lane(plan, lefts, rights, split))
 
     gradient, gain_final = norm_backward(
         cotangent.astype(F32).reshape(tokens, width), gains[5], final_normed, final_scale
     )
     branch = (0.5 * gradient).astype(BF16)
-    r1 = grads(pick_columns(plan, after_2, orders), branch)
+    r1 = grads((pick_columns(plan, after_2, orders), branch))
     r1.go()
     before_grad = (dot_back(branch, w_ffn2_out) * swish_slope(before_2)).astype(BF16)
-    r2 = grads(pick(ffn2_hidden), before_grad)
+    r2 = grads((pick(ffn2_hidden), before_grad))
     r2.go()
-    step(land=[r1], go=[r1], since=[before_grad])
+    step(land=[r1], go=[r1])
     input_grad, gain_ffn2 = norm_backward(
         dot_back(before_grad, w_ffn2_in), gains[4], ffn2_normed, ffn2_scale
     )
     gradient = gradient + input_grad
     conv_branch = after(gradient.astype(BF16), jax.tree.leaves(ready(r1)))
-    r3 = grads(pick(activated), conv_branch)
-    r3.go()
     act_grad = dot_back(conv_branch, w_conv_out) * swish_slope(inner_out)
     conv_grad, gain_inner = norm_backward(act_grad, gains[3], inner_normed, inner_scale)
-    step(land=[r2], go=[r2], since=[conv_branch])
+    step(land=[r2], go=[r2])
     kernel_terms, ext_grad = depthwise_back(
         extended,
         edge_ids,
@@ -857,22 +885,19 @@
         [glu_grad * gate_sig, glu_grad * gated[:, :width] * gate_sig * (1.0 - gate_sig)],
         axis=-1,
     ).astype(BF16)
-    r4 = grads(pick(conv_hidden), gated_grad)
-    r4.go()
     norm_grad, gain_conv = norm_backward(
         dot_back(gated_grad, w_conv_in), gains[2], conv_normed, conv_scale
     )
     gradient = gradient + norm_grad
-    attn_branch = step(
-        land=[r1, r3], go=[r1, r3], chain=gradient.astype(BF16), since=[kernel_terms]
-    )
+    attn_branch = gradient.astype(BF16)
     head_grads = dot_back(attn_branch, w_attn_out).astype(BF16)
     heads = Lane(heads_lane(plan, to_groups(head_grads)))
-    r5 = grads(pick(mixed), attn_branch)
-    r5.go()
-    step(go=[heads])
+    r3 = grads(
+        (pick(activated), conv_branch), (pick(conv_hidden), gated_grad), (pick(mixed), attn_branch)
+    )
+    step(go=[heads, r3])
     step(land=[heads], go=[heads])
-    step(land=[r2, r4], go=[r2, r4], since=ready(heads)[0])
+    step(land=[r1, r3], go=[r1, r3], since=ready(heads)[0])
     row_grads = as_rows(finish(heads))
     query_grad, key_grad, value_grad = attend_back(
         row_queries,
@@ -884,7 +909,7 @@
         row_ids,
         row_cosine,
         row_sine,
-        jax.tree.leaves(ready(r2, r4)),
+        jax.tree.leaves(ready(r1, r3)),
     )
     heads = Lane(
         heads_lane(
@@ -896,51 +921,55 @@
     )
     step(go=[heads])
     step(land=[heads], go=[heads])
-    step(land=[r1, r2, r3, r4, r5], go=[r3, r4, r5], since=ready(heads)[0])
+    step(land=[r1, r2, r3], go=[r2, r3], since=ready(heads)[0])
     returned = finish(heads)
-    returned = after(returned, jax.tree.leaves(ready(r1, r2, r3, r4, r5)))
+    returned = after(returned, jax.tree.leaves(ready(r1, r2, r3)))
     hold(r1, returned)
-    hold(r2, returned)
     packed_grad = jnp.concatenate(
         [from_groups(returned[..., part * group : (part + 1) * group]) for part in range(3)],
         axis=-1,
     )
     packed_grad = lax.optimization_barrier(packed_grad)
-    r6 = grads(pick(attn_hidden), packed_grad)
+    r6 = grads((pick(attn_hidden), packed_grad), split=0)
     r6.go()
     norm_grad, gain_attn = norm_backward(
         dot_back(packed_grad, w_qkv), gains[1], attn_normed, attn_scale
     )
     gradient = gradient + norm_grad
     branch = (0.5 * gradient).astype(BF16)
+    step(land=[r2], go=[r2], since=[packed_grad])
     branch = step(land=[r6], go=[r6], chain=branch)
-    r7 = grads(pick_columns(plan, after_1, orders), branch)
+    r7 = grads((pick_columns(plan, after_1, orders), branch), split=1)
     r7.go()
     before_grad = (dot_back(branch, w_ffn1_out) * swish_slope(before_1)).astype(BF16)
     before_grad = lax.optimization_barrier(before_grad)
-
-    def small_sums():
-        total = jnp.concatenate([grad_gains, grad_kernel], axis=0)
-        total = jnp.dot(total, tree_pick.astype(F32), precision=HIGHEST)
-        return total[:, : width // 2] + send(total[:, width // 2 :], plan.flip_pairs(plan.rows))
-
-    before_grad = lax.optimization_barrier(before_grad)
-    r8 = grads(pick(ffn1_hidden), before_grad, small_sums)
+    r8 = grads((pick(ffn1_hidden), before_grad), split=2)
     r8.go()
-    before_grad = step(land=[r7], go=[r7], chain=before_grad)
+    step(land=[r1, r2, r3], go=[r1, r2, r3], since=[branch])
+    step(land=[r7, r8], go=[r7, r8])
+    before_grad = after(before_grad, jax.tree.leaves(ready(r1, r2, r3, r7, r8)))
     input_grad, gain_ffn1 = norm_backward(
         dot_back(before_grad, w_ffn1_in), gains[0], ffn1_normed, ffn1_scale
     )
     gradient = gradient + input_grad
     grad_gains = jnp.stack([gain_ffn1, gain_attn, gain_conv, gain_inner, gain_ffn2, gain_final])
-    step(land=[r8], go=[r8])
-    step(land=[r1, r2, r3, r4, r5], go=[r3, r4, r5], since=[gradient])
+    small_sums = jnp.concatenate([grad_gains, grad_kernel], axis=0)
+    small_sums = jnp.dot(small_sums, tree_pick.astype(F32), precision=HIGHEST)
+    r9 = Lane(small_grad_lane(plan, small_sums))
+    finish(r1, r2, since=[before_grad])
+    step(land=[r3], go=[r3], since=[before_grad])
+    hold(r9, *r1.result, *r2.result)
     step(land=[r6], go=[r6])
-    finish(r1, r2, r3, r4, r5, r6, r7, r8)
-    grad_ffn1_in, small_shard = r8.result
-    grad_ffn1_out, grad_qkv = r7.result, r6.result
-    grad_attn_out, grad_conv_in, grad_conv_out = r5.result, r4.result, r3.result
-    grad_ffn2_in, grad_ffn2_out = r2.result, r1.result
+    step(land=[r7], go=[r7], since=[input_grad, *waited(r6)])
+    while r8.operand is not None:
+        step(land=[r9], since=jax.tree.leaves(ready(r8)))
+        r9.go()
+        step(land=[r7, r8], go=[r7, r8])
+        step(land=[r1, r2, r3, r6], go=[r1, r2, r3, r6], since=jax.tree.leaves(ready(r8))[:1])
+    finish(r1, r2, r3, r6, r7, r9)
+    (grad_ffn1_in,), (grad_ffn1_out,), (grad_qkv,) = r8.result, r7.result, r6.result
+    grad_conv_out, grad_conv_in, grad_attn_out = r3.result
+    (grad_ffn2_in,), (grad_ffn2_out,), small_shard = r2.result, r1.result, r9.result
     shard_gains, shard_kernel = small_shard[: grad_gains.shape[0]], small_shard[grad_gains.shape[0] :]
 
     return (

time: 822 us -> 739 us (0.90)
  starting transfers between devices: 164 us -> 115 us
  waiting for transfers between devices: 221 us -> 176 us
  matrix products: 142 us -> 126 us
  other arithmetic: 123 us -> 137 us
    ppermute x95 -> x83, starting transfers between devices: 158 us -> 108 us  [send(): return lax.ppermute(x, BOTH, pairs)]
    ppermute x95 -> x83, waiting for transfers between devices: 216 us -> 175 us  [send(): return lax.ppermute(x, BOTH, pairs)]
    convert_element_type x17 -> x20, other arithmetic: 19.8 us -> 30.9 us  [the longest x12 23 us: grad_lane(): kept = (kept[:half].astype(F32) + stay.astype(F32)).astype(BF16)]
    concatenate x17 -> x22, other arithmetic: 12.3 us -> 22.4 us  [the longest x8 7.51 us: grad_lane(): jnp.concatenate([own, arrived[0][:, k * size:(k + 1) * size]], axis=0)]
    dot_general x18, matrix products: 52.5 us -> 43.9 us  [dot(): return jnp.dot(left, right, preferred_element_type=F32)]
    dot_general x16 -> x18, matrix products: 39.1 us -> 33.6 us  [dot_over_frames(): lax.dot_general(left, right, (((0,), (0,)), ((), ())), preferred_element_...]
    select_n x37 -> x32, other arithmetic: 47.7 us -> 42.4 us  [after(): jnp.where(flag, x, jnp.zeros((), x.dtype))]
    unnamed x278 -> x327, local copies, waits for them, and re-layouts: 18.5 us -> 16.3 us
  transfers between devices with their start and end apart: 102 -> 90, of which waited for: 34 -> 24; matrix products, arithmetic and copies ran while one was open for 36% -> 41% of each run, Pallas kernels for 6% -> 11%
where the time goes in v2:
time: 739 us; the launch traced here: 727 us
  waiting for transfers between devices  176 us (24%)
  other arithmetic  137 us (19%)
  matrix products  126 us (17%)
  starting transfers between devices  115 us (16%)
  Pallas kernels  81.5 us (11%)
  local copies, waits for them, and re-layouts  55.2 us (7%)
  between operations  36.9 us (5%)
    ppermute x83, waiting for transfers between devices, send(): return lax.ppermute(x, BOTH, pairs)  175 us
    ppermute x83, starting transfers between devices, send(): return lax.ppermute(x, BOTH, pairs)  108 us
    dot_general x12, matrix products, dot_back(): lax.dot_general(left, right, (((1,), (1,)), ((), ())), preferred_element_...  46 us
    dot_general x18, matrix products, dot(): return jnp.dot(left, right, preferred_element_type=F32)  43.9 us
    select_n x32, other arithmetic, after(): jnp.where(flag, x, jnp.zeros((), x.dtype))  42.4 us
    dot_general x18, matrix products, dot_over_frames(): lax.dot_general(left, right, (((0,), (0,)), ((), ())), preferred_element_...  33.6 us
    pallas_call x1, Pallas kernels, attend_back(): pl.pallas_call(lambda *refs: attend_back_kernel(*refs[:13], *refs[13 + le...  23.7 us
    convert_element_type x12, other arithmetic, grad_lane(): kept = (kept[:half].astype(F32) + stay.astype(F32)).astype(BF16)  23 us
  transfers between devices with their start and end apart: 90, of which 24 were waited for; matrix products, arithmetic and copies ran while one was open for 41% of the time, Pallas kernels for 11%

profile of v2, /device:TPU:0, one launch (start us, length us, event | category | flops | bytes accessed | tf_op | source)
XLA Modules:
  0.0 727.5 jit_solution(191712479507281254)
XLA Ops:
  10.5 3.0 collective-permute-start
  24.6 5.7 collective-permute-done.3
  32.3 5.3 collective-permute-start.4
  37.7 10.0 %collective-permute-done.4 = bf16[37,512]{1,0:T(8,128)(2,1)S(1)} collective-permute-done((bf16[37,512]{1,0:T(8,128)(2,1)}, bf16[37,512]{1,0:T(8,128)(2,1)S(1)}, u32[]{:S(2)}, u32[]{:S(2)}) %collective-permute-start.4) | collective-permute-done | bytes 37920 | tf_op jit(solution)/shard_map/ppermute | solution.py:68
  53.0 5.2 collective-permute-start.11
  58.2 7.8 %collective-permute-done.7 = bf16[4,128,1024]{2,1,0:T(8,128)(2,1)} collective-permute-done((bf16[4,128,1024]{2,1,0:T(8,128)(2,1)S(1)}, bf16[4,128,1024]{2,1,0:T(8,128)(2,1)}, u32[]{:S(2)}, u32[]{:S(2)}) %collective-permute-start.7) | collective-permute-done | bytes 1048608 | tf_op jit(solution)/shard_map/ppermute | solution.py:68
  71.7 4.6 collective-permute-start.12
  77.5 22.9 %collective-permute-done.12 = bf16[2,128,1024]{2,1,0:T(8,128)(2,1)S(1)} collective-permute-done((bf16[2,128,1024]{2,1,0:T(8,128)(2,1)S(1)}, bf16[2,128,1024]{2,1,0:T(8,128)(2,1)S(1)}, u32[]{:S(2)}, u32[]{:S(2)}) %collective-permute-start.12) | collective-permute-done | bytes 524320 | tf_op jit(solution)/shard_map/ppermute | solution.py:68
  107.0 12.5 %collective-permute-done.13 = bf16[4,128,1024]{2,1,0:T(8,128)(2,1)} collective-permute-done((bf16[4,128,1024]{2,1,0:T(8,128)(2,1)}, bf16[4,128,1024]{2,1,0:T(8,128)(2,1)}, u32[]{:S(2)}, u32[]{:S(2)}) %collective-permute-start.13) | collective-permute-done | bytes 1048608 | tf_op jit(solution)/shard_map/ppermute | solution.py:68
  119.4 3.6 broadcast_select_fusion.6
  125.0 5.6 fusion.85
  140.1 13.0 %collective-permute-done.14.refs_1_ = bf16[8,128,1024]{2,1,0:T(8,128)(2,1)} collective-permute-done((bf16[8,128,1024]{2,1,0:T(8,128)(2,1)}, bf16[8,128,1024]{2,1,0:T(8,128)(2,1)}, u32[]{:S(2)}, u32[]{:S(2)}) %collective-permute-start.14) | collective-permute-done | bytes 2097184 | tf_op jit(solution)/shard_map/ppermute | solution.py:68
  156.0 5.1 assemble.3
  161.2 4.6 multiply_convert_fusion.1
  166.1 3.0 assemble.4
  172.6 4.7 fusion.213.refs_0_
  189.9 3.5 collective-permute-start.27
  205.4 5.7 collective-permute-done.27
  214.1 9.3 %collective-permute-done.18 = bf16[2,256,384]{2,1,0:T(8,128)(2,1)} collective-permute-done((bf16[2,256,384]{2,1,0:T(8,128)(2,1)S(1)}, bf16[2,256,384]{2,1,0:T(8,128)(2,1)}, u32[]{:S(2)}, u32[]{:S(2)}) %collective-permute-start.18) | collective-permute-done | bytes 393248 | tf_op jit(solution)/shard_map/ppermute | solution.py:68
  223.4 21.6 %collective-permute-done.19 = bf16[2,256,384]{2,1,0:T(8,128)(2,1)} collective-permute-done((bf16[2,256,384]{2,1,0:T(8,128)(2,1)S(1)}, bf16[2,256,384]{2,1,0:T(8,128)(2,1)}, u32[]{:S(2)}, u32[]{:S(2)}) %collective-permute-start.19) | collective-permute-done | bytes 393248 | tf_op jit(solution)/shard_map/ppermute | solution.py:68
  249.6 13.4 %attend.1 = (bf16[2,1024,128]{2,1,0:T(8,128)(2,1)}, f32[2,1024,2]{2,1,0:T(8,128)}) custom-call(bf16[2,1024,128]{2,1,0:T(8,128)(2,1)} %bitcast.341, bf16[2,1024,128]{2,1,0:T(8,128)(2,1)} %bitcast.343, bf16[2,1024,128]{2,1,0:T(8,128)(2,1)} %bitcast.345, s32[2,1024,1]{2,1,0:T(8,128)} %copy.90.refs_3_.refs_7_, s32[2,1,1024]{2,1,0:T(1,128)} %bitcast.398), custom_call_target="tpu_custom_call" | custom-call | tf_op jit(solution)/shard_map/attend/pallas_call | solution.py:431
  269.4 12.5 %collective-permute-start.22 = (bf16[2,256,128]{2,1,0:T(8,128)(2,1)S(1)}, bf16[2,256,128]{2,1,0:T(8,128)(2,1)S(1)}, u32[]{:S(2)}, u32[]{:S(2)}) collective-permute-start(bf16[2,256,128]{2,1,0:T(8,128)(2,1)S(1)} %get-tuple-element.196.refs_0_), channel_id=1, source_target_pairs={{0,8},{1,9},{2,10},{3,11},{4,12},{5,13},{6,14},{7,15},{8,0},{9,1},... | collective-permute-start | bytes 393224 | tf_op jit(solution)/shard_map/ppermute | solution.py:68
  293.6 7.6 %collective-permute-done.24 = bf16[2,256,128]{2,1,0:T(8,128)(2,1)S(1)} collective-permute-done((bf16[2,256,128]{2,1,0:T(8,128)(2,1)S(1)}, bf16[2,256,128]{2,1,0:T(8,128)(2,1)S(1)}, u32[]{:S(2)}, u32[]{:S(2)}) %collective-permute-start.24) | collective-permute-done | bytes 131104 | tf_op jit(solution)/shard_map/ppermute | solution.py:68
  312.1 3.6 fusion.20
  325.7 4.9 depthwise.1
  336.1 3.1 broadcast_select_fusion.5.refs_1_
  340.9 7.8 %multiply_convert_fusion = (bf16[256,4096]{1,0:T(8,128)(2,1)S(1)}, f32[256,4096]{1,0:T(8,128)}) fusion(bf16[1024,4096]{1,0:T(8,128)(2,1)} %all-gather.8.cloned.1.call-done, f32[256,1024]{1,0:T(8,128)S(1)} %get-tuple-element.231, f32[1024]{0:T(1024)S(1)} %bitcast.417, f32[256]{0:T(256)S(1)} %add_rsqrt_fusion.1, f32[256]{0:T(256)S(1)} %broadcast_multiply_fusion.12), kind=kOutput, calls=%fused_computation.21 | convolution fusion | flops 2153775104 | bytes 15734784 | tf_op jit(solution)/shard_map/dot_general | solution.py:335
  355.5 4.3 assemble.5
  365.0 4.2 fusion
  369.7 8.1 %multiply_reduce_fusion = (f32[1024]{0:T(1024)}, f32[256]{0:T(256)S(1)}, f32[256]{0:T(256)S(1)}, f32[256,1024]{1,0:T(8,128)}) fusion(f32[256,1024]{1,0:T(8,128)S(1)} %copy-done.25, f32[256]{0:T(256)S(1)} %add_rsqrt_fusion.1, f32[256]{0:T(256)S(1)} %broadcast_multiply_fusion.12, f32[1024]{0:T(1024)S(1)} %bitcast.419, bf16[256,4096]{1,0:T(8,128)(2,1)} %fusion, ...), kind=kOutput, calls=%fused_computation.209 | convolution fusion | flops 2149579264 | bytes 12595200 | tf_op jit(solution)/shard_map/dot_general | solution.py:339
  385.0 3.6 multiply_reduce_fusion.1
  393.6 8.4 %depthwise_back.1 = (f32[2,31,1024]{2,1,0:T(8,128)S(1)}, f32[2,160,1024]{2,1,0:T(8,128)S(1)}) custom-call(bf16[2,160,1024]{2,1,0:T(8,128)(2,1)S(1)} %copy-done.6, f32[2,160,1]{2,1,0:T(8,128)S(1)} %copy-done.7, f32[2,128,1024]{2,1,0:T(8,128)S(1)} %bitcast.334, f32[31,1024]{1,0:T(8,128)S(1)} %slice.811.refs_2_.refs_3_, ...), custom_call_target="tpu_custom_call" | custom-call | tf_op jit(solution)/shard_map/depthwise_back/pallas_call | solution.py:565
  417.4 3.1 fusion.81
  421.6 4.8 convolution_convert_fusion.1
  434.6 5.4 collective-permute-done.42
  456.8 23.7 %attend_back.1 = (bf16[2,1024,128]{2,1,0:T(8,128)(2,1)}, bf16[2,1024,128]{2,1,0:T(8,128)(2,1)}, bf16[2,1024,128]{2,1,0:T(8,128)(2,1)}) custom-call(bf16[2,1024,128]{2,1,0:T(8,128)(2,1)} %bitcast.342, bf16[2,1024,128]{2,1,0:T(8,128)(2,1)} %bitcast.344, bf16[2,1024,128]{2,1,0:T(8,128)(2,1)} %bitcast.346, bf16[2,1024,128]{2,1,0:T(8,128)(2,1)} %get-tuple-element.41.refs_3_, ...), custom_call_target="tpu_custom_call" | custom-call | tf_op jit(solution)/shard_map/attend_back/pallas_call | solution.py:460
  503.7 19.4 %collective-permute-done.49 = bf16[256,4096]{1,0:T(8,128)(2,1)} collective-permute-done((bf16[256,4096]{1,0:T(8,128)(2,1)}, bf16[256,4096]{1,0:T(8,128)(2,1)}, u32[]{:S(2)}, u32[]{:S(2)}) %collective-permute-start.49) | collective-permute-done | bytes 2097184 | tf_op jit(solution)/shard_map/ppermute | solution.py:68
  549.7 6.9 multiply_reduce_fusion.3
  562.5 3.4 fusion.121
  567.0 7.5 %fusion.1 = bf16[256,4096]{1,0:T(8,128)(2,1)S(1)} fusion(bf16[256,1024]{1,0:T(8,128)(2,1)} %get-tuple-element.100.refs_0_, bf16[4096,1024]{1,0:T(8,128)(2,1)} %copy-done.4, f32[256,4096]{1,0:T(8,128)} %get-tuple-element.225), kind=kOutput, calls=%fused_computation.5 | convolution fusion | flops 2156920832 | bytes 15204352 | tf_op jit(solution)/shard_map/dot_general | solution.py:339
  610.8 8.4 %multiply_reduce_fusion.4 = (f32[1024]{0:T(1024)}, f32[256]{0:T(256)}, f32[256]{0:T(256)}, f32[256,1024]{1,0:T(8,128)}) fusion(bf16[2,128,1024]{2,1,0:T(8,128)(2,1)S(1)} %copy-done.42, f32[256]{0:T(256)S(1)} %copy-done.144, f32[256]{0:T(256)S(1)} %copy-done.142, f32[1024]{0:T(1024)S(1)} %bitcast.406, bf16[256,4096]{1,0:T(8,128)(2,1)} %broadcast_select_fusion.refs_0_, ...), kind=kOutput, calls=%fused_computation.213 | convolution fusion | flops 2149841408 | bytes 12070912 | tf_op jit(solution)/shard_map/dot_general | solution.py:339
  628.8 5.0 convolution_convert_fusion
  643.0 4.3 add_convert_fusion.1
  670.2 3.8 collective-permute-done.66
  686.3 2.9 collective-permute-start.75
  689.3 15.1 %collective-permute-done.67 = bf16[64,4096]{1,0:T(8,128)(2,1)S(1)} collective-permute-done((bf16[64,4096]{1,0:T(8,128)(2,1)}, bf16[64,4096]{1,0:T(8,128)(2,1)S(1)}, u32[]{:S(2)}, u32[]{:S(2)}) %collective-permute-start.67) | collective-permute-done | bytes 524320 | tf_op jit(solution)/shard_map/ppermute | solution.py:68
  706.5 2.9 collective-permute-start.86
  712.1 6.6 collective-permute-done.86
  (787 shorter events, 329.1 us)
Async XLA Ops:
  7.2 165.4 %all-gather.4.cloned.1.call-start = ((), (), s32[]{:S(2)}) async-start(), calls=%async_computation | async-start | bytes 6488064 | tf_op jit(solution)/shard_map/all_gather | solution.py:695
  7.9 301.3 %all-gather.6.cloned.1.call-start = ((), (), s32[]{:S(2)}) async-start(), calls=%async_computation.1 | async-start | bytes 8650752 | tf_op jit(solution)/shard_map/all_gather | solution.py:697
  9.7 331.3 %all-gather.8.cloned.1.call-start = ((), (), s32[]{:S(2)}) async-start(), calls=%async_computation.2 | async-start | bytes 8650752 | tf_op jit(solution)/shard_map/all_gather | solution.py:702
  67.7 38.1 %collective-permute-start.8 = (bf16[8,128,1024]{2,1,0:T(8,128)(2,1)S(1)}, bf16[8,128,1024]{2,1,0:T(8,128)(2,1)}, u32[]{:S(2)}, u32[]{:S(2)}) collective-permute-start(bf16[8,128,1024]{2,1,0:T(8,128)(2,1)S(1)} %pad_maximum_fusion.3.refs_0_), channel_id=1, source_target_pairs={{0,2},{1,3},{2,0},{3,1},{4,5},{5,4},{6,7},{7,6},{8,10},{9,11},{10,... | collective-permute-start | bytes 6291464 | tf_op jit(solution)/shard_map/ppermute | solution.py:68
  71.7 28.7 %collective-permute-start.12 = (bf16[2,128,1024]{2,1,0:T(8,128)(2,1)S(1)}, bf16[2,128,1024]{2,1,0:T(8,128)(2,1)S(1)}, u32[]{:S(2)}, u32[]{:S(2)}) collective-permute-start(bf16[2,128,1024]{2,1,0:T(8,128)(2,1)S(1)} %maximum_select_fusion.4), channel_id=1, source_target_pairs={{0,8},{1,9},{2,10},{3,11},{4,12},{5,13},{6,14},{7,15},{8,0},{9,1},... | collective-permute-start | bytes 1572872 | tf_op jit(solution)/shard_map/ppermute | solution.py:68
  123.0 30.1 %collective-permute-start.14 = (bf16[8,128,1024]{2,1,0:T(8,128)(2,1)}, bf16[8,128,1024]{2,1,0:T(8,128)(2,1)}, u32[]{:S(2)}, u32[]{:S(2)}) collective-permute-start(bf16[8,128,1024]{2,1,0:T(8,128)(2,1)} %get-tuple-element.144.refs_0_), channel_id=1, source_target_pairs={{0,2},{1,3},{2,0},{3,1},{4,5},{5,4},{6,7},{7,6},{8,10},{9,11},{10,... | collective-permute-start | bytes 6291464 | tf_op jit(solution)/shard_map/ppermute | solution.py:68
  130.5 25.5 %collective-permute-start.9 = (bf16[8,128,1024]{2,1,0:T(8,128)(2,1)S(1)}, bf16[8,128,1024]{2,1,0:T(8,128)(2,1)}, u32[]{:S(2)}, u32[]{:S(2)}) collective-permute-start(bf16[8,128,1024]{2,1,0:T(8,128)(2,1)S(1)} %copy-done.1), channel_id=1, source_target_pairs={{0,4},{1,5},{2,6},{3,7},{4,0},{5,1},{6,2},{7,3},{8,12},{9,13},{10,... | collective-permute-start | bytes 6291464 | tf_op jit(solution)/shard_map/ppermute | solution.py:68
  130.5 25.5 %collective-permute-start.10 = (bf16[8,128,1024]{2,1,0:T(8,128)(2,1)}, bf16[8,128,1024]{2,1,0:T(8,128)(2,1)}, u32[]{:S(2)}, u32[]{:S(2)}) collective-permute-start(bf16[8,128,1024]{2,1,0:T(8,128)(2,1)} %collective-permute-done.8.refs_1_), channel_id=1, source_target_pairs={{0,4},{1,5},{2,6},{3,7},{4,0},{5,1},{6,2},{7,3},{8,12},{9,13},{10,... | collective-permute-start | bytes 6291464 | tf_op jit(solution)/shard_map/ppermute | solution.py:68
  140.0 26.1 %collective-permute-start.15 = (bf16[8,128,1024]{2,1,0:T(8,128)(2,1)}, bf16[8,128,1024]{2,1,0:T(8,128)(2,1)S(1)}, u32[]{:S(2)}, u32[]{:S(2)}) collective-permute-start(bf16[8,128,1024]{2,1,0:T(8,128)(2,1)} %get-tuple-element.145.refs_0_), channel_id=1, source_target_pairs={{0,4},{1,5},{2,6},{3,7},{4,0},{5,1},{6,2},{7,3},{8,12},{9,13},{10,... | collective-permute-start | bytes 6291464 | tf_op jit(solution)/shard_map/ppermute | solution.py:68
  155.4 30.7 %collective-permute-start.61 = (bf16[256,512]{1,0:T(8,128)(2,1)}, bf16[256,512]{1,0:T(8,128)(2,1)}, u32[]{:S(2)}, u32[]{:S(2)}) collective-permute-start(bf16[256,512]{1,0:T(8,128)(2,1)} %get-tuple-element.177), channel_id=1, source_target_pairs={{0,4},{1,5},{2,6},{3,7},{4,0},{5,1},{6,2},{7,3},{8,12},{9,13},{10,... | collective-permute-start | bytes 786440 | tf_op jit(solution)/shard_map/ppermute | solution.py:68
  189.9 21.1 %collective-permute-start.27 = (bf16[1,128,1024]{2,1,0:T(8,128)(2,1)}, bf16[1,128,1024]{2,1,0:T(8,128)(2,1)}, u32[]{:S(2)}, u32[]{:S(2)}) collective-permute-start(bf16[1,128,1024]{2,1,0:T(8,128)(2,1)} %select_bitcast_fusion), channel_id=1, source_target_pairs={{0,16},{1,17},{2,18},{3,19},{4,20},{5,21},{6,22},{7,23},{8,24},{9,... | collective-permute-start | bytes 786440 | tf_op jit(solution)/shard_map/ppermute | solution.py:68
  195.5 88.1 %collective-permute-start.59 = (bf16[256,2048]{1,0:T(8,128)(2,1)}, bf16[256,2048]{1,0:T(8,128)(2,1)}, u32[]{:S(2)}, u32[]{:S(2)}) collective-permute-start(bf16[256,2048]{1,0:T(8,128)(2,1)} %get-tuple-element.62), channel_id=1, source_target_pairs={{0,4},{1,5},{2,6},{3,7},{4,0},{5,1},{6,2},{7,3},{8,12},{9,13},{10,... | collective-permute-start | bytes 3145736 | tf_op jit(solution)/shard_map/ppermute | solution.py:68
  198.9 24.5 %collective-permute-start.18 = (bf16[2,256,384]{2,1,0:T(8,128)(2,1)S(1)}, bf16[2,256,384]{2,1,0:T(8,128)(2,1)}, u32[]{:S(2)}, u32[]{:S(2)}) collective-permute-start(bf16[2,256,384]{2,1,0:T(8,128)(2,1)S(1)} %get-tuple-element.160.refs_0_), channel_id=1, source_target_pairs={{0,8},{1,9},{2,10},{3,11},{4,12},{5,13},{6,14},{7,15},{8,0},{9,1},... | collective-permute-start | bytes 1179656 | tf_op jit(solution)/shard_map/ppermute | solution.py:68
  200.4 44.7 %collective-permute-start.19 = (bf16[2,256,384]{2,1,0:T(8,128)(2,1)S(1)}, bf16[2,256,384]{2,1,0:T(8,128)(2,1)}, u32[]{:S(2)}, u32[]{:S(2)}) collective-permute-start(bf16[2,256,384]{2,1,0:T(8,128)(2,1)S(1)} %get-tuple-element.162.refs_1_), channel_id=1, source_target_pairs={{0,16},{1,17},{2,18},{3,19},{4,20},{5,21},{6,22},{7,23},{8,24},{9,... | collective-permute-start | bytes 1179656 | tf_op jit(solution)/shard_map/ppermute | solution.py:68
  200.9 44.2 %collective-permute-start.20 = (bf16[2,256,384]{2,1,0:T(8,128)(2,1)S(1)}, bf16[2,256,384]{2,1,0:T(8,128)(2,1)}, u32[]{:S(2)}, u32[]{:S(2)}) collective-permute-start(bf16[2,256,384]{2,1,0:T(8,128)(2,1)S(1)} %get-tuple-element.161.refs_2_), channel_id=1, source_target_pairs={{0,24},{1,25},{2,26},{3,27},{4,28},{5,29},{6,30},{7,31},{8,16},{9,... | collective-permute-start | bytes 1179656 | tf_op jit(solution)/shard_map/ppermute | solution.py:68
  211.1 76.8 %collective-permute-start.53 = (bf16[256,512]{1,0:T(8,128)(2,1)}, bf16[256,512]{1,0:T(8,128)(2,1)}, u32[]{:S(2)}, u32[]{:S(2)}) collective-permute-start(bf16[256,512]{1,0:T(8,128)(2,1)} %get-tuple-element.192), channel_id=1, source_target_pairs={{0,4},{1,5},{2,6},{3,7},{4,0},{5,1},{6,2},{7,3},{8,12},{9,13},{10,... | collective-permute-start | bytes 786440 | tf_op jit(solution)/shard_map/ppermute | solution.py:68
  223.4 41.5 %collective-permute-start.28 = (bf16[2,128,1024]{2,1,0:T(8,128)(2,1)}, bf16[2,128,1024]{2,1,0:T(8,128)(2,1)S(1)}, u32[]{:S(2)}, u32[]{:S(2)}) collective-permute-start(bf16[2,128,1024]{2,1,0:T(8,128)(2,1)} %pad_maximum_fusion.22), channel_id=1, source_target_pairs={{0,8},{1,9},{2,10},{3,11},{4,12},{5,13},{6,14},{7,15},{8,0},{9,1},... | collective-permute-start | bytes 1572872 | tf_op jit(solution)/shard_map/ppermute | solution.py:68
  266.3 39.8 %collective-permute-start.29 = (bf16[4,128,1024]{2,1,0:T(8,128)(2,1)S(1)}, bf16[4,128,1024]{2,1,0:T(8,128)(2,1)}, u32[]{:S(2)}, u32[]{:S(2)}) collective-permute-start(bf16[4,128,1024]{2,1,0:T(8,128)(2,1)S(1)} %maximum_select_fusion.2), channel_id=1, source_target_pairs={{0,1},{1,0},{2,3},{3,2},{4,6},{5,7},{6,4},{7,5},{8,9},{9,8},{10,11... | collective-permute-start | bytes 3145736 | tf_op jit(solution)/shard_map/ppermute | solution.py:68
  269.4 23.7 %collective-permute-start.22 = (bf16[2,256,128]{2,1,0:T(8,128)(2,1)S(1)}, bf16[2,256,128]{2,1,0:T(8,128)(2,1)S(1)}, u32[]{:S(2)}, u32[]{:S(2)}) collective-permute-start(bf16[2,256,128]{2,1,0:T(8,128)(2,1)S(1)} %get-tuple-element.196.refs_0_), channel_id=1, source_target_pairs={{0,8},{1,9},{2,10},{3,11},{4,12},{5,13},{6,14},{7,15},{8,0},{9,1},... | collective-permute-start | bytes 393224 | tf_op jit(solution)/shard_map/ppermute | solution.py:68
  307.7 28.4 %collective-permute-start.30 = (bf16[8,128,1024]{2,1,0:T(8,128)(2,1)S(1)}, bf16[8,128,1024]{2,1,0:T(8,128)(2,1)}, u32[]{:S(2)}, u32[]{:S(2)}) collective-permute-start(bf16[8,128,1024]{2,1,0:T(8,128)(2,1)S(1)} %pad_maximum_fusion.5.refs_0_), channel_id=1, source_target_pairs={{0,2},{1,3},{2,0},{3,1},{4,5},{5,4},{6,7},{7,6},{8,10},{9,11},{10,... | collective-permute-start | bytes 6291464 | tf_op jit(solution)/shard_map/ppermute | solution.py:68
  309.0 46.5 %collective-permute-start.31 = (bf16[8,128,1024]{2,1,0:T(8,128)(2,1)S(1)}, bf16[8,128,1024]{2,1,0:T(8,128)(2,1)}, u32[]{:S(2)}, u32[]{:S(2)}) collective-permute-start(bf16[8,128,1024]{2,1,0:T(8,128)(2,1)S(1)} %pad_maximum_fusion.5.refs_0_), channel_id=1, source_target_pairs={{0,4},{1,5},{2,6},{3,7},{4,0},{5,1},{6,2},{7,3},{8,12},{9,13},{10,... | collective-permute-start | bytes 6291464 | tf_op jit(solution)/shard_map/ppermute | solution.py:68
  354.4 77.8 %collective-permute-start.44 = (bf16[256,1536]{1,0:T(8,128)(2,1)}, bf16[256,1536]{1,0:T(8,128)(2,1)}, u32[]{:S(2)}, u32[]{:S(2)}) collective-permute-start(bf16[256,1536]{1,0:T(8,128)(2,1)} %pad_maximum_fusion.20), channel_id=1, source_target_pairs={{0,4},{1,5},{2,6},{3,7},{4,0},{5,1},{6,2},{7,3},{8,12},{9,13},{10,... | collective-permute-start | bytes 2359304 | tf_op jit(solution)/shard_map/ppermute | solution.py:68
  408.4 34.1 %collective-permute-start.40 = (bf16[1024,1024]{1,0:T(8,128)(2,1)}, bf16[1024,1024]{1,0:T(8,128)(2,1)}, u32[]{:S(2)}, u32[]{:S(2)}) collective-permute-start(bf16[1024,1024]{1,0:T(8,128)(2,1)} %convolution_convert_fusion.11.refs_0_.refs_4_), channel_id=1, source_target_pairs={{0,2},{1,3},{2,0},{3,1},{4,5},{5,4},{6,7},{7,6},{8,10},{9,11},{10,... | collective-permute-start | bytes 6291464 | tf_op jit(solution)/shard_map/ppermute | solution.py:68
  416.2 31.9 %collective-permute-start.45 = (bf16[256,4096]{1,0:T(8,128)(2,1)}, bf16[256,4096]{1,0:T(8,128)(2,1)}, u32[]{:S(2)}, u32[]{:S(2)}) collective-permute-start(bf16[256,4096]{1,0:T(8,128)(2,1)} %pad_maximum_fusion.7), channel_id=1, source_target_pairs={{0,4},{1,5},{2,6},{3,7},{4,0},{5,1},{6,2},{7,3},{8,12},{9,13},{10,... | collective-permute-start | bytes 6291464 | tf_op jit(solution)/shard_map/ppermute | solution.py:68
  440.0 55.0 %collective-permute-start.48 = (bf16[256,4096]{1,0:T(8,128)(2,1)S(1)}, bf16[256,4096]{1,0:T(8,128)(2,1)}, u32[]{:S(2)}, u32[]{:S(2)}) collective-permute-start(bf16[256,4096]{1,0:T(8,128)(2,1)S(1)} %convolution_convert_fusion.2.refs_5_), channel_id=1, source_target_pairs={{0,2},{1,3},{2,0},{3,1},{4,5},{5,4},{6,7},{7,6},{8,10},{9,11},{10,... | collective-permute-start | bytes 6291464 | tf_op jit(solution)/shard_map/ppermute | solution.py:68
  447.0 53.6 %collective-permute-start.47 = (bf16[512,1024]{1,0:T(8,128)(2,1)}, bf16[512,1024]{1,0:T(8,128)(2,1)}, u32[]{:S(2)}, u32[]{:S(2)}) collective-permute-start(bf16[512,1024]{1,0:T(8,128)(2,1)} %get-tuple-element.115.refs_13_), channel_id=1, source_target_pairs={{0,1},{1,0},{2,3},{3,2},{4,6},{5,7},{6,4},{7,5},{8,9},{9,8},{10,11... | collective-permute-start | bytes 3145736 | tf_op jit(solution)/shard_map/ppermute | solution.py:68
  486.1 37.0 %collective-permute-start.49 = (bf16[256,4096]{1,0:T(8,128)(2,1)}, bf16[256,4096]{1,0:T(8,128)(2,1)}, u32[]{:S(2)}, u32[]{:S(2)}) collective-permute-start(bf16[256,4096]{1,0:T(8,128)(2,1)} %pad_maximum_fusion.9.refs_14_), channel_id=1, source_target_pairs={{0,2},{1,3},{2,0},{3,1},{4,5},{5,4},{6,7},{7,6},{8,10},{9,11},{10,... | collective-permute-start | bytes 6291464 | tf_op jit(solution)/shard_map/ppermute | solution.py:68
  490.9 38.8 %collective-permute-start.50 = (bf16[2,256,384]{2,1,0:T(8,128)(2,1)}, bf16[2,256,384]{2,1,0:T(8,128)(2,1)}, u32[]{:S(2)}, u32[]{:S(2)}) collective-permute-start(bf16[2,256,384]{2,1,0:T(8,128)(2,1)} %get-tuple-element.151.refs_0_), channel_id=1, source_target_pairs={{0,8},{1,9},{2,10},{3,11},{4,12},{5,13},{6,14},{7,15},{8,0},{9,1},... | collective-permute-start | bytes 1179656 | tf_op jit(solution)/shard_map/ppermute | solution.py:68
  491.7 38.0 %collective-permute-start.51 = (bf16[2,256,384]{2,1,0:T(8,128)(2,1)}, bf16[2,256,384]{2,1,0:T(8,128)(2,1)}, u32[]{:S(2)}, u32[]{:S(2)}) collective-permute-start(bf16[2,256,384]{2,1,0:T(8,128)(2,1)} %get-tuple-element.152.refs_1_), channel_id=1, source_target_pairs={{0,16},{1,17},{2,18},{3,19},{4,20},{5,21},{6,22},{7,23},{8,24},{9,... | collective-permute-start | bytes 1179656 | tf_op jit(solution)/shard_map/ppermute | solution.py:68
  495.0 34.8 %collective-permute-start.52 = (bf16[2,256,384]{2,1,0:T(8,128)(2,1)}, bf16[2,256,384]{2,1,0:T(8,128)(2,1)S(1)}, u32[]{:S(2)}, u32[]{:S(2)}) collective-permute-start(bf16[2,256,384]{2,1,0:T(8,128)(2,1)} %get-tuple-element.153.refs_2_), channel_id=1, source_target_pairs={{0,24},{1,25},{2,26},{3,27},{4,28},{5,29},{6,30},{7,31},{8,16},{9,... | collective-permute-start | bytes 1179656 | tf_op jit(solution)/shard_map/ppermute | solution.py:68
  500.6 42.5 %collective-permute-start.56 = (bf16[128,4096]{1,0:T(8,128)(2,1)}, bf16[128,4096]{1,0:T(8,128)(2,1)}, u32[]{:S(2)}, u32[]{:S(2)}) collective-permute-start(bf16[128,4096]{1,0:T(8,128)(2,1)} %get-tuple-element.113.refs_1_), channel_id=1, source_target_pairs={{0,1},{1,0},{2,3},{3,2},{4,6},{5,7},{6,4},{7,5},{8,9},{9,8},{10,11... | collective-permute-start | bytes 3145736 | tf_op jit(solution)/shard_map/ppermute | solution.py:68
  527.0 54.4 %collective-permute-start.58 = (bf16[128,4096]{1,0:T(8,128)(2,1)}, bf16[128,4096]{1,0:T(8,128)(2,1)}, u32[]{:S(2)}, u32[]{:S(2)}) collective-permute-start(bf16[128,4096]{1,0:T(8,128)(2,1)} %get-tuple-element.111.refs_2_), channel_id=1, source_target_pairs={{0,1},{1,0},{2,3},{3,2},{4,6},{5,7},{6,4},{7,5},{8,9},{9,8},{10,11... | collective-permute-start | bytes 3145736 | tf_op jit(solution)/shard_map/ppermute | solution.py:68
  546.1 29.1 %collective-permute-start.57 = (bf16[64,4096]{1,0:T(8,128)(2,1)}, bf16[64,4096]{1,0:T(8,128)(2,1)}, u32[]{:S(2)}, u32[]{:S(2)}) collective-permute-start(bf16[64,4096]{1,0:T(8,128)(2,1)} %get-tuple-element.137), channel_id=1, source_target_pairs={{0,8},{1,9},{2,10},{3,11},{4,12},{5,13},{6,14},{7,15},{8,0},{9,1},... | collective-permute-start | bytes 1572872 | tf_op jit(solution)/shard_map/ppermute | solution.py:68
  548.6 29.0 %collective-permute-start.55 = (bf16[256,1024]{1,0:T(8,128)(2,1)}, bf16[256,1024]{1,0:T(8,128)(2,1)}, u32[]{:S(2)}, u32[]{:S(2)}) collective-permute-start(bf16[256,1024]{1,0:T(8,128)(2,1)} %broadcast_select_fusion.15), channel_id=1, source_target_pairs={{0,8},{1,9},{2,10},{3,11},{4,12},{5,13},{6,14},{7,15},{8,0},{9,1},... | collective-permute-start | bytes 1572872 | tf_op jit(solution)/shard_map/ppermute | solution.py:68
  566.5 28.4 %collective-permute-start.69 = (bf16[256,3072]{1,0:T(8,128)(2,1)}, bf16[256,3072]{1,0:T(8,128)(2,1)S(1)}, u32[]{:S(2)}, u32[]{:S(2)}) collective-permute-start(bf16[256,3072]{1,0:T(8,128)(2,1)} %convolution_convert_fusion.6.refs_0_), channel_id=1, source_target_pairs={{0,2},{1,3},{2,0},{3,1},{4,5},{5,4},{6,7},{7,6},{8,10},{9,11},{10,... | collective-permute-start | bytes 4718600 | tf_op jit(solution)/shard_map/ppermute | solution.py:68
  575.3 22.8 %collective-permute-start.62 = (bf16[256,4096]{1,0:T(8,128)(2,1)S(1)}, bf16[256,4096]{1,0:T(8,128)(2,1)S(1)}, u32[]{:S(2)}, u32[]{:S(2)}) collective-permute-start(bf16[256,4096]{1,0:T(8,128)(2,1)S(1)} %fusion.1), channel_id=1, source_target_pairs={{0,4},{1,5},{2,6},{3,7},{4,0},{5,1},{6,2},{7,3},{8,12},{9,13},{10,... | collective-permute-start | bytes 6291464 | tf_op jit(solution)/shard_map/ppermute | solution.py:68
  577.5 30.0 %collective-permute-start.81 = (bf16[32,4096]{1,0:T(8,128)(2,1)}, bf16[32,4096]{1,0:T(8,128)(2,1)}, u32[]{:S(2)}, u32[]{:S(2)}) collective-permute-start(bf16[32,4096]{1,0:T(8,128)(2,1)} %add_convert_fusion.34.refs_1_), channel_id=1, source_target_pairs={{0,16},{1,17},{2,18},{3,19},{4,20},{5,21},{6,22},{7,23},{8,24},{9,... | collective-permute-start | bytes 786440 | tf_op jit(solution)/shard_map/ppermute | solution.py:68
  582.1 37.1 %collective-permute-start.80 = (bf16[128,1024]{1,0:T(8,128)(2,1)S(1)}, bf16[128,1024]{1,0:T(8,128)(2,1)}, u32[]{:S(2)}, u32[]{:S(2)}) collective-permute-start(bf16[128,1024]{1,0:T(8,128)(2,1)S(1)} %add_convert_fusion.35.refs_0_), channel_id=1, source_target_pairs={{0,16},{1,17},{2,18},{3,19},{4,20},{5,21},{6,22},{7,23},{8,24},{9,... | collective-permute-start | bytes 786440 | tf_op jit(solution)/shard_map/ppermute | solution.py:68
  586.0 40.8 %collective-permute-start.78 = (bf16[64,4096]{1,0:T(8,128)(2,1)}, bf16[64,4096]{1,0:T(8,128)(2,1)}, u32[]{:S(2)}, u32[]{:S(2)}) collective-permute-start(bf16[64,4096]{1,0:T(8,128)(2,1)} %get-tuple-element.131.refs_2_), channel_id=1, source_target_pairs={{0,8},{1,9},{2,10},{3,11},{4,12},{5,13},{6,14},{7,15},{8,0},{9,1},... | collective-permute-start | bytes 1572872 | tf_op jit(solution)/shard_map/ppermute | solution.py:68
  594.9 47.4 %collective-permute-start.71 = (bf16[512,1024]{1,0:T(8,128)(2,1)}, bf16[512,1024]{1,0:T(8,128)(2,1)}, u32[]{:S(2)}, u32[]{:S(2)}) collective-permute-start(bf16[512,1024]{1,0:T(8,128)(2,1)} %convolution_convert_fusion.12.refs_4_), channel_id=1, source_target_pairs={{0,2},{1,3},{2,0},{3,1},{4,5},{5,4},{6,7},{7,6},{8,10},{9,11},{10,... | collective-permute-start | bytes 3145736 | tf_op jit(solution)/shard_map/ppermute | solution.py:68
  598.1 45.0 %collective-permute-start.72 = (bf16[512,1024]{1,0:T(8,128)(2,1)}, bf16[512,1024]{1,0:T(8,128)(2,1)}, u32[]{:S(2)}, u32[]{:S(2)}) collective-permute-start(bf16[512,1024]{1,0:T(8,128)(2,1)} %convolution_convert_fusion.13.refs_3_), channel_id=1, source_target_pairs={{0,2},{1,3},{2,0},{3,1},{4,5},{5,4},{6,7},{7,6},{8,10},{9,11},{10,... | collective-permute-start | bytes 3145736 | tf_op jit(solution)/shard_map/ppermute | solution.py:68
  607.5 31.5 %collective-permute-start.70 = (bf16[128,3072]{1,0:T(8,128)(2,1)}, bf16[128,3072]{1,0:T(8,128)(2,1)S(1)}, u32[]{:S(2)}, u32[]{:S(2)}) collective-permute-start(bf16[128,3072]{1,0:T(8,128)(2,1)} %get-tuple-element.117), channel_id=1, source_target_pairs={{0,1},{1,0},{2,3},{3,2},{4,6},{5,7},{6,4},{7,5},{8,9},{9,8},{10,11... | collective-permute-start | bytes 2359304 | tf_op jit(solution)/shard_map/ppermute | solution.py:68
  619.2 29.6 %collective-permute-start.64 = (bf16[128,4096]{1,0:T(8,128)(2,1)S(1)}, bf16[128,4096]{1,0:T(8,128)(2,1)}, u32[]{:S(2)}, u32[]{:S(2)}) collective-permute-start(bf16[128,4096]{1,0:T(8,128)(2,1)S(1)} %copy-done.28), channel_id=1, source_target_pairs={{0,2},{1,3},{2,0},{3,1},{4,5},{5,4},{6,7},{7,6},{8,10},{9,11},{10,... | collective-permute-start | bytes 3145736 | tf_op jit(solution)/shard_map/ppermute | solution.py:68
  636.7 26.8 %collective-permute-start.63 = (bf16[128,4096]{1,0:T(8,128)(2,1)S(1)}, bf16[128,4096]{1,0:T(8,128)(2,1)}, u32[]{:S(2)}, u32[]{:S(2)}) collective-permute-start(bf16[128,4096]{1,0:T(8,128)(2,1)S(1)} %copy-done.27), channel_id=1, source_target_pairs={{0,2},{1,3},{2,0},{3,1},{4,5},{5,4},{6,7},{7,6},{8,10},{9,11},{10,... | collective-permute-start | bytes 3145736 | tf_op jit(solution)/shard_map/ppermute | solution.py:68
  676.6 27.8 %collective-permute-start.67 = (bf16[64,4096]{1,0:T(8,128)(2,1)}, bf16[64,4096]{1,0:T(8,128)(2,1)S(1)}, u32[]{:S(2)}, u32[]{:S(2)}) collective-permute-start(bf16[64,4096]{1,0:T(8,128)(2,1)} %get-tuple-element.168.refs_0_), channel_id=1, source_target_pairs={{0,8},{1,9},{2,10},{3,11},{4,12},{5,13},{6,14},{7,15},{8,0},{9,1},... | collective-permute-start | bytes 1572872 | tf_op jit(solution)/shard_map/ppermute | solution.py:68
  679.4 27.0 %collective-permute-start.85 = (f32[37,64]{1,0:T(8,128)S(1)}, f32[37,64]{1,0:T(8,128)S(1)}, u32[]{:S(2)}, u32[]{:S(2)}) collective-permute-start(f32[37,64]{1,0:T(8,128)S(1)} %slice.933), channel_id=1, source_target_pairs={{0,8},{1,9},{2,10},{3,11},{4,12},{5,13},{6,14},{7,15},{8,0},{9,1},... | collective-permute-start | bytes 28424 | tf_op jit(solution)/shard_map/ppermute | solution.py:68
  681.9 27.5 %collective-permute-start.77 = (bf16[32,3072]{1,0:T(8,128)(2,1)}, bf16[32,3072]{1,0:T(8,128)(2,1)}, u32[]{:S(2)}, u32[]{:S(2)}) collective-permute-start(bf16[32,3072]{1,0:T(8,128)(2,1)} %add_convert_fusion.36), channel_id=1, source_target_pairs={{0,16},{1,17},{2,18},{3,19},{4,20},{5,21},{6,22},{7,23},{8,24},{9,... | collective-permute-start | bytes 589832 | tf_op jit(solution)/shard_map/ppermute | solution.py:68
  686.3 24.8 %collective-permute-start.75 = (bf16[128,1024]{1,0:T(8,128)(2,1)}, bf16[128,1024]{1,0:T(8,128)(2,1)S(1)}, u32[]{:S(2)}, u32[]{:S(2)}) collective-permute-start(bf16[128,1024]{1,0:T(8,128)(2,1)} %add_convert_fusion.30), channel_id=1, source_target_pairs={{0,16},{1,17},{2,18},{3,19},{4,20},{5,21},{6,22},{7,23},{8,24},{9,... | collective-permute-start | bytes 786440 | tf_op jit(solution)/shard_map/ppermute | solution.py:68
  (206 other events, 1910.4 us)
Sparse Core Ops, SparseCore 0:
  10.9 91.2 all-gather.3
  105.1 81.8 all-gather.5
  189.9 107.2 all-gather.7

commit v3 on v2

--- a/solution.py
+++ b/solution.py
@@ -451,7 +451,7 @@
 
 def attend_back(query, keys, values, mixed, grads, totals, ids, cosine, sine, tokens=()):
     rows, length, size = query.shape
-    tile = 256
+    tile = 1024 if length <= 1024 else 256
     heads = size // HEAD_DIM
     whole = pl.BlockSpec((1, length, size), lambda r, t: (r, 0, 0))
     part = pl.BlockSpec((1, tile, size), lambda r, t: (r, t, 0))

time: 739 us -> 734 us (level)
  transfers between devices with their start and end apart: 90 -> 90, of which waited for: 24 -> 23; matrix products, arithmetic and copies ran while one was open for 41% -> 42% of each run, Pallas kernels for 11% -> 11%
where the time goes in v3:
time: 734 us; the launch traced here: 723 us
  waiting for transfers between devices  175 us (24%)
  other arithmetic  137 us (19%)
  matrix products  125 us (17%)
  starting transfers between devices  115 us (16%)
  Pallas kernels  76.7 us (10%)
  local copies, waits for them, and re-layouts  55.2 us (8%)
  between operations  37.1 us (5%)
    ppermute x83, waiting for transfers between devices, send(): return lax.ppermute(x, BOTH, pairs)  175 us
    ppermute x83, starting transfers between devices, send(): return lax.ppermute(x, BOTH, pairs)  108 us
    dot_general x12, matrix products, dot_back(): lax.dot_general(left, right, (((1,), (1,)), ((), ())), preferred_element_...  46.1 us
    dot_general x18, matrix products, dot(): return jnp.dot(left, right, preferred_element_type=F32)  43.9 us
    select_n x32, other arithmetic, after(): jnp.where(flag, x, jnp.zeros((), x.dtype))  42.4 us
    dot_general x18, matrix products, dot_over_frames(): lax.dot_general(left, right, (((0,), (0,)), ((), ())), preferred_element_...  33.2 us
    convert_element_type x12, other arithmetic, grad_lane(): kept = (kept[:half].astype(F32) + stay.astype(F32)).astype(BF16)  23 us
    pallas_call x1, Pallas kernels, attend_back(): pl.pallas_call(lambda *refs: attend_back_kernel(*refs[:13], *refs[13 + le...  18.8 us
  transfers between devices with their start and end apart: 90, of which 23 were waited for; matrix products, arithmetic and copies ran while one was open for 42% of the time, Pallas kernels for 11%

profile of v3, /device:TPU:0, one launch (start us, length us, event | category | flops | bytes accessed | tf_op | source)
XLA Modules:
  0.0 722.6 jit_solution(10853726695105364420)
XLA Ops:
  10.4 3.0 collective-permute-start
  24.6 5.7 collective-permute-done.3
  32.3 5.3 collective-permute-start.4
  37.7 10.0 %collective-permute-done.4 = bf16[37,512]{1,0:T(8,128)(2,1)S(1)} collective-permute-done((bf16[37,512]{1,0:T(8,128)(2,1)}, bf16[37,512]{1,0:T(8,128)(2,1)S(1)}, u32[]{:S(2)}, u32[]{:S(2)}) %collective-permute-start.4) | collective-permute-done | bytes 37920 | tf_op jit(solution)/shard_map/ppermute | solution.py:68
  53.0 5.8 collective-permute-start.11
  58.8 7.2 collective-permute-done.7
  71.7 4.5 collective-permute-start.12
  77.5 23.0 %collective-permute-done.12 = bf16[2,128,1024]{2,1,0:T(8,128)(2,1)S(1)} collective-permute-done((bf16[2,128,1024]{2,1,0:T(8,128)(2,1)S(1)}, bf16[2,128,1024]{2,1,0:T(8,128)(2,1)S(1)}, u32[]{:S(2)}, u32[]{:S(2)}) %collective-permute-start.12) | collective-permute-done | bytes 524320 | tf_op jit(solution)/shard_map/ppermute | solution.py:68
  106.9 12.5 %collective-permute-done.13 = bf16[4,128,1024]{2,1,0:T(8,128)(2,1)} collective-permute-done((bf16[4,128,1024]{2,1,0:T(8,128)(2,1)}, bf16[4,128,1024]{2,1,0:T(8,128)(2,1)}, u32[]{:S(2)}, u32[]{:S(2)}) %collective-permute-start.13) | collective-permute-done | bytes 1048608 | tf_op jit(solution)/shard_map/ppermute | solution.py:68
  119.4 3.5 broadcast_select_fusion.6
  124.9 5.6 fusion.85
  140.0 13.0 %collective-permute-done.14.refs_1_ = bf16[8,128,1024]{2,1,0:T(8,128)(2,1)} collective-permute-done((bf16[8,128,1024]{2,1,0:T(8,128)(2,1)}, bf16[8,128,1024]{2,1,0:T(8,128)(2,1)}, u32[]{:S(2)}, u32[]{:S(2)}) %collective-permute-start.14) | collective-permute-done | bytes 2097184 | tf_op jit(solution)/shard_map/ppermute | solution.py:68
  156.0 5.3 assemble.3
  161.3 4.6 multiply_convert_fusion.1
  166.2 3.0 assemble.4
  172.7 4.7 fusion.213.refs_0_
  190.0 3.4 collective-permute-start.27
  205.3 5.7 collective-permute-done.27
  214.0 9.3 %collective-permute-done.18 = bf16[2,256,384]{2,1,0:T(8,128)(2,1)} collective-permute-done((bf16[2,256,384]{2,1,0:T(8,128)(2,1)S(1)}, bf16[2,256,384]{2,1,0:T(8,128)(2,1)}, u32[]{:S(2)}, u32[]{:S(2)}) %collective-permute-start.18) | collective-permute-done | bytes 393248 | tf_op jit(solution)/shard_map/ppermute | solution.py:68
  223.3 21.5 %collective-permute-done.19 = bf16[2,256,384]{2,1,0:T(8,128)(2,1)} collective-permute-done((bf16[2,256,384]{2,1,0:T(8,128)(2,1)S(1)}, bf16[2,256,384]{2,1,0:T(8,128)(2,1)}, u32[]{:S(2)}, u32[]{:S(2)}) %collective-permute-start.19) | collective-permute-done | bytes 393248 | tf_op jit(solution)/shard_map/ppermute | solution.py:68
  249.4 13.4 %attend.1 = (bf16[2,1024,128]{2,1,0:T(8,128)(2,1)}, f32[2,1024,2]{2,1,0:T(8,128)}) custom-call(bf16[2,1024,128]{2,1,0:T(8,128)(2,1)} %bitcast.341, bf16[2,1024,128]{2,1,0:T(8,128)(2,1)} %bitcast.343, bf16[2,1024,128]{2,1,0:T(8,128)(2,1)} %bitcast.345, s32[2,1024,1]{2,1,0:T(8,128)} %copy.90.refs_3_.refs_7_, s32[2,1,1024]{2,1,0:T(1,128)} %bitcast.398), custom_call_target="tpu_custom_call" | custom-call | tf_op jit(solution)/shard_map/attend/pallas_call | solution.py:431
  269.2 12.5 %collective-permute-start.22 = (bf16[2,256,128]{2,1,0:T(8,128)(2,1)S(1)}, bf16[2,256,128]{2,1,0:T(8,128)(2,1)S(1)}, u32[]{:S(2)}, u32[]{:S(2)}) collective-permute-start(bf16[2,256,128]{2,1,0:T(8,128)(2,1)S(1)} %get-tuple-element.196.refs_0_), channel_id=1, source_target_pairs={{0,8},{1,9},{2,10},{3,11},{4,12},{5,13},{6,14},{7,15},{8,0},{9,1},... | collective-permute-start | bytes 393224 | tf_op jit(solution)/shard_map/ppermute | solution.py:68
  285.0 2.8 pad_maximum_fusion.11
  293.7 7.6 %collective-permute-done.24 = bf16[2,256,128]{2,1,0:T(8,128)(2,1)S(1)} collective-permute-done((bf16[2,256,128]{2,1,0:T(8,128)(2,1)S(1)}, bf16[2,256,128]{2,1,0:T(8,128)(2,1)S(1)}, u32[]{:S(2)}, u32[]{:S(2)}) %collective-permute-start.24) | collective-permute-done | bytes 131104 | tf_op jit(solution)/shard_map/ppermute | solution.py:68
  312.1 3.6 fusion.20
  325.7 4.9 depthwise.1
  336.1 3.1 broadcast_select_fusion.5.refs_1_
  340.9 7.8 %multiply_convert_fusion = (bf16[256,4096]{1,0:T(8,128)(2,1)S(1)}, f32[256,4096]{1,0:T(8,128)}) fusion(bf16[1024,4096]{1,0:T(8,128)(2,1)} %all-gather.8.cloned.1.call-done, f32[256,1024]{1,0:T(8,128)S(1)} %get-tuple-element.231, f32[1024]{0:T(1024)S(1)} %bitcast.417, f32[256]{0:T(256)S(1)} %add_rsqrt_fusion.1, f32[256]{0:T(256)S(1)} %broadcast_multiply_fusion.12), kind=kOutput, calls=%fused_computation.21 | convolution fusion | flops 2153775104 | bytes 15734784 | tf_op jit(solution)/shard_map/dot_general | solution.py:335
  355.5 4.3 assemble.5
  365.0 4.2 fusion
  369.7 8.1 %multiply_reduce_fusion = (f32[1024]{0:T(1024)}, f32[256]{0:T(256)S(1)}, f32[256]{0:T(256)S(1)}, f32[256,1024]{1,0:T(8,128)}) fusion(f32[256,1024]{1,0:T(8,128)S(1)} %copy-done.25, f32[256]{0:T(256)S(1)} %add_rsqrt_fusion.1, f32[256]{0:T(256)S(1)} %broadcast_multiply_fusion.12, f32[1024]{0:T(1024)S(1)} %bitcast.419, bf16[256,4096]{1,0:T(8,128)(2,1)} %fusion, ...), kind=kOutput, calls=%fused_computation.209 | convolution fusion | flops 2149579264 | bytes 12595200 | tf_op jit(solution)/shard_map/dot_general | solution.py:339
  385.0 3.6 multiply_reduce_fusion.1
  388.8 2.8 pad_maximum_fusion
  393.6 8.4 %depthwise_back.1 = (f32[2,31,1024]{2,1,0:T(8,128)S(1)}, f32[2,160,1024]{2,1,0:T(8,128)S(1)}) custom-call(bf16[2,160,1024]{2,1,0:T(8,128)(2,1)S(1)} %copy-done.6, f32[2,160,1]{2,1,0:T(8,128)S(1)} %copy-done.7, f32[2,128,1024]{2,1,0:T(8,128)S(1)} %bitcast.334, f32[31,1024]{1,0:T(8,128)S(1)} %slice.811.refs_2_.refs_3_, ...), custom_call_target="tpu_custom_call" | custom-call | tf_op jit(solution)/shard_map/depthwise_back/pallas_call | solution.py:565
  417.4 3.1 fusion.81
  421.5 4.8 convolution_convert_fusion.1
  434.5 5.4 collective-permute-done.42
  456.8 18.8 %attend_back.1 = (bf16[2,1024,128]{2,1,0:T(8,128)(2,1)}, bf16[2,1024,128]{2,1,0:T(8,128)(2,1)}, bf16[2,1024,128]{2,1,0:T(8,128)(2,1)}) custom-call(bf16[2,1024,128]{2,1,0:T(8,128)(2,1)} %bitcast.342, bf16[2,1024,128]{2,1,0:T(8,128)(2,1)} %bitcast.344, bf16[2,1024,128]{2,1,0:T(8,128)(2,1)} %bitcast.346, bf16[2,1024,128]{2,1,0:T(8,128)(2,1)} %get-tuple-element.41.refs_3_, ...), custom_call_target="tpu_custom_call" | custom-call | tf_op jit(solution)/shard_map/attend_back/pallas_call | solution.py:460
  498.9 19.4 %collective-permute-done.49 = bf16[256,4096]{1,0:T(8,128)(2,1)} collective-permute-done((bf16[256,4096]{1,0:T(8,128)(2,1)}, bf16[256,4096]{1,0:T(8,128)(2,1)}, u32[]{:S(2)}, u32[]{:S(2)}) %collective-permute-start.49) | collective-permute-done | bytes 2097184 | tf_op jit(solution)/shard_map/ppermute | solution.py:68
  544.6 6.9 multiply_reduce_fusion.3
  557.2 3.4 fusion.121
  562.3 7.5 %fusion.1 = bf16[256,4096]{1,0:T(8,128)(2,1)S(1)} fusion(bf16[256,1024]{1,0:T(8,128)(2,1)} %get-tuple-element.100.refs_0_, bf16[4096,1024]{1,0:T(8,128)(2,1)} %copy-done.4, f32[256,4096]{1,0:T(8,128)} %get-tuple-element.225), kind=kOutput, calls=%fused_computation.5 | convolution fusion | flops 2156920832 | bytes 15204352 | tf_op jit(solution)/shard_map/dot_general | solution.py:339
  605.7 8.5 %multiply_reduce_fusion.4 = (f32[1024]{0:T(1024)}, f32[256]{0:T(256)}, f32[256]{0:T(256)}, f32[256,1024]{1,0:T(8,128)}) fusion(bf16[2,128,1024]{2,1,0:T(8,128)(2,1)S(1)} %copy-done.42, f32[256]{0:T(256)S(1)} %copy-done.144, f32[256]{0:T(256)S(1)} %copy-done.142, f32[1024]{0:T(1024)S(1)} %bitcast.406, bf16[256,4096]{1,0:T(8,128)(2,1)} %broadcast_select_fusion.refs_0_, ...), kind=kOutput, calls=%fused_computation.213 | convolution fusion | flops 2149841408 | bytes 12070912 | tf_op jit(solution)/shard_map/dot_general | solution.py:339
  623.8 5.0 convolution_convert_fusion
  638.0 4.3 add_convert_fusion.1
  665.0 4.0 collective-permute-done.66
  684.0 15.3 %collective-permute-done.67 = bf16[64,4096]{1,0:T(8,128)(2,1)S(1)} collective-permute-done((bf16[64,4096]{1,0:T(8,128)(2,1)}, bf16[64,4096]{1,0:T(8,128)(2,1)S(1)}, u32[]{:S(2)}, u32[]{:S(2)}) %collective-permute-start.67) | collective-permute-done | bytes 524320 | tf_op jit(solution)/shard_map/ppermute | solution.py:68
  707.0 6.5 collective-permute-done.86
  (787 shorter events, 328.8 us)
Async XLA Ops:
  7.2 165.5 %all-gather.4.cloned.1.call-start = ((), (), s32[]{:S(2)}) async-start(), calls=%async_computation | async-start | bytes 6488064 | tf_op jit(solution)/shard_map/all_gather | solution.py:695
  7.9 301.3 %all-gather.6.cloned.1.call-start = ((), (), s32[]{:S(2)}) async-start(), calls=%async_computation.1 | async-start | bytes 8650752 | tf_op jit(solution)/shard_map/all_gather | solution.py:697
  9.7 331.2 %all-gather.8.cloned.1.call-start = ((), (), s32[]{:S(2)}) async-start(), calls=%async_computation.2 | async-start | bytes 8650752 | tf_op jit(solution)/shard_map/all_gather | solution.py:702
  67.7 38.1 %collective-permute-start.8 = (bf16[8,128,1024]{2,1,0:T(8,128)(2,1)S(1)}, bf16[8,128,1024]{2,1,0:T(8,128)(2,1)}, u32[]{:S(2)}, u32[]{:S(2)}) collective-permute-start(bf16[8,128,1024]{2,1,0:T(8,128)(2,1)S(1)} %pad_maximum_fusion.3.refs_0_), channel_id=1, source_target_pairs={{0,2},{1,3},{2,0},{3,1},{4,5},{5,4},{6,7},{7,6},{8,10},{9,11},{10,... | collective-permute-start | bytes 6291464 | tf_op jit(solution)/shard_map/ppermute | solution.py:68
  71.7 28.7 %collective-permute-start.12 = (bf16[2,128,1024]{2,1,0:T(8,128)(2,1)S(1)}, bf16[2,128,1024]{2,1,0:T(8,128)(2,1)S(1)}, u32[]{:S(2)}, u32[]{:S(2)}) collective-permute-start(bf16[2,128,1024]{2,1,0:T(8,128)(2,1)S(1)} %maximum_select_fusion.4), channel_id=1, source_target_pairs={{0,8},{1,9},{2,10},{3,11},{4,12},{5,13},{6,14},{7,15},{8,0},{9,1},... | collective-permute-start | bytes 1572872 | tf_op jit(solution)/shard_map/ppermute | solution.py:68
  123.0 30.1 %collective-permute-start.14 = (bf16[8,128,1024]{2,1,0:T(8,128)(2,1)}, bf16[8,128,1024]{2,1,0:T(8,128)(2,1)}, u32[]{:S(2)}, u32[]{:S(2)}) collective-permute-start(bf16[8,128,1024]{2,1,0:T(8,128)(2,1)} %get-tuple-element.144.refs_0_), channel_id=1, source_target_pairs={{0,2},{1,3},{2,0},{3,1},{4,5},{5,4},{6,7},{7,6},{8,10},{9,11},{10,... | collective-permute-start | bytes 6291464 | tf_op jit(solution)/shard_map/ppermute | solution.py:68
  130.5 25.5 %collective-permute-start.9 = (bf16[8,128,1024]{2,1,0:T(8,128)(2,1)S(1)}, bf16[8,128,1024]{2,1,0:T(8,128)(2,1)}, u32[]{:S(2)}, u32[]{:S(2)}) collective-permute-start(bf16[8,128,1024]{2,1,0:T(8,128)(2,1)S(1)} %copy-done.1), channel_id=1, source_target_pairs={{0,4},{1,5},{2,6},{3,7},{4,0},{5,1},{6,2},{7,3},{8,12},{9,13},{10,... | collective-permute-start | bytes 6291464 | tf_op jit(solution)/shard_map/ppermute | solution.py:68
  130.5 25.5 %collective-permute-start.10 = (bf16[8,128,1024]{2,1,0:T(8,128)(2,1)}, bf16[8,128,1024]{2,1,0:T(8,128)(2,1)}, u32[]{:S(2)}, u32[]{:S(2)}) collective-permute-start(bf16[8,128,1024]{2,1,0:T(8,128)(2,1)} %collective-permute-done.8.refs_1_), channel_id=1, source_target_pairs={{0,4},{1,5},{2,6},{3,7},{4,0},{5,1},{6,2},{7,3},{8,12},{9,13},{10,... | collective-permute-start | bytes 6291464 | tf_op jit(solution)/shard_map/ppermute | solution.py:68
  139.9 26.2 %collective-permute-start.15 = (bf16[8,128,1024]{2,1,0:T(8,128)(2,1)}, bf16[8,128,1024]{2,1,0:T(8,128)(2,1)S(1)}, u32[]{:S(2)}, u32[]{:S(2)}) collective-permute-start(bf16[8,128,1024]{2,1,0:T(8,128)(2,1)} %get-tuple-element.145.refs_0_), channel_id=1, source_target_pairs={{0,4},{1,5},{2,6},{3,7},{4,0},{5,1},{6,2},{7,3},{8,12},{9,13},{10,... | collective-permute-start | bytes 6291464 | tf_op jit(solution)/shard_map/ppermute | solution.py:68
  155.4 30.8 %collective-permute-start.61 = (bf16[256,512]{1,0:T(8,128)(2,1)}, bf16[256,512]{1,0:T(8,128)(2,1)}, u32[]{:S(2)}, u32[]{:S(2)}) collective-permute-start(bf16[256,512]{1,0:T(8,128)(2,1)} %get-tuple-element.177), channel_id=1, source_target_pairs={{0,4},{1,5},{2,6},{3,7},{4,0},{5,1},{6,2},{7,3},{8,12},{9,13},{10,... | collective-permute-start | bytes 786440 | tf_op jit(solution)/shard_map/ppermute | solution.py:68
  190.0 21.0 %collective-permute-start.27 = (bf16[1,128,1024]{2,1,0:T(8,128)(2,1)}, bf16[1,128,1024]{2,1,0:T(8,128)(2,1)}, u32[]{:S(2)}, u32[]{:S(2)}) collective-permute-start(bf16[1,128,1024]{2,1,0:T(8,128)(2,1)} %select_bitcast_fusion), channel_id=1, source_target_pairs={{0,16},{1,17},{2,18},{3,19},{4,20},{5,21},{6,22},{7,23},{8,24},{9,... | collective-permute-start | bytes 786440 | tf_op jit(solution)/shard_map/ppermute | solution.py:68
  195.4 88.2 %collective-permute-start.59 = (bf16[256,2048]{1,0:T(8,128)(2,1)}, bf16[256,2048]{1,0:T(8,128)(2,1)}, u32[]{:S(2)}, u32[]{:S(2)}) collective-permute-start(bf16[256,2048]{1,0:T(8,128)(2,1)} %get-tuple-element.62), channel_id=1, source_target_pairs={{0,4},{1,5},{2,6},{3,7},{4,0},{5,1},{6,2},{7,3},{8,12},{9,13},{10,... | collective-permute-start | bytes 3145736 | tf_op jit(solution)/shard_map/ppermute | solution.py:68
  198.8 24.5 %collective-permute-start.18 = (bf16[2,256,384]{2,1,0:T(8,128)(2,1)S(1)}, bf16[2,256,384]{2,1,0:T(8,128)(2,1)}, u32[]{:S(2)}, u32[]{:S(2)}) collective-permute-start(bf16[2,256,384]{2,1,0:T(8,128)(2,1)S(1)} %get-tuple-element.160.refs_0_), channel_id=1, source_target_pairs={{0,8},{1,9},{2,10},{3,11},{4,12},{5,13},{6,14},{7,15},{8,0},{9,1},... | collective-permute-start | bytes 1179656 | tf_op jit(solution)/shard_map/ppermute | solution.py:68
  200.3 44.6 %collective-permute-start.19 = (bf16[2,256,384]{2,1,0:T(8,128)(2,1)S(1)}, bf16[2,256,384]{2,1,0:T(8,128)(2,1)}, u32[]{:S(2)}, u32[]{:S(2)}) collective-permute-start(bf16[2,256,384]{2,1,0:T(8,128)(2,1)S(1)} %get-tuple-element.162.refs_1_), channel_id=1, source_target_pairs={{0,16},{1,17},{2,18},{3,19},{4,20},{5,21},{6,22},{7,23},{8,24},{9,... | collective-permute-start | bytes 1179656 | tf_op jit(solution)/shard_map/ppermute | solution.py:68
  200.9 44.0 %collective-permute-start.20 = (bf16[2,256,384]{2,1,0:T(8,128)(2,1)S(1)}, bf16[2,256,384]{2,1,0:T(8,128)(2,1)}, u32[]{:S(2)}, u32[]{:S(2)}) collective-permute-start(bf16[2,256,384]{2,1,0:T(8,128)(2,1)S(1)} %get-tuple-element.161.refs_2_), channel_id=1, source_target_pairs={{0,24},{1,25},{2,26},{3,27},{4,28},{5,29},{6,30},{7,31},{8,16},{9,... | collective-permute-start | bytes 1179656 | tf_op jit(solution)/shard_map/ppermute | solution.py:68
  211.0 76.8 %collective-permute-start.53 = (bf16[256,512]{1,0:T(8,128)(2,1)}, bf16[256,512]{1,0:T(8,128)(2,1)}, u32[]{:S(2)}, u32[]{:S(2)}) collective-permute-start(bf16[256,512]{1,0:T(8,128)(2,1)} %get-tuple-element.192), channel_id=1, source_target_pairs={{0,4},{1,5},{2,6},{3,7},{4,0},{5,1},{6,2},{7,3},{8,12},{9,13},{10,... | collective-permute-start | bytes 786440 | tf_op jit(solution)/shard_map/ppermute | solution.py:68
  223.3 41.4 %collective-permute-start.28 = (bf16[2,128,1024]{2,1,0:T(8,128)(2,1)}, bf16[2,128,1024]{2,1,0:T(8,128)(2,1)S(1)}, u32[]{:S(2)}, u32[]{:S(2)}) collective-permute-start(bf16[2,128,1024]{2,1,0:T(8,128)(2,1)} %pad_maximum_fusion.22), channel_id=1, source_target_pairs={{0,8},{1,9},{2,10},{3,11},{4,12},{5,13},{6,14},{7,15},{8,0},{9,1},... | collective-permute-start | bytes 1572872 | tf_op jit(solution)/shard_map/ppermute | solution.py:68
  266.1 40.1 %collective-permute-start.29 = (bf16[4,128,1024]{2,1,0:T(8,128)(2,1)S(1)}, bf16[4,128,1024]{2,1,0:T(8,128)(2,1)}, u32[]{:S(2)}, u32[]{:S(2)}) collective-permute-start(bf16[4,128,1024]{2,1,0:T(8,128)(2,1)S(1)} %maximum_select_fusion.2), channel_id=1, source_target_pairs={{0,1},{1,0},{2,3},{3,2},{4,6},{5,7},{6,4},{7,5},{8,9},{9,8},{10,11... | collective-permute-start | bytes 3145736 | tf_op jit(solution)/shard_map/ppermute | solution.py:68
  269.2 23.8 %collective-permute-start.22 = (bf16[2,256,128]{2,1,0:T(8,128)(2,1)S(1)}, bf16[2,256,128]{2,1,0:T(8,128)(2,1)S(1)}, u32[]{:S(2)}, u32[]{:S(2)}) collective-permute-start(bf16[2,256,128]{2,1,0:T(8,128)(2,1)S(1)} %get-tuple-element.196.refs_0_), channel_id=1, source_target_pairs={{0,8},{1,9},{2,10},{3,11},{4,12},{5,13},{6,14},{7,15},{8,0},{9,1},... | collective-permute-start | bytes 393224 | tf_op jit(solution)/shard_map/ppermute | solution.py:68
  307.8 28.2 %collective-permute-start.30 = (bf16[8,128,1024]{2,1,0:T(8,128)(2,1)S(1)}, bf16[8,128,1024]{2,1,0:T(8,128)(2,1)}, u32[]{:S(2)}, u32[]{:S(2)}) collective-permute-start(bf16[8,128,1024]{2,1,0:T(8,128)(2,1)S(1)} %pad_maximum_fusion.5.refs_0_), channel_id=1, source_target_pairs={{0,2},{1,3},{2,0},{3,1},{4,5},{5,4},{6,7},{7,6},{8,10},{9,11},{10,... | collective-permute-start | bytes 6291464 | tf_op jit(solution)/shard_map/ppermute | solution.py:68
  308.9 46.5 %collective-permute-start.31 = (bf16[8,128,1024]{2,1,0:T(8,128)(2,1)S(1)}, bf16[8,128,1024]{2,1,0:T(8,128)(2,1)}, u32[]{:S(2)}, u32[]{:S(2)}) collective-permute-start(bf16[8,128,1024]{2,1,0:T(8,128)(2,1)S(1)} %pad_maximum_fusion.5.refs_0_), channel_id=1, source_target_pairs={{0,4},{1,5},{2,6},{3,7},{4,0},{5,1},{6,2},{7,3},{8,12},{9,13},{10,... | collective-permute-start | bytes 6291464 | tf_op jit(solution)/shard_map/ppermute | solution.py:68
  354.4 77.8 %collective-permute-start.44 = (bf16[256,1536]{1,0:T(8,128)(2,1)}, bf16[256,1536]{1,0:T(8,128)(2,1)}, u32[]{:S(2)}, u32[]{:S(2)}) collective-permute-start(bf16[256,1536]{1,0:T(8,128)(2,1)} %pad_maximum_fusion.20), channel_id=1, source_target_pairs={{0,4},{1,5},{2,6},{3,7},{4,0},{5,1},{6,2},{7,3},{8,12},{9,13},{10,... | collective-permute-start | bytes 2359304 | tf_op jit(solution)/shard_map/ppermute | solution.py:68
  408.4 34.1 %collective-permute-start.40 = (bf16[1024,1024]{1,0:T(8,128)(2,1)}, bf16[1024,1024]{1,0:T(8,128)(2,1)}, u32[]{:S(2)}, u32[]{:S(2)}) collective-permute-start(bf16[1024,1024]{1,0:T(8,128)(2,1)} %convolution_convert_fusion.11.refs_0_.refs_4_), channel_id=1, source_target_pairs={{0,2},{1,3},{2,0},{3,1},{4,5},{5,4},{6,7},{7,6},{8,10},{9,11},{10,... | collective-permute-start | bytes 6291464 | tf_op jit(solution)/shard_map/ppermute | solution.py:68
  416.1 31.9 %collective-permute-start.45 = (bf16[256,4096]{1,0:T(8,128)(2,1)}, bf16[256,4096]{1,0:T(8,128)(2,1)}, u32[]{:S(2)}, u32[]{:S(2)}) collective-permute-start(bf16[256,4096]{1,0:T(8,128)(2,1)} %pad_maximum_fusion.7), channel_id=1, source_target_pairs={{0,4},{1,5},{2,6},{3,7},{4,0},{5,1},{6,2},{7,3},{8,12},{9,13},{10,... | collective-permute-start | bytes 6291464 | tf_op jit(solution)/shard_map/ppermute | solution.py:68
  439.9 50.1 %collective-permute-start.48 = (bf16[256,4096]{1,0:T(8,128)(2,1)S(1)}, bf16[256,4096]{1,0:T(8,128)(2,1)}, u32[]{:S(2)}, u32[]{:S(2)}) collective-permute-start(bf16[256,4096]{1,0:T(8,128)(2,1)S(1)} %convolution_convert_fusion.2.refs_5_), channel_id=1, source_target_pairs={{0,2},{1,3},{2,0},{3,1},{4,5},{5,4},{6,7},{7,6},{8,10},{9,11},{10,... | collective-permute-start | bytes 6291464 | tf_op jit(solution)/shard_map/ppermute | solution.py:68
  447.0 48.7 %collective-permute-start.47 = (bf16[512,1024]{1,0:T(8,128)(2,1)}, bf16[512,1024]{1,0:T(8,128)(2,1)}, u32[]{:S(2)}, u32[]{:S(2)}) collective-permute-start(bf16[512,1024]{1,0:T(8,128)(2,1)} %get-tuple-element.115.refs_13_), channel_id=1, source_target_pairs={{0,1},{1,0},{2,3},{3,2},{4,6},{5,7},{6,4},{7,5},{8,9},{9,8},{10,11... | collective-permute-start | bytes 3145736 | tf_op jit(solution)/shard_map/ppermute | solution.py:68
  481.3 37.0 %collective-permute-start.49 = (bf16[256,4096]{1,0:T(8,128)(2,1)}, bf16[256,4096]{1,0:T(8,128)(2,1)}, u32[]{:S(2)}, u32[]{:S(2)}) collective-permute-start(bf16[256,4096]{1,0:T(8,128)(2,1)} %pad_maximum_fusion.9.refs_14_), channel_id=1, source_target_pairs={{0,2},{1,3},{2,0},{3,1},{4,5},{5,4},{6,7},{7,6},{8,10},{9,11},{10,... | collective-permute-start | bytes 6291464 | tf_op jit(solution)/shard_map/ppermute | solution.py:68
  486.0 38.6 %collective-permute-start.50 = (bf16[2,256,384]{2,1,0:T(8,128)(2,1)}, bf16[2,256,384]{2,1,0:T(8,128)(2,1)}, u32[]{:S(2)}, u32[]{:S(2)}) collective-permute-start(bf16[2,256,384]{2,1,0:T(8,128)(2,1)} %get-tuple-element.151.refs_0_), channel_id=1, source_target_pairs={{0,8},{1,9},{2,10},{3,11},{4,12},{5,13},{6,14},{7,15},{8,0},{9,1},... | collective-permute-start | bytes 1179656 | tf_op jit(solution)/shard_map/ppermute | solution.py:68
  486.8 37.8 %collective-permute-start.51 = (bf16[2,256,384]{2,1,0:T(8,128)(2,1)}, bf16[2,256,384]{2,1,0:T(8,128)(2,1)}, u32[]{:S(2)}, u32[]{:S(2)}) collective-permute-start(bf16[2,256,384]{2,1,0:T(8,128)(2,1)} %get-tuple-element.152.refs_1_), channel_id=1, source_target_pairs={{0,16},{1,17},{2,18},{3,19},{4,20},{5,21},{6,22},{7,23},{8,24},{9,... | collective-permute-start | bytes 1179656 | tf_op jit(solution)/shard_map/ppermute | solution.py:68
  490.0 34.6 %collective-permute-start.52 = (bf16[2,256,384]{2,1,0:T(8,128)(2,1)}, bf16[2,256,384]{2,1,0:T(8,128)(2,1)S(1)}, u32[]{:S(2)}, u32[]{:S(2)}) collective-permute-start(bf16[2,256,384]{2,1,0:T(8,128)(2,1)} %get-tuple-element.153.refs_2_), channel_id=1, source_target_pairs={{0,24},{1,25},{2,26},{3,27},{4,28},{5,29},{6,30},{7,31},{8,16},{9,... | collective-permute-start | bytes 1179656 | tf_op jit(solution)/shard_map/ppermute | solution.py:68
  495.7 42.3 %collective-permute-start.56 = (bf16[128,4096]{1,0:T(8,128)(2,1)}, bf16[128,4096]{1,0:T(8,128)(2,1)}, u32[]{:S(2)}, u32[]{:S(2)}) collective-permute-start(bf16[128,4096]{1,0:T(8,128)(2,1)} %get-tuple-element.113.refs_1_), channel_id=1, source_target_pairs={{0,1},{1,0},{2,3},{3,2},{4,6},{5,7},{6,4},{7,5},{8,9},{9,8},{10,11... | collective-permute-start | bytes 3145736 | tf_op jit(solution)/shard_map/ppermute | solution.py:68
  522.1 54.2 %collective-permute-start.58 = (bf16[128,4096]{1,0:T(8,128)(2,1)}, bf16[128,4096]{1,0:T(8,128)(2,1)}, u32[]{:S(2)}, u32[]{:S(2)}) collective-permute-start(bf16[128,4096]{1,0:T(8,128)(2,1)} %get-tuple-element.111.refs_2_), channel_id=1, source_target_pairs={{0,1},{1,0},{2,3},{3,2},{4,6},{5,7},{6,4},{7,5},{8,9},{9,8},{10,11... | collective-permute-start | bytes 3145736 | tf_op jit(solution)/shard_map/ppermute | solution.py:68
  541.1 29.5 %collective-permute-start.57 = (bf16[64,4096]{1,0:T(8,128)(2,1)}, bf16[64,4096]{1,0:T(8,128)(2,1)}, u32[]{:S(2)}, u32[]{:S(2)}) collective-permute-start(bf16[64,4096]{1,0:T(8,128)(2,1)} %get-tuple-element.137), channel_id=1, source_target_pairs={{0,8},{1,9},{2,10},{3,11},{4,12},{5,13},{6,14},{7,15},{8,0},{9,1},... | collective-permute-start | bytes 1572872 | tf_op jit(solution)/shard_map/ppermute | solution.py:68
  543.6 29.0 %collective-permute-start.55 = (bf16[256,1024]{1,0:T(8,128)(2,1)}, bf16[256,1024]{1,0:T(8,128)(2,1)}, u32[]{:S(2)}, u32[]{:S(2)}) collective-permute-start(bf16[256,1024]{1,0:T(8,128)(2,1)} %broadcast_select_fusion.15), channel_id=1, source_target_pairs={{0,8},{1,9},{2,10},{3,11},{4,12},{5,13},{6,14},{7,15},{8,0},{9,1},... | collective-permute-start | bytes 1572872 | tf_op jit(solution)/shard_map/ppermute | solution.py:68
  561.2 28.6 %collective-permute-start.69 = (bf16[256,3072]{1,0:T(8,128)(2,1)}, bf16[256,3072]{1,0:T(8,128)(2,1)S(1)}, u32[]{:S(2)}, u32[]{:S(2)}) collective-permute-start(bf16[256,3072]{1,0:T(8,128)(2,1)} %convolution_convert_fusion.6.refs_0_), channel_id=1, source_target_pairs={{0,2},{1,3},{2,0},{3,1},{4,5},{5,4},{6,7},{7,6},{8,10},{9,11},{10,... | collective-permute-start | bytes 4718600 | tf_op jit(solution)/shard_map/ppermute | solution.py:68
  570.5 22.5 %collective-permute-start.62 = (bf16[256,4096]{1,0:T(8,128)(2,1)S(1)}, bf16[256,4096]{1,0:T(8,128)(2,1)S(1)}, u32[]{:S(2)}, u32[]{:S(2)}) collective-permute-start(bf16[256,4096]{1,0:T(8,128)(2,1)S(1)} %fusion.1), channel_id=1, source_target_pairs={{0,4},{1,5},{2,6},{3,7},{4,0},{5,1},{6,2},{7,3},{8,12},{9,13},{10,... | collective-permute-start | bytes 6291464 | tf_op jit(solution)/shard_map/ppermute | solution.py:68
  572.7 29.8 %collective-permute-start.81 = (bf16[32,4096]{1,0:T(8,128)(2,1)}, bf16[32,4096]{1,0:T(8,128)(2,1)}, u32[]{:S(2)}, u32[]{:S(2)}) collective-permute-start(bf16[32,4096]{1,0:T(8,128)(2,1)} %add_convert_fusion.34.refs_1_), channel_id=1, source_target_pairs={{0,16},{1,17},{2,18},{3,19},{4,20},{5,21},{6,22},{7,23},{8,24},{9,... | collective-permute-start | bytes 786440 | tf_op jit(solution)/shard_map/ppermute | solution.py:68
  577.0 37.2 %collective-permute-start.80 = (bf16[128,1024]{1,0:T(8,128)(2,1)S(1)}, bf16[128,1024]{1,0:T(8,128)(2,1)}, u32[]{:S(2)}, u32[]{:S(2)}) collective-permute-start(bf16[128,1024]{1,0:T(8,128)(2,1)S(1)} %add_convert_fusion.35.refs_0_), channel_id=1, source_target_pairs={{0,16},{1,17},{2,18},{3,19},{4,20},{5,21},{6,22},{7,23},{8,24},{9,... | collective-permute-start | bytes 786440 | tf_op jit(solution)/shard_map/ppermute | solution.py:68
  581.1 40.7 %collective-permute-start.78 = (bf16[64,4096]{1,0:T(8,128)(2,1)}, bf16[64,4096]{1,0:T(8,128)(2,1)}, u32[]{:S(2)}, u32[]{:S(2)}) collective-permute-start(bf16[64,4096]{1,0:T(8,128)(2,1)} %get-tuple-element.131.refs_2_), channel_id=1, source_target_pairs={{0,8},{1,9},{2,10},{3,11},{4,12},{5,13},{6,14},{7,15},{8,0},{9,1},... | collective-permute-start | bytes 1572872 | tf_op jit(solution)/shard_map/ppermute | solution.py:68
  589.8 47.5 %collective-permute-start.71 = (bf16[512,1024]{1,0:T(8,128)(2,1)}, bf16[512,1024]{1,0:T(8,128)(2,1)}, u32[]{:S(2)}, u32[]{:S(2)}) collective-permute-start(bf16[512,1024]{1,0:T(8,128)(2,1)} %convolution_convert_fusion.12.refs_4_), channel_id=1, source_target_pairs={{0,2},{1,3},{2,0},{3,1},{4,5},{5,4},{6,7},{7,6},{8,10},{9,11},{10,... | collective-permute-start | bytes 3145736 | tf_op jit(solution)/shard_map/ppermute | solution.py:68
  593.0 45.0 %collective-permute-start.72 = (bf16[512,1024]{1,0:T(8,128)(2,1)}, bf16[512,1024]{1,0:T(8,128)(2,1)}, u32[]{:S(2)}, u32[]{:S(2)}) collective-permute-start(bf16[512,1024]{1,0:T(8,128)(2,1)} %convolution_convert_fusion.13.refs_3_), channel_id=1, source_target_pairs={{0,2},{1,3},{2,0},{3,1},{4,5},{5,4},{6,7},{7,6},{8,10},{9,11},{10,... | collective-permute-start | bytes 3145736 | tf_op jit(solution)/shard_map/ppermute | solution.py:68
  602.5 31.6 %collective-permute-start.70 = (bf16[128,3072]{1,0:T(8,128)(2,1)}, bf16[128,3072]{1,0:T(8,128)(2,1)S(1)}, u32[]{:S(2)}, u32[]{:S(2)}) collective-permute-start(bf16[128,3072]{1,0:T(8,128)(2,1)} %get-tuple-element.117), channel_id=1, source_target_pairs={{0,1},{1,0},{2,3},{3,2},{4,6},{5,7},{6,4},{7,5},{8,9},{9,8},{10,11... | collective-permute-start | bytes 2359304 | tf_op jit(solution)/shard_map/ppermute | solution.py:68
  614.2 29.6 %collective-permute-start.64 = (bf16[128,4096]{1,0:T(8,128)(2,1)S(1)}, bf16[128,4096]{1,0:T(8,128)(2,1)}, u32[]{:S(2)}, u32[]{:S(2)}) collective-permute-start(bf16[128,4096]{1,0:T(8,128)(2,1)S(1)} %copy-done.28), channel_id=1, source_target_pairs={{0,2},{1,3},{2,0},{3,1},{4,5},{5,4},{6,7},{7,6},{8,10},{9,11},{10,... | collective-permute-start | bytes 3145736 | tf_op jit(solution)/shard_map/ppermute | solution.py:68
  631.7 26.7 %collective-permute-start.63 = (bf16[128,4096]{1,0:T(8,128)(2,1)S(1)}, bf16[128,4096]{1,0:T(8,128)(2,1)}, u32[]{:S(2)}, u32[]{:S(2)}) collective-permute-start(bf16[128,4096]{1,0:T(8,128)(2,1)S(1)} %copy-done.27), channel_id=1, source_target_pairs={{0,2},{1,3},{2,0},{3,1},{4,5},{5,4},{6,7},{7,6},{8,10},{9,11},{10,... | collective-permute-start | bytes 3145736 | tf_op jit(solution)/shard_map/ppermute | solution.py:68
  671.6 27.7 %collective-permute-start.67 = (bf16[64,4096]{1,0:T(8,128)(2,1)}, bf16[64,4096]{1,0:T(8,128)(2,1)S(1)}, u32[]{:S(2)}, u32[]{:S(2)}) collective-permute-start(bf16[64,4096]{1,0:T(8,128)(2,1)} %get-tuple-element.168.refs_0_), channel_id=1, source_target_pairs={{0,8},{1,9},{2,10},{3,11},{4,12},{5,13},{6,14},{7,15},{8,0},{9,1},... | collective-permute-start | bytes 1572872 | tf_op jit(solution)/shard_map/ppermute | solution.py:68
  674.4 27.2 %collective-permute-start.85 = (f32[37,64]{1,0:T(8,128)S(1)}, f32[37,64]{1,0:T(8,128)S(1)}, u32[]{:S(2)}, u32[]{:S(2)}) collective-permute-start(f32[37,64]{1,0:T(8,128)S(1)} %slice.933), channel_id=1, source_target_pairs={{0,8},{1,9},{2,10},{3,11},{4,12},{5,13},{6,14},{7,15},{8,0},{9,1},... | collective-permute-start | bytes 28424 | tf_op jit(solution)/shard_map/ppermute | solution.py:68
  677.0 27.4 %collective-permute-start.77 = (bf16[32,3072]{1,0:T(8,128)(2,1)}, bf16[32,3072]{1,0:T(8,128)(2,1)}, u32[]{:S(2)}, u32[]{:S(2)}) collective-permute-start(bf16[32,3072]{1,0:T(8,128)(2,1)} %add_convert_fusion.36), channel_id=1, source_target_pairs={{0,16},{1,17},{2,18},{3,19},{4,20},{5,21},{6,22},{7,23},{8,24},{9,... | collective-permute-start | bytes 589832 | tf_op jit(solution)/shard_map/ppermute | solution.py:68
  681.3 24.8 %collective-permute-start.75 = (bf16[128,1024]{1,0:T(8,128)(2,1)}, bf16[128,1024]{1,0:T(8,128)(2,1)S(1)}, u32[]{:S(2)}, u32[]{:S(2)}) collective-permute-start(bf16[128,1024]{1,0:T(8,128)(2,1)} %add_convert_fusion.30), channel_id=1, source_target_pairs={{0,16},{1,17},{2,18},{3,19},{4,20},{5,21},{6,22},{7,23},{8,24},{9,... | collective-permute-start | bytes 786440 | tf_op jit(solution)/shard_map/ppermute | solution.py:68
  (206 other events, 1912.4 us)
Sparse Core Ops, SparseCore 0:
  10.9 91.3 all-gather.3
  105.1 81.8 all-gather.5
  190.0 107.2 all-gather.7

commit v4 on v3

--- a/solution.py
+++ b/solution.py
@@ -371,15 +371,14 @@
 
 
 def attend_back_kernel(
-    q_ref, k_ref, v_ref, o_ref, do_ref, total_ref, idq_ref, idk_ref, cq_ref, sq_ref, ck_ref,
-    sk_ref, turn_ref, dq_ref, dk_ref, dv_ref, dk_sum, dv_sum,
+    q_ref, k_ref, v_ref, do_ref, total_ref, idq_ref, idk_ref, cq_ref, sq_ref, ck_ref, sk_ref,
+    turn_ref, dq_ref, dk_ref, dv_ref, dk_sum, dv_sum,
 ):
     step = pl.program_id(1)
     size = q_ref.shape[-1]
     scale = HEAD_DIM**-0.5
     query, keys, values, grads = q_ref[0] * scale, k_ref[0], v_ref[0], do_ref[0]
     different = idk_ref[0] != idq_ref[0]
-    product = grads.astype(F32) * o_ref[0].astype(F32)
 
     @pl.when(step == 0)
     def _():
@@ -391,13 +390,6 @@
         lanes = head_lanes(size, head)
         one_query = jnp.where(lanes, query, 0)
         one_grad = jnp.where(lanes, grads, 0)
-        delta = lax.dot_general(
-            jnp.where(lanes, jnp.ones((8, size), F32), 0.0),
-            product,
-            (((1,), (1,)), ((), ())),
-            precision=HIGHEST,
-            preferred_element_type=F32,
-        )[:1]
         scores = lax.dot_general(
             keys, one_query, (((1,), (1,)), ((), ())), preferred_element_type=F32
         )
@@ -405,6 +397,7 @@
         prob_grads = lax.dot_general(
             values, one_grad, (((1,), (1,)), ((), ())), preferred_element_type=F32
         )
+        delta = jnp.sum(probs * prob_grads, axis=0, keepdims=True)
         score_grads = (probs * (prob_grads - delta)).astype(BF16)
         dk_sum[...] += jnp.dot(score_grads, one_query, preferred_element_type=F32)
         dv_sum[...] += jnp.dot(probs.astype(BF16), one_grad, preferred_element_type=F32)
@@ -449,7 +442,7 @@
     )(query, keys, values, ids[:, :, None], ids[:, None, :], *tokens)
 
 
-def attend_back(query, keys, values, mixed, grads, totals, ids, cosine, sine, tokens=()):
+def attend_back(query, keys, values, grads, totals, ids, cosine, sine, tokens=()):
     rows, length, size = query.shape
     tile = 1024 if length <= 1024 else 256
     heads = size // HEAD_DIM
@@ -458,14 +451,13 @@
     lane = np.arange(size)
     turn = jnp.asarray((lane[:, None] == (lane ^ (HEAD_DIM // 2))[None, :]).astype(np.float32))
     return pl.pallas_call(
-        lambda *refs: attend_back_kernel(*refs[:13], *refs[13 + len(tokens) :]),
+        lambda *refs: attend_back_kernel(*refs[:12], *refs[12 + len(tokens) :]),
         out_shape=[jax.ShapeDtypeStruct(query.shape, BF16)] * 3,
         grid=(rows, length // tile),
         in_specs=[
             part,
             whole,
             whole,
-            part,
             part,
             pl.BlockSpec((1, heads, tile), lambda r, t: (r, 0, t)),
             pl.BlockSpec((1, 1, tile), lambda r, t: (r, 0, t)),
@@ -482,7 +474,7 @@
         compiler_params=pltpu.CompilerParams(vmem_limit_bytes=VMEM_LIMIT),
         name="attend_back",
     )(
-        query, keys, values, mixed, grads, totals.transpose(0, 2, 1), ids[:, None, :],
+        query, keys, values, grads, totals.transpose(0, 2, 1), ids[:, None, :],
         ids[:, :, None], cosine, sine, cosine, sine, turn, *tokens,
     )
 
@@ -903,7 +895,6 @@
         row_queries,
         row_keys,
         row_values,
-        mixed_rows,
         row_grads,
         row_totals,
         row_ids,

time: 734 us -> 735 us (level)
  transfers between devices with their start and end apart: 90 -> 90, of which waited for: 23 -> 27; matrix products, arithmetic and copies ran while one was open for 42% -> 42% of each run, Pallas kernels for 11% -> 11%
where the time goes in v4:
time: 735 us; the launch traced here: 723 us
  waiting for transfers between devices  172 us (23%)
  other arithmetic  137 us (19%)
  matrix products  125 us (17%)
  starting transfers between devices  119 us (16%)
  Pallas kernels  76.5 us (10%)
  local copies, waits for them, and re-layouts  55.3 us (8%)
  between operations  37.1 us (5%)
    ppermute x83, waiting for transfers between devices, send(): return lax.ppermute(x, BOTH, pairs)  169 us
    ppermute x83, starting transfers between devices, send(): return lax.ppermute(x, BOTH, pairs)  112 us
    dot_general x12, matrix products, dot_back(): lax.dot_general(left, right, (((1,), (1,)), ((), ())), preferred_element_...  46.1 us
    dot_general x18, matrix products, dot(): return jnp.dot(left, right, preferred_element_type=F32)  43.9 us
    select_n x32, other arithmetic, after(): jnp.where(flag, x, jnp.zeros((), x.dtype))  42.4 us
    dot_general x18, matrix products, dot_over_frames(): lax.dot_general(left, right, (((0,), (0,)), ((), ())), preferred_element_...  33.2 us
    convert_element_type x12, other arithmetic, grad_lane(): kept = (kept[:half].astype(F32) + stay.astype(F32)).astype(BF16)  23 us
    pallas_call x1, Pallas kernels, attend_back(): pl.pallas_call(lambda *refs: attend_back_kernel(*refs[:12], *refs[12 + le...  18.4 us
  transfers between devices with their start and end apart: 90, of which 27 were waited for; matrix products, arithmetic and copies ran while one was open for 42% of the time, Pallas kernels for 11%

profile of v4, /device:TPU:0, one launch (start us, length us, event | category | flops | bytes accessed | tf_op | source)
XLA Modules:
  0.0 723.1 jit_solution(9001399144892002059)
XLA Ops:
  10.4 3.0 collective-permute-start
  24.5 5.7 collective-permute-done.3
  32.3 5.3 collective-permute-start.4
  37.6 10.0 %collective-permute-done.4 = bf16[37,512]{1,0:T(8,128)(2,1)S(1)} collective-permute-done((bf16[37,512]{1,0:T(8,128)(2,1)}, bf16[37,512]{1,0:T(8,128)(2,1)S(1)}, u32[]{:S(2)}, u32[]{:S(2)}) %collective-permute-start.4) | collective-permute-done | bytes 37920 | tf_op jit(solution)/shard_map/ppermute | solution.py:68
  53.0 5.8 collective-permute-start.11
  58.7 7.2 collective-permute-done.7
  71.7 4.6 collective-permute-start.12
  77.5 22.8 %collective-permute-done.12 = bf16[2,128,1024]{2,1,0:T(8,128)(2,1)S(1)} collective-permute-done((bf16[2,128,1024]{2,1,0:T(8,128)(2,1)S(1)}, bf16[2,128,1024]{2,1,0:T(8,128)(2,1)S(1)}, u32[]{:S(2)}, u32[]{:S(2)}) %collective-permute-start.12) | collective-permute-done | bytes 524320 | tf_op jit(solution)/shard_map/ppermute | solution.py:68
  107.0 11.4 %collective-permute-done.13 = bf16[4,128,1024]{2,1,0:T(8,128)(2,1)} collective-permute-done((bf16[4,128,1024]{2,1,0:T(8,128)(2,1)}, bf16[4,128,1024]{2,1,0:T(8,128)(2,1)}, u32[]{:S(2)}, u32[]{:S(2)}) %collective-permute-start.13) | collective-permute-done | bytes 1048608 | tf_op jit(solution)/shard_map/ppermute | solution.py:68
  118.4 3.5 broadcast_select_fusion.6
  124.0 5.6 fusion.85
  139.1 13.0 %collective-permute-done.14.refs_1_ = bf16[8,128,1024]{2,1,0:T(8,128)(2,1)} collective-permute-done((bf16[8,128,1024]{2,1,0:T(8,128)(2,1)}, bf16[8,128,1024]{2,1,0:T(8,128)(2,1)}, u32[]{:S(2)}, u32[]{:S(2)}) %collective-permute-start.14) | collective-permute-done | bytes 2097184 | tf_op jit(solution)/shard_map/ppermute | solution.py:68
  155.3 5.4 assemble.3
  160.7 4.6 multiply_convert_fusion.1
  165.6 3.0 assemble.4
  172.2 4.7 fusion.213.refs_0_
  189.6 3.1 collective-permute-start.27
  204.6 5.2 collective-permute-done.27
  212.8 10.1 %collective-permute-done.18 = bf16[2,256,384]{2,1,0:T(8,128)(2,1)} collective-permute-done((bf16[2,256,384]{2,1,0:T(8,128)(2,1)S(1)}, bf16[2,256,384]{2,1,0:T(8,128)(2,1)}, u32[]{:S(2)}, u32[]{:S(2)}) %collective-permute-start.18) | collective-permute-done | bytes 393248 | tf_op jit(solution)/shard_map/ppermute | solution.py:68
  223.0 13.7 %collective-permute-done.19 = bf16[2,256,384]{2,1,0:T(8,128)(2,1)} collective-permute-done((bf16[2,256,384]{2,1,0:T(8,128)(2,1)S(1)}, bf16[2,256,384]{2,1,0:T(8,128)(2,1)}, u32[]{:S(2)}, u32[]{:S(2)}) %collective-permute-start.19) | collective-permute-done | bytes 393248 | tf_op jit(solution)/shard_map/ppermute | solution.py:68
  241.3 13.4 %attend.1 = (bf16[2,1024,128]{2,1,0:T(8,128)(2,1)}, f32[2,1024,2]{2,1,0:T(8,128)}) custom-call(bf16[2,1024,128]{2,1,0:T(8,128)(2,1)} %bitcast.341, bf16[2,1024,128]{2,1,0:T(8,128)(2,1)} %bitcast.343, bf16[2,1024,128]{2,1,0:T(8,128)(2,1)} %bitcast.345, s32[2,1024,1]{2,1,0:T(8,128)} %copy.90.refs_3_.refs_6_, s32[2,1,1024]{2,1,0:T(1,128)} %bitcast.399), custom_call_target="tpu_custom_call" | custom-call | tf_op jit(solution)/shard_map/attend/pallas_call | solution.py:424
  263.3 17.8 %collective-permute-start.22 = (bf16[2,256,128]{2,1,0:T(8,128)(2,1)S(1)}, bf16[2,256,128]{2,1,0:T(8,128)(2,1)S(1)}, u32[]{:S(2)}, u32[]{:S(2)}) collective-permute-start(bf16[2,256,128]{2,1,0:T(8,128)(2,1)S(1)} %get-tuple-element.196.refs_0_), channel_id=1, source_target_pairs={{0,8},{1,9},{2,10},{3,11},{4,12},{5,13},{6,14},{7,15},{8,0},{9,1},... | collective-permute-start | bytes 393224 | tf_op jit(solution)/shard_map/ppermute | solution.py:68
  284.6 2.8 pad_maximum_fusion.11
  293.1 4.8 collective-permute-done.23
  309.9 3.6 fusion.20
  325.9 4.9 depthwise.1
  336.3 3.1 broadcast_select_fusion.5.refs_1_
  339.4 3.2 collective-permute-start.32
  342.6 7.8 %multiply_convert_fusion = (bf16[256,4096]{1,0:T(8,128)(2,1)S(1)}, f32[256,4096]{1,0:T(8,128)}) fusion(bf16[1024,4096]{1,0:T(8,128)(2,1)} %all-gather.8.cloned.1.call-done, f32[256,1024]{1,0:T(8,128)S(1)} %get-tuple-element.231, f32[1024]{0:T(1024)S(1)} %bitcast.417, f32[256]{0:T(256)S(1)} %add_rsqrt_fusion.1, f32[256]{0:T(256)S(1)} %broadcast_multiply_fusion.12), kind=kOutput, calls=%fused_computation.21 | convolution fusion | flops 2153775104 | bytes 15734784 | tf_op jit(solution)/shard_map/dot_general | solution.py:335
  357.2 4.3 assemble.5
  366.7 4.2 fusion
  371.4 8.1 %multiply_reduce_fusion = (f32[1024]{0:T(1024)}, f32[256]{0:T(256)S(1)}, f32[256]{0:T(256)S(1)}, f32[256,1024]{1,0:T(8,128)}) fusion(f32[256,1024]{1,0:T(8,128)S(1)} %copy-done.25, f32[256]{0:T(256)S(1)} %add_rsqrt_fusion.1, f32[256]{0:T(256)S(1)} %broadcast_multiply_fusion.12, f32[1024]{0:T(1024)S(1)} %bitcast.419, bf16[256,4096]{1,0:T(8,128)(2,1)} %fusion, ...), kind=kOutput, calls=%fused_computation.209 | convolution fusion | flops 2149579264 | bytes 12595200 | tf_op jit(solution)/shard_map/dot_general | solution.py:339
  386.7 3.6 multiply_reduce_fusion.1
  395.2 8.4 %depthwise_back.1 = (f32[2,31,1024]{2,1,0:T(8,128)S(1)}, f32[2,160,1024]{2,1,0:T(8,128)S(1)}) custom-call(bf16[2,160,1024]{2,1,0:T(8,128)(2,1)S(1)} %copy-done.6, f32[2,160,1]{2,1,0:T(8,128)S(1)} %copy-done.7, f32[2,128,1024]{2,1,0:T(8,128)S(1)} %bitcast.334, f32[31,1024]{1,0:T(8,128)S(1)} %slice.811.refs_2_.refs_3_, ...), custom_call_target="tpu_custom_call" | custom-call | tf_op jit(solution)/shard_map/depthwise_back/pallas_call | solution.py:557
  419.1 3.1 fusion.81
  423.2 4.8 convolution_convert_fusion.1
  436.2 5.4 collective-permute-done.42
  458.3 18.4 %attend_back.1 = (bf16[2,1024,128]{2,1,0:T(8,128)(2,1)}, bf16[2,1024,128]{2,1,0:T(8,128)(2,1)}, bf16[2,1024,128]{2,1,0:T(8,128)(2,1)}) custom-call(bf16[2,1024,128]{2,1,0:T(8,128)(2,1)} %bitcast.342, bf16[2,1024,128]{2,1,0:T(8,128)(2,1)} %bitcast.344, bf16[2,1024,128]{2,1,0:T(8,128)(2,1)} %bitcast.346, bf16[2,1024,128]{2,1,0:T(8,128)(2,1)} %bitcast.361, ...), custom_call_target="tpu_custom_call" | custom-call | tf_op jit(solution)/shard_map/attend_back/pallas_call | solution.py:453
  500.1 19.6 %collective-permute-done.49 = bf16[256,4096]{1,0:T(8,128)(2,1)} collective-permute-done((bf16[256,4096]{1,0:T(8,128)(2,1)}, bf16[256,4096]{1,0:T(8,128)(2,1)}, u32[]{:S(2)}, u32[]{:S(2)}) %collective-permute-start.49) | collective-permute-done | bytes 2097184 | tf_op jit(solution)/shard_map/ppermute | solution.py:68
  546.1 6.9 multiply_reduce_fusion.3
  558.6 3.4 fusion.121
  563.5 7.5 %fusion.1 = bf16[256,4096]{1,0:T(8,128)(2,1)S(1)} fusion(bf16[256,1024]{1,0:T(8,128)(2,1)} %get-tuple-element.100.refs_0_, bf16[4096,1024]{1,0:T(8,128)(2,1)} %copy-done.4, f32[256,4096]{1,0:T(8,128)} %get-tuple-element.225), kind=kOutput, calls=%fused_computation.5 | convolution fusion | flops 2156920832 | bytes 15204352 | tf_op jit(solution)/shard_map/dot_general | solution.py:339
  606.7 8.5 %multiply_reduce_fusion.4 = (f32[1024]{0:T(1024)}, f32[256]{0:T(256)}, f32[256]{0:T(256)}, f32[256,1024]{1,0:T(8,128)}) fusion(bf16[2,128,1024]{2,1,0:T(8,128)(2,1)S(1)} %copy-done.42, f32[256]{0:T(256)S(1)} %copy-done.144, f32[256]{0:T(256)S(1)} %copy-done.142, f32[1024]{0:T(1024)S(1)} %bitcast.406, bf16[256,4096]{1,0:T(8,128)(2,1)} %broadcast_select_fusion.refs_0_, ...), kind=kOutput, calls=%fused_computation.213 | convolution fusion | flops 2149841408 | bytes 12070912 | tf_op jit(solution)/shard_map/dot_general | solution.py:339
  625.1 5.0 convolution_convert_fusion
  638.6 4.3 add_convert_fusion.1
  666.6 3.7 collective-permute-done.66
  683.5 16.5 %collective-permute-done.67 = bf16[64,4096]{1,0:T(8,128)(2,1)S(1)} collective-permute-done((bf16[64,4096]{1,0:T(8,128)(2,1)}, bf16[64,4096]{1,0:T(8,128)(2,1)S(1)}, u32[]{:S(2)}, u32[]{:S(2)}) %collective-permute-start.67) | collective-permute-done | bytes 524320 | tf_op jit(solution)/shard_map/ppermute | solution.py:68
  707.7 6.3 collective-permute-done.86
  (787 shorter events, 334.8 us)
Async XLA Ops:
  7.2 165.0 %all-gather.4.cloned.1.call-start = ((), (), s32[]{:S(2)}) async-start(), calls=%async_computation | async-start | bytes 6488064 | tf_op jit(solution)/shard_map/all_gather | solution.py:687
  7.9 299.1 %all-gather.6.cloned.1.call-start = ((), (), s32[]{:S(2)}) async-start(), calls=%async_computation.1 | async-start | bytes 8650752 | tf_op jit(solution)/shard_map/all_gather | solution.py:689
  9.7 332.9 %all-gather.8.cloned.1.call-start = ((), (), s32[]{:S(2)}) async-start(), calls=%async_computation.2 | async-start | bytes 8650752 | tf_op jit(solution)/shard_map/all_gather | solution.py:694
  67.7 38.2 %collective-permute-start.8 = (bf16[8,128,1024]{2,1,0:T(8,128)(2,1)S(1)}, bf16[8,128,1024]{2,1,0:T(8,128)(2,1)}, u32[]{:S(2)}, u32[]{:S(2)}) collective-permute-start(bf16[8,128,1024]{2,1,0:T(8,128)(2,1)S(1)} %pad_maximum_fusion.3.refs_0_), channel_id=1, source_target_pairs={{0,2},{1,3},{2,0},{3,1},{4,5},{5,4},{6,7},{7,6},{8,10},{9,11},{10,... | collective-permute-start | bytes 6291464 | tf_op jit(solution)/shard_map/ppermute | solution.py:68
  71.7 28.7 %collective-permute-start.12 = (bf16[2,128,1024]{2,1,0:T(8,128)(2,1)S(1)}, bf16[2,128,1024]{2,1,0:T(8,128)(2,1)S(1)}, u32[]{:S(2)}, u32[]{:S(2)}) collective-permute-start(bf16[2,128,1024]{2,1,0:T(8,128)(2,1)S(1)} %maximum_select_fusion.4), channel_id=1, source_target_pairs={{0,8},{1,9},{2,10},{3,11},{4,12},{5,13},{6,14},{7,15},{8,0},{9,1},... | collective-permute-start | bytes 1572872 | tf_op jit(solution)/shard_map/ppermute | solution.py:68
  121.9 30.1 %collective-permute-start.14 = (bf16[8,128,1024]{2,1,0:T(8,128)(2,1)}, bf16[8,128,1024]{2,1,0:T(8,128)(2,1)}, u32[]{:S(2)}, u32[]{:S(2)}) collective-permute-start(bf16[8,128,1024]{2,1,0:T(8,128)(2,1)} %get-tuple-element.144.refs_0_), channel_id=1, source_target_pairs={{0,2},{1,3},{2,0},{3,1},{4,5},{5,4},{6,7},{7,6},{8,10},{9,11},{10,... | collective-permute-start | bytes 6291464 | tf_op jit(solution)/shard_map/ppermute | solution.py:68
  129.5 25.7 %collective-permute-start.9 = (bf16[8,128,1024]{2,1,0:T(8,128)(2,1)S(1)}, bf16[8,128,1024]{2,1,0:T(8,128)(2,1)}, u32[]{:S(2)}, u32[]{:S(2)}) collective-permute-start(bf16[8,128,1024]{2,1,0:T(8,128)(2,1)S(1)} %copy-done.1), channel_id=1, source_target_pairs={{0,4},{1,5},{2,6},{3,7},{4,0},{5,1},{6,2},{7,3},{8,12},{9,13},{10,... | collective-permute-start | bytes 6291464 | tf_op jit(solution)/shard_map/ppermute | solution.py:68
  129.5 25.7 %collective-permute-start.10 = (bf16[8,128,1024]{2,1,0:T(8,128)(2,1)}, bf16[8,128,1024]{2,1,0:T(8,128)(2,1)}, u32[]{:S(2)}, u32[]{:S(2)}) collective-permute-start(bf16[8,128,1024]{2,1,0:T(8,128)(2,1)} %collective-permute-done.8.refs_1_), channel_id=1, source_target_pairs={{0,4},{1,5},{2,6},{3,7},{4,0},{5,1},{6,2},{7,3},{8,12},{9,13},{10,... | collective-permute-start | bytes 6291464 | tf_op jit(solution)/shard_map/ppermute | solution.py:68
  139.0 26.6 %collective-permute-start.15 = (bf16[8,128,1024]{2,1,0:T(8,128)(2,1)}, bf16[8,128,1024]{2,1,0:T(8,128)(2,1)S(1)}, u32[]{:S(2)}, u32[]{:S(2)}) collective-permute-start(bf16[8,128,1024]{2,1,0:T(8,128)(2,1)} %get-tuple-element.145.refs_0_), channel_id=1, source_target_pairs={{0,4},{1,5},{2,6},{3,7},{4,0},{5,1},{6,2},{7,3},{8,12},{9,13},{10,... | collective-permute-start | bytes 6291464 | tf_op jit(solution)/shard_map/ppermute | solution.py:68
  155.1 30.7 %collective-permute-start.61 = (bf16[256,512]{1,0:T(8,128)(2,1)}, bf16[256,512]{1,0:T(8,128)(2,1)}, u32[]{:S(2)}, u32[]{:S(2)}) collective-permute-start(bf16[256,512]{1,0:T(8,128)(2,1)} %get-tuple-element.177), channel_id=1, source_target_pairs={{0,4},{1,5},{2,6},{3,7},{4,0},{5,1},{6,2},{7,3},{8,12},{9,13},{10,... | collective-permute-start | bytes 786440 | tf_op jit(solution)/shard_map/ppermute | solution.py:68
  194.8 88.4 %collective-permute-start.59 = (bf16[256,2048]{1,0:T(8,128)(2,1)}, bf16[256,2048]{1,0:T(8,128)(2,1)}, u32[]{:S(2)}, u32[]{:S(2)}) collective-permute-start(bf16[256,2048]{1,0:T(8,128)(2,1)} %get-tuple-element.62), channel_id=1, source_target_pairs={{0,4},{1,5},{2,6},{3,7},{4,0},{5,1},{6,2},{7,3},{8,12},{9,13},{10,... | collective-permute-start | bytes 3145736 | tf_op jit(solution)/shard_map/ppermute | solution.py:68
  198.1 24.8 %collective-permute-start.18 = (bf16[2,256,384]{2,1,0:T(8,128)(2,1)S(1)}, bf16[2,256,384]{2,1,0:T(8,128)(2,1)}, u32[]{:S(2)}, u32[]{:S(2)}) collective-permute-start(bf16[2,256,384]{2,1,0:T(8,128)(2,1)S(1)} %get-tuple-element.160.refs_0_), channel_id=1, source_target_pairs={{0,8},{1,9},{2,10},{3,11},{4,12},{5,13},{6,14},{7,15},{8,0},{9,1},... | collective-permute-start | bytes 1179656 | tf_op jit(solution)/shard_map/ppermute | solution.py:68
  199.7 37.0 %collective-permute-start.19 = (bf16[2,256,384]{2,1,0:T(8,128)(2,1)S(1)}, bf16[2,256,384]{2,1,0:T(8,128)(2,1)}, u32[]{:S(2)}, u32[]{:S(2)}) collective-permute-start(bf16[2,256,384]{2,1,0:T(8,128)(2,1)S(1)} %get-tuple-element.162.refs_1_), channel_id=1, source_target_pairs={{0,16},{1,17},{2,18},{3,19},{4,20},{5,21},{6,22},{7,23},{8,24},{9,... | collective-permute-start | bytes 1179656 | tf_op jit(solution)/shard_map/ppermute | solution.py:68
  200.1 36.6 %collective-permute-start.20 = (bf16[2,256,384]{2,1,0:T(8,128)(2,1)S(1)}, bf16[2,256,384]{2,1,0:T(8,128)(2,1)}, u32[]{:S(2)}, u32[]{:S(2)}) collective-permute-start(bf16[2,256,384]{2,1,0:T(8,128)(2,1)S(1)} %get-tuple-element.161.refs_2_), channel_id=1, source_target_pairs={{0,24},{1,25},{2,26},{3,27},{4,28},{5,29},{6,30},{7,31},{8,16},{9,... | collective-permute-start | bytes 1179656 | tf_op jit(solution)/shard_map/ppermute | solution.py:68
  209.8 77.6 %collective-permute-start.53 = (bf16[256,512]{1,0:T(8,128)(2,1)}, bf16[256,512]{1,0:T(8,128)(2,1)}, u32[]{:S(2)}, u32[]{:S(2)}) collective-permute-start(bf16[256,512]{1,0:T(8,128)(2,1)} %get-tuple-element.192), channel_id=1, source_target_pairs={{0,4},{1,5},{2,6},{3,7},{4,0},{5,1},{6,2},{7,3},{8,12},{9,13},{10,... | collective-permute-start | bytes 786440 | tf_op jit(solution)/shard_map/ppermute | solution.py:68
  223.0 35.6 %collective-permute-start.28 = (bf16[2,128,1024]{2,1,0:T(8,128)(2,1)}, bf16[2,128,1024]{2,1,0:T(8,128)(2,1)S(1)}, u32[]{:S(2)}, u32[]{:S(2)}) collective-permute-start(bf16[2,128,1024]{2,1,0:T(8,128)(2,1)} %pad_maximum_fusion.22), channel_id=1, source_target_pairs={{0,8},{1,9},{2,10},{3,11},{4,12},{5,13},{6,14},{7,15},{8,0},{9,1},... | collective-permute-start | bytes 1572872 | tf_op jit(solution)/shard_map/ppermute | solution.py:68
  260.0 44.4 %collective-permute-start.29 = (bf16[4,128,1024]{2,1,0:T(8,128)(2,1)S(1)}, bf16[4,128,1024]{2,1,0:T(8,128)(2,1)}, u32[]{:S(2)}, u32[]{:S(2)}) collective-permute-start(bf16[4,128,1024]{2,1,0:T(8,128)(2,1)S(1)} %maximum_select_fusion.2), channel_id=1, source_target_pairs={{0,1},{1,0},{2,3},{3,2},{4,6},{5,7},{6,4},{7,5},{8,9},{9,8},{10,11... | collective-permute-start | bytes 3145736 | tf_op jit(solution)/shard_map/ppermute | solution.py:68
  263.3 29.7 %collective-permute-start.22 = (bf16[2,256,128]{2,1,0:T(8,128)(2,1)S(1)}, bf16[2,256,128]{2,1,0:T(8,128)(2,1)S(1)}, u32[]{:S(2)}, u32[]{:S(2)}) collective-permute-start(bf16[2,256,128]{2,1,0:T(8,128)(2,1)S(1)} %get-tuple-element.196.refs_0_), channel_id=1, source_target_pairs={{0,8},{1,9},{2,10},{3,11},{4,12},{5,13},{6,14},{7,15},{8,0},{9,1},... | collective-permute-start | bytes 393224 | tf_op jit(solution)/shard_map/ppermute | solution.py:68
  305.9 30.3 %collective-permute-start.30 = (bf16[8,128,1024]{2,1,0:T(8,128)(2,1)S(1)}, bf16[8,128,1024]{2,1,0:T(8,128)(2,1)}, u32[]{:S(2)}, u32[]{:S(2)}) collective-permute-start(bf16[8,128,1024]{2,1,0:T(8,128)(2,1)S(1)} %pad_maximum_fusion.5.refs_0_), channel_id=1, source_target_pairs={{0,2},{1,3},{2,0},{3,1},{4,5},{5,4},{6,7},{7,6},{8,10},{9,11},{10,... | collective-permute-start | bytes 6291464 | tf_op jit(solution)/shard_map/ppermute | solution.py:68
  307.1 50.1 %collective-permute-start.31 = (bf16[8,128,1024]{2,1,0:T(8,128)(2,1)S(1)}, bf16[8,128,1024]{2,1,0:T(8,128)(2,1)}, u32[]{:S(2)}, u32[]{:S(2)}) collective-permute-start(bf16[8,128,1024]{2,1,0:T(8,128)(2,1)S(1)} %pad_maximum_fusion.5.refs_0_), channel_id=1, source_target_pairs={{0,4},{1,5},{2,6},{3,7},{4,0},{5,1},{6,2},{7,3},{8,12},{9,13},{10,... | collective-permute-start | bytes 6291464 | tf_op jit(solution)/shard_map/ppermute | solution.py:68
  356.1 77.8 %collective-permute-start.44 = (bf16[256,1536]{1,0:T(8,128)(2,1)}, bf16[256,1536]{1,0:T(8,128)(2,1)}, u32[]{:S(2)}, u32[]{:S(2)}) collective-permute-start(bf16[256,1536]{1,0:T(8,128)(2,1)} %pad_maximum_fusion.20), channel_id=1, source_target_pairs={{0,4},{1,5},{2,6},{3,7},{4,0},{5,1},{6,2},{7,3},{8,12},{9,13},{10,... | collective-permute-start | bytes 2359304 | tf_op jit(solution)/shard_map/ppermute | solution.py:68
  410.1 34.1 %collective-permute-start.40 = (bf16[1024,1024]{1,0:T(8,128)(2,1)}, bf16[1024,1024]{1,0:T(8,128)(2,1)}, u32[]{:S(2)}, u32[]{:S(2)}) collective-permute-start(bf16[1024,1024]{1,0:T(8,128)(2,1)} %convolution_convert_fusion.11.refs_0_.refs_4_), channel_id=1, source_target_pairs={{0,2},{1,3},{2,0},{3,1},{4,5},{5,4},{6,7},{7,6},{8,10},{9,11},{10,... | collective-permute-start | bytes 6291464 | tf_op jit(solution)/shard_map/ppermute | solution.py:68
  417.8 31.7 %collective-permute-start.45 = (bf16[256,4096]{1,0:T(8,128)(2,1)}, bf16[256,4096]{1,0:T(8,128)(2,1)}, u32[]{:S(2)}, u32[]{:S(2)}) collective-permute-start(bf16[256,4096]{1,0:T(8,128)(2,1)} %pad_maximum_fusion.7), channel_id=1, source_target_pairs={{0,4},{1,5},{2,6},{3,7},{4,0},{5,1},{6,2},{7,3},{8,12},{9,13},{10,... | collective-permute-start | bytes 6291464 | tf_op jit(solution)/shard_map/ppermute | solution.py:68
  441.6 48.9 %collective-permute-start.48 = (bf16[256,4096]{1,0:T(8,128)(2,1)S(1)}, bf16[256,4096]{1,0:T(8,128)(2,1)}, u32[]{:S(2)}, u32[]{:S(2)}) collective-permute-start(bf16[256,4096]{1,0:T(8,128)(2,1)S(1)} %convolution_convert_fusion.2.refs_5_), channel_id=1, source_target_pairs={{0,2},{1,3},{2,0},{3,1},{4,5},{5,4},{6,7},{7,6},{8,10},{9,11},{10,... | collective-permute-start | bytes 6291464 | tf_op jit(solution)/shard_map/ppermute | solution.py:68
  448.6 47.8 %collective-permute-start.47 = (bf16[512,1024]{1,0:T(8,128)(2,1)}, bf16[512,1024]{1,0:T(8,128)(2,1)}, u32[]{:S(2)}, u32[]{:S(2)}) collective-permute-start(bf16[512,1024]{1,0:T(8,128)(2,1)} %get-tuple-element.115.refs_12_), channel_id=1, source_target_pairs={{0,1},{1,0},{2,3},{3,2},{4,6},{5,7},{6,4},{7,5},{8,9},{9,8},{10,11... | collective-permute-start | bytes 3145736 | tf_op jit(solution)/shard_map/ppermute | solution.py:68
  482.4 37.3 %collective-permute-start.49 = (bf16[256,4096]{1,0:T(8,128)(2,1)}, bf16[256,4096]{1,0:T(8,128)(2,1)}, u32[]{:S(2)}, u32[]{:S(2)}) collective-permute-start(bf16[256,4096]{1,0:T(8,128)(2,1)} %pad_maximum_fusion.9.refs_13_), channel_id=1, source_target_pairs={{0,2},{1,3},{2,0},{3,1},{4,5},{5,4},{6,7},{7,6},{8,10},{9,11},{10,... | collective-permute-start | bytes 6291464 | tf_op jit(solution)/shard_map/ppermute | solution.py:68
  486.8 39.2 %collective-permute-start.50 = (bf16[2,256,384]{2,1,0:T(8,128)(2,1)}, bf16[2,256,384]{2,1,0:T(8,128)(2,1)}, u32[]{:S(2)}, u32[]{:S(2)}) collective-permute-start(bf16[2,256,384]{2,1,0:T(8,128)(2,1)} %get-tuple-element.151.refs_0_), channel_id=1, source_target_pairs={{0,8},{1,9},{2,10},{3,11},{4,12},{5,13},{6,14},{7,15},{8,0},{9,1},... | collective-permute-start | bytes 1179656 | tf_op jit(solution)/shard_map/ppermute | solution.py:68
  487.6 38.5 %collective-permute-start.51 = (bf16[2,256,384]{2,1,0:T(8,128)(2,1)}, bf16[2,256,384]{2,1,0:T(8,128)(2,1)}, u32[]{:S(2)}, u32[]{:S(2)}) collective-permute-start(bf16[2,256,384]{2,1,0:T(8,128)(2,1)} %get-tuple-element.152.refs_1_), channel_id=1, source_target_pairs={{0,16},{1,17},{2,18},{3,19},{4,20},{5,21},{6,22},{7,23},{8,24},{9,... | collective-permute-start | bytes 1179656 | tf_op jit(solution)/shard_map/ppermute | solution.py:68
  490.5 35.5 %collective-permute-start.52 = (bf16[2,256,384]{2,1,0:T(8,128)(2,1)}, bf16[2,256,384]{2,1,0:T(8,128)(2,1)S(1)}, u32[]{:S(2)}, u32[]{:S(2)}) collective-permute-start(bf16[2,256,384]{2,1,0:T(8,128)(2,1)} %get-tuple-element.153.refs_2_), channel_id=1, source_target_pairs={{0,24},{1,25},{2,26},{3,27},{4,28},{5,29},{6,30},{7,31},{8,16},{9,... | collective-permute-start | bytes 1179656 | tf_op jit(solution)/shard_map/ppermute | solution.py:68
  496.5 42.9 %collective-permute-start.56 = (bf16[128,4096]{1,0:T(8,128)(2,1)}, bf16[128,4096]{1,0:T(8,128)(2,1)}, u32[]{:S(2)}, u32[]{:S(2)}) collective-permute-start(bf16[128,4096]{1,0:T(8,128)(2,1)} %get-tuple-element.113.refs_1_), channel_id=1, source_target_pairs={{0,1},{1,0},{2,3},{3,2},{4,6},{5,7},{6,4},{7,5},{8,9},{9,8},{10,11... | collective-permute-start | bytes 3145736 | tf_op jit(solution)/shard_map/ppermute | solution.py:68
  523.5 53.2 %collective-permute-start.58 = (bf16[128,4096]{1,0:T(8,128)(2,1)}, bf16[128,4096]{1,0:T(8,128)(2,1)}, u32[]{:S(2)}, u32[]{:S(2)}) collective-permute-start(bf16[128,4096]{1,0:T(8,128)(2,1)} %get-tuple-element.111.refs_2_), channel_id=1, source_target_pairs={{0,1},{1,0},{2,3},{3,2},{4,6},{5,7},{6,4},{7,5},{8,9},{9,8},{10,11... | collective-permute-start | bytes 3145736 | tf_op jit(solution)/shard_map/ppermute | solution.py:68
  542.5 29.2 %collective-permute-start.57 = (bf16[64,4096]{1,0:T(8,128)(2,1)}, bf16[64,4096]{1,0:T(8,128)(2,1)}, u32[]{:S(2)}, u32[]{:S(2)}) collective-permute-start(bf16[64,4096]{1,0:T(8,128)(2,1)} %get-tuple-element.137), channel_id=1, source_target_pairs={{0,8},{1,9},{2,10},{3,11},{4,12},{5,13},{6,14},{7,15},{8,0},{9,1},... | collective-permute-start | bytes 1572872 | tf_op jit(solution)/shard_map/ppermute | solution.py:68
  545.0 28.9 %collective-permute-start.55 = (bf16[256,1024]{1,0:T(8,128)(2,1)}, bf16[256,1024]{1,0:T(8,128)(2,1)}, u32[]{:S(2)}, u32[]{:S(2)}) collective-permute-start(bf16[256,1024]{1,0:T(8,128)(2,1)} %broadcast_select_fusion.15), channel_id=1, source_target_pairs={{0,8},{1,9},{2,10},{3,11},{4,12},{5,13},{6,14},{7,15},{8,0},{9,1},... | collective-permute-start | bytes 1572872 | tf_op jit(solution)/shard_map/ppermute | solution.py:68
  562.1 20.3 %collective-permute-start.60 = (bf16[256,1024]{1,0:T(8,128)(2,1)}, bf16[256,1024]{1,0:T(8,128)(2,1)}, u32[]{:S(2)}, u32[]{:S(2)}) collective-permute-start(bf16[256,1024]{1,0:T(8,128)(2,1)} %get-tuple-element.100.refs_0_), channel_id=1, source_target_pairs={{0,4},{1,5},{2,6},{3,7},{4,0},{5,1},{6,2},{7,3},{8,12},{9,13},{10,... | collective-permute-start | bytes 1572872 | tf_op jit(solution)/shard_map/ppermute | solution.py:68
  562.6 28.3 %collective-permute-start.69 = (bf16[256,3072]{1,0:T(8,128)(2,1)}, bf16[256,3072]{1,0:T(8,128)(2,1)S(1)}, u32[]{:S(2)}, u32[]{:S(2)}) collective-permute-start(bf16[256,3072]{1,0:T(8,128)(2,1)} %convolution_convert_fusion.6.refs_0_), channel_id=1, source_target_pairs={{0,2},{1,3},{2,0},{3,1},{4,5},{5,4},{6,7},{7,6},{8,10},{9,11},{10,... | collective-permute-start | bytes 4718600 | tf_op jit(solution)/shard_map/ppermute | solution.py:68
  571.7 22.1 %collective-permute-start.62 = (bf16[256,4096]{1,0:T(8,128)(2,1)S(1)}, bf16[256,4096]{1,0:T(8,128)(2,1)S(1)}, u32[]{:S(2)}, u32[]{:S(2)}) collective-permute-start(bf16[256,4096]{1,0:T(8,128)(2,1)S(1)} %fusion.1), channel_id=1, source_target_pairs={{0,4},{1,5},{2,6},{3,7},{4,0},{5,1},{6,2},{7,3},{8,12},{9,13},{10,... | collective-permute-start | bytes 6291464 | tf_op jit(solution)/shard_map/ppermute | solution.py:68
  573.9 29.6 %collective-permute-start.81 = (bf16[32,4096]{1,0:T(8,128)(2,1)}, bf16[32,4096]{1,0:T(8,128)(2,1)}, u32[]{:S(2)}, u32[]{:S(2)}) collective-permute-start(bf16[32,4096]{1,0:T(8,128)(2,1)} %add_convert_fusion.34.refs_1_), channel_id=1, source_target_pairs={{0,16},{1,17},{2,18},{3,19},{4,20},{5,21},{6,22},{7,23},{8,24},{9,... | collective-permute-start | bytes 786440 | tf_op jit(solution)/shard_map/ppermute | solution.py:68
  577.5 37.7 %collective-permute-start.80 = (bf16[128,1024]{1,0:T(8,128)(2,1)S(1)}, bf16[128,1024]{1,0:T(8,128)(2,1)}, u32[]{:S(2)}, u32[]{:S(2)}) collective-permute-start(bf16[128,1024]{1,0:T(8,128)(2,1)S(1)} %add_convert_fusion.35.refs_0_), channel_id=1, source_target_pairs={{0,16},{1,17},{2,18},{3,19},{4,20},{5,21},{6,22},{7,23},{8,24},{9,... | collective-permute-start | bytes 786440 | tf_op jit(solution)/shard_map/ppermute | solution.py:68
  582.4 40.7 %collective-permute-start.78 = (bf16[64,4096]{1,0:T(8,128)(2,1)}, bf16[64,4096]{1,0:T(8,128)(2,1)}, u32[]{:S(2)}, u32[]{:S(2)}) collective-permute-start(bf16[64,4096]{1,0:T(8,128)(2,1)} %get-tuple-element.131.refs_2_), channel_id=1, source_target_pairs={{0,8},{1,9},{2,10},{3,11},{4,12},{5,13},{6,14},{7,15},{8,0},{9,1},... | collective-permute-start | bytes 1572872 | tf_op jit(solution)/shard_map/ppermute | solution.py:68
  590.9 47.0 %collective-permute-start.71 = (bf16[512,1024]{1,0:T(8,128)(2,1)}, bf16[512,1024]{1,0:T(8,128)(2,1)}, u32[]{:S(2)}, u32[]{:S(2)}) collective-permute-start(bf16[512,1024]{1,0:T(8,128)(2,1)} %convolution_convert_fusion.12.refs_4_), channel_id=1, source_target_pairs={{0,2},{1,3},{2,0},{3,1},{4,5},{5,4},{6,7},{7,6},{8,10},{9,11},{10,... | collective-permute-start | bytes 3145736 | tf_op jit(solution)/shard_map/ppermute | solution.py:68
  593.8 44.8 %collective-permute-start.72 = (bf16[512,1024]{1,0:T(8,128)(2,1)}, bf16[512,1024]{1,0:T(8,128)(2,1)}, u32[]{:S(2)}, u32[]{:S(2)}) collective-permute-start(bf16[512,1024]{1,0:T(8,128)(2,1)} %convolution_convert_fusion.13.refs_3_), channel_id=1, source_target_pairs={{0,2},{1,3},{2,0},{3,1},{4,5},{5,4},{6,7},{7,6},{8,10},{9,11},{10,... | collective-permute-start | bytes 3145736 | tf_op jit(solution)/shard_map/ppermute | solution.py:68
  603.5 31.5 %collective-permute-start.70 = (bf16[128,3072]{1,0:T(8,128)(2,1)}, bf16[128,3072]{1,0:T(8,128)(2,1)S(1)}, u32[]{:S(2)}, u32[]{:S(2)}) collective-permute-start(bf16[128,3072]{1,0:T(8,128)(2,1)} %get-tuple-element.117), channel_id=1, source_target_pairs={{0,1},{1,0},{2,3},{3,2},{4,6},{5,7},{6,4},{7,5},{8,9},{9,8},{10,11... | collective-permute-start | bytes 2359304 | tf_op jit(solution)/shard_map/ppermute | solution.py:68
  615.2 29.1 %collective-permute-start.64 = (bf16[128,4096]{1,0:T(8,128)(2,1)S(1)}, bf16[128,4096]{1,0:T(8,128)(2,1)}, u32[]{:S(2)}, u32[]{:S(2)}) collective-permute-start(bf16[128,4096]{1,0:T(8,128)(2,1)S(1)} %copy-done.28), channel_id=1, source_target_pairs={{0,2},{1,3},{2,0},{3,1},{4,5},{5,4},{6,7},{7,6},{8,10},{9,11},{10,... | collective-permute-start | bytes 3145736 | tf_op jit(solution)/shard_map/ppermute | solution.py:68
  633.0 27.0 %collective-permute-start.63 = (bf16[128,4096]{1,0:T(8,128)(2,1)S(1)}, bf16[128,4096]{1,0:T(8,128)(2,1)}, u32[]{:S(2)}, u32[]{:S(2)}) collective-permute-start(bf16[128,4096]{1,0:T(8,128)(2,1)S(1)} %copy-done.27), channel_id=1, source_target_pairs={{0,2},{1,3},{2,0},{3,1},{4,5},{5,4},{6,7},{7,6},{8,10},{9,11},{10,... | collective-permute-start | bytes 3145736 | tf_op jit(solution)/shard_map/ppermute | solution.py:68
  672.9 27.2 %collective-permute-start.67 = (bf16[64,4096]{1,0:T(8,128)(2,1)}, bf16[64,4096]{1,0:T(8,128)(2,1)S(1)}, u32[]{:S(2)}, u32[]{:S(2)}) collective-permute-start(bf16[64,4096]{1,0:T(8,128)(2,1)} %get-tuple-element.168.refs_0_), channel_id=1, source_target_pairs={{0,8},{1,9},{2,10},{3,11},{4,12},{5,13},{6,14},{7,15},{8,0},{9,1},... | collective-permute-start | bytes 1572872 | tf_op jit(solution)/shard_map/ppermute | solution.py:68
  675.3 26.9 %collective-permute-start.85 = (f32[37,64]{1,0:T(8,128)S(1)}, f32[37,64]{1,0:T(8,128)S(1)}, u32[]{:S(2)}, u32[]{:S(2)}) collective-permute-start(f32[37,64]{1,0:T(8,128)S(1)} %slice.933), channel_id=1, source_target_pairs={{0,8},{1,9},{2,10},{3,11},{4,12},{5,13},{6,14},{7,15},{8,0},{9,1},... | collective-permute-start | bytes 28424 | tf_op jit(solution)/shard_map/ppermute | solution.py:68
  678.2 26.9 %collective-permute-start.77 = (bf16[32,3072]{1,0:T(8,128)(2,1)}, bf16[32,3072]{1,0:T(8,128)(2,1)}, u32[]{:S(2)}, u32[]{:S(2)}) collective-permute-start(bf16[32,3072]{1,0:T(8,128)(2,1)} %add_convert_fusion.36), channel_id=1, source_target_pairs={{0,16},{1,17},{2,18},{3,19},{4,20},{5,21},{6,22},{7,23},{8,24},{9,... | collective-permute-start | bytes 589832 | tf_op jit(solution)/shard_map/ppermute | solution.py:68
  682.6 24.2 %collective-permute-start.75 = (bf16[128,1024]{1,0:T(8,128)(2,1)}, bf16[128,1024]{1,0:T(8,128)(2,1)S(1)}, u32[]{:S(2)}, u32[]{:S(2)}) collective-permute-start(bf16[128,1024]{1,0:T(8,128)(2,1)} %add_convert_fusion.30), channel_id=1, source_target_pairs={{0,16},{1,17},{2,18},{3,19},{4,20},{5,21},{6,22},{7,23},{8,24},{9,... | collective-permute-start | bytes 786440 | tf_op jit(solution)/shard_map/ppermute | solution.py:68
  (206 other events, 1929.0 us)
Sparse Core Ops, SparseCore 0:
  10.9 91.2 all-gather.3
  105.6 81.7 all-gather.5
  190.3 111.1 all-gather.7
